TPU v7x, 32 devices: a whole 2x2x4 slice. The times are simulated.
32 devices in a mesh: pipe: 2 (over y), ctx: 4 (over x, core), tp: 4 (over z).
Axes of the slice: x: 2, y: 2, z: 4, core: 2. Of those that a mesh axis runs over, the one named last changes fastest.
Arguments:
- queries: bfloat16 [2, 2048, 4096], P('pipe', 'ctx', 'tp'), may hold values from -24 to 24
- keys: bfloat16 [2, 2048, 4096], P('pipe', 'ctx', 'tp'), may hold values from -24 to 24
- values: bfloat16 [2, 2048, 4096], P('pipe', 'ctx', 'tp'), may hold values from -6 to 6
- stream: bfloat16 [2, 2048, 8192], P('pipe', 'ctx', 'tp'), may hold values from -6 to 6
- grad_stream: bfloat16 [2, 2048, 8192], P('pipe', 'ctx', 'tp'), may hold values from -6 to 6
- out_proj: bfloat16 [2, 4096, 8192], P('pipe', 'tp'), may hold values from -0.09375 to 0.09375
- doc_ids: int32 [2, 2048], P('pipe'), may hold values from 0 to 1, never falling along the last dimension, each value on 1 to 1536 neighbouring positions
Outputs:
- grad_queries: bfloat16 [2, 2048, 4096], P('pipe', 'ctx', 'tp')
- grad_keys: bfloat16 [2, 2048, 4096], P('pipe', 'ctx', 'tp')
- grad_values: bfloat16 [2, 2048, 4096], P('pipe', 'ctx', 'tp')
- next_stream: bfloat16 [2, 2048, 8192], P('pipe', 'ctx', 'tp')
- next_grad: bfloat16 [2, 2048, 8192], P('pipe', 'ctx', 'tp')
Inputs may be any that keep to these rules, and one draw needn't show every extreme that they name: `doc_ids`: document numbers never fall along a micro-batch; a document has at most 1536 tokens.
All inputs are finite; a program needn't handle non-finite values.
Results may differ from a plain program's by a relative error of at most 0.02.
Values may be sent and summed in bfloat16 or wider, within the bound.
No kernel may reach another device: no remote copies, remote signals or barrier semaphores. Data moves between devices by JAX's collectives and lax.ppermute only.
A program may use at most 192 MiB of HBM per device.

v0:
```python
import jax
import jax.numpy as jnp
from jax import lax
from jax.sharding import PartitionSpec as P

HD = 128
WINDOW = 512


NEG = -1e30


def shifted(block, axis, distance):
    devices = range(lax.axis_size(axis))
    route = [((i - distance) % len(devices), i) for i in devices]
    return lax.ppermute(block, axis, route)


def from_behind(block, axis, distance):
    devices = range(lax.axis_size(axis))
    route = [(i - distance, i) for i in devices if i - distance in devices]
    return lax.ppermute(block, axis, route)


def block_terms(query_block, key_block, value_block, dout_block, visible):
    scaling = HD ** (-0.5)
    scores = (
        jnp.einsum("qhd,khd->hqk", query_block, key_block, preferred_element_type=jnp.float32)
        * scaling
    )
    masked = jnp.where(visible[None], scores, NEG)
    row_max = jnp.max(masked, axis=-1, keepdims=True)
    exponent = jnp.where(visible[None], jnp.exp(masked - row_max), 0.0)
    row_sum = jnp.sum(exponent, axis=-1, keepdims=True)
    probability = exponent / row_sum
    weights = probability.astype(jnp.bfloat16)
    attended = jnp.einsum(
        "hqk,khd->qhd", weights, value_block, preferred_element_type=jnp.float32
    ).astype(jnp.bfloat16)
    row_delta = jnp.einsum("qhd,qhd->hq", dout_block, attended, preferred_element_type=jnp.float32)[
        ..., None
    ]
    d_prob = jnp.einsum("qhd,khd->hqk", dout_block, value_block, preferred_element_type=jnp.float32)
    d_score = (probability * (d_prob - row_delta)).astype(jnp.bfloat16)
    d_value = jnp.einsum("hqk,qhd->khd", weights, dout_block, preferred_element_type=jnp.float32)
    d_query = (
        jnp.einsum("hqk,khd->qhd", d_score, key_block, preferred_element_type=jnp.float32) * scaling
    ).astype(jnp.bfloat16)
    d_key = (
        jnp.einsum("hqk,qhd->khd", d_score, query_block, preferred_element_type=jnp.float32)
        * scaling
    )
    return (attended, d_query, d_key, d_value)


def body(queries, keys, values, stream, grad_stream, out_proj, doc_ids):
    row_count = queries.shape[1]
    feature = queries.shape[2]
    head_count = feature // HD
    weight = out_proj[0]
    grad_rows = grad_stream[0]
    grad_next = shifted(grad_stream, "pipe", -1)
    d_out = lax.dot_general(
        lax.all_gather(grad_rows, "tp", axis=1, tiled=True),
        weight,
        (((1,), (1,)), ((), ())),
        preferred_element_type=jnp.float32,
    ).astype(jnp.bfloat16)
    pair_own = jnp.stack([keys[0], values[0]])
    pair_prev = from_behind(pair_own, "ctx", 1)
    key_all = jnp.concatenate([pair_prev[0], keys[0]], 0).reshape(2 * row_count, head_count, HD)
    value_all = jnp.concatenate([pair_prev[1], values[0]], 0).reshape(2 * row_count, head_count, HD)
    shard_index = lax.axis_index("ctx")
    query_pos = shard_index * row_count + jnp.arange(row_count, dtype=jnp.int32)
    key_pos = (shard_index - 1) * row_count + jnp.arange(2 * row_count, dtype=jnp.int32)
    doc_row = doc_ids[0]
    query_doc = lax.dynamic_slice_in_dim(doc_row, shard_index * row_count, row_count)
    prev_doc = lax.dynamic_slice_in_dim(
        doc_row, jnp.maximum(shard_index - 1, 0) * row_count, row_count
    )
    key_doc = jnp.concatenate([prev_doc, query_doc], 0)
    visible = (key_pos[None, :] <= query_pos[:, None]) & (
        query_pos[:, None] - key_pos[None, :] < WINDOW
    )
    visible = visible & (key_pos[None, :] >= 0) & (key_doc[None, :] == query_doc[:, None])
    query_block = queries[0].reshape(row_count, head_count, HD)
    dout_block = d_out.reshape(row_count, head_count, HD)
    attended, d_query, d_key, d_value = block_terms(
        query_block, key_all, value_all, dout_block, visible
    )
    earlier_terms = jnp.stack(
        [
            d_key[:row_count].reshape(row_count, feature),
            d_value[:row_count].reshape(row_count, feature),
        ]
    )
    returned = from_behind(earlier_terms.astype(jnp.bfloat16), "ctx", -1).astype(
        earlier_terms.dtype
    )
    key_total = d_key[row_count:].reshape(row_count, feature) + returned[0]
    value_total = d_value[row_count:].reshape(row_count, feature) + returned[1]
    attended_flat = attended.reshape(row_count, feature)
    partial_value = jnp.dot(attended_flat, weight, preferred_element_type=jnp.float32).astype(
        jnp.bfloat16
    )
    own_share = lax.psum_scatter(partial_value, "tp", scatter_dimension=1, tiled=True).astype(
        jnp.float32
    )
    rebuilt = (stream[0].astype(jnp.float32) - own_share).astype(jnp.bfloat16)
    stream_next = shifted(rebuilt[None], "pipe", -1)
    grad_queries = d_query.reshape(1, row_count, feature)
    grad_keys = key_total.astype(jnp.bfloat16).reshape(1, row_count, feature)
    grad_values = value_total.astype(jnp.bfloat16).reshape(1, row_count, feature)
    return (grad_queries, grad_keys, grad_values, stream_next, grad_next)


def solution(mesh):
    in_specs = (
        P("pipe", "ctx", "tp"),
        P("pipe", "ctx", "tp"),
        P("pipe", "ctx", "tp"),
        P("pipe", "ctx", "tp"),
        P("pipe", "ctx", "tp"),
        P("pipe", "tp", None),
        P("pipe", None),
    )
    out_specs = (
        P("pipe", "ctx", "tp"),
        P("pipe", "ctx", "tp"),
        P("pipe", "ctx", "tp"),
        P("pipe", "ctx", "tp"),
        P("pipe", "ctx", "tp"),
    )
    return jax.shard_map(body, mesh=mesh, in_specs=in_specs, out_specs=out_specs, check_vma=False)
```

profile of v0, /device:TPU:0, one launch (start us, length us, event | category | flops | bytes accessed | tf_op | source)
XLA Modules:
  0.0 412.1 jit_solution(7919685327465313102)
XLA Ops:
  11.5 3.8 collective-permute-start
  16.0 1.9 copy.65
  19.3 1.7 fusion.20
  21.0 3.3 fusion.38
  24.2 1.7 copy.31
  25.9 2.6 copy.35
  28.6 8.1 %fusion.31 = f32[8,1024,512]{2,1,0:T(8,128)} fusion(bf16[512,8,128]{0,2,1:T(8,128)(2,1)S(1)} %bitcast.73, bf16[512,8,128]{2,0,1:T(8,128)(2,1)S(1)} %copy.32, bf16[512,8,128]{2,0,1:T(8,128)(2,1)S(1)} %copy.31), kind=kOutput, calls=%fused_computation.40 | convolution fusion | flops 1077936128 | bytes 19922944 | tf_op jit(solution)/shard_map/qhd,khd->hqk/dot_general | solution.py:28
  36.6 18.4 %fusion.39 = (f32[8,512]{1,0:T(8,128)S(1)}, f32[8,512,1024]{1,2,0:T(8,128)}) fusion(f32[8,1024,512]{2,1,0:T(8,128)} %fusion.31, pred[512,1024]{0,1:T(8,128)(4,1)} %fusion.20), kind=kOutput, calls=%fused_computation.55 | output fusion | flops 29361152 | bytes 34095104 | tf_op jit(solution)/shard_map/sub | solution.py:33
  55.1 9.3 %fusion.13 = bf16[8,512,1024]{1,2,0:T(8,128)(2,1)} fusion(f32[8,512,1024]{1,2,0:T(8,128)} %get-tuple-element.22, f32[8,512]{1,0:T(8,128)S(1)} %get-tuple-element.21), kind=kLoop, calls=%fused_computation.15 | loop fusion | flops 8388608 | bytes 25182208 | tf_op jit(solution)/shard_map/convert_element_type | solution.py:36
  64.4 97.5 %all-gather.3.cloned.1.call-done = bf16[1,512,8192]{2,1,0:T(8,128)(2,1)} async-done(((bf16[1,512,2048]{2,1,0:T(8,128)(2,1)}), bf16[1,512,8192]{2,1,0:T(8,128)(2,1)}) %all-gather.3.cloned.1.call-update) | async-done | bytes 8388624 | tf_op jit(solution)/shard_map/all_gather | solution.py:64
  162.0 14.8 %fusion.26 = bf16[64,8,8,128]{3,1,2,0:T(8,128)(2,1)S(1)} fusion(bf16[1,1024,8192]{2,1,0:T(8,128)(2,1)} %param.12, bf16[1,512,8192]{2,1,0:T(8,128)(2,1)} %all-gather.3.cloned.1.call-done), kind=kOutput, calls=%fused_computation.39 | convolution fusion | flops 8590458880 | bytes 26214400 | tf_op jit(solution)/shard_map/dot_general | solution.py:63
  179.6 1.9 copy.60
  181.5 5.5 %multiply_reduce_fusion = (f32[8,512]{1,0:T(8,128)S(1)}, bf16[8,128,512]{2,1,0:T(8,128)(2,1)S(1)}) fusion(f32[8,512,128]{1,2,0:T(8,128)S(1)} %copy.60, bf16[8,512,1024]{1,2,0:T(8,128)(2,1)} %fusion.13, bf16[512,8,128]{2,0,1:T(8,128)(2,1)} %copy.36, bf16[512,8,128]{2,0,1:T(8,128)(2,1)} %copy.35), kind=kOutput, calls=%fused_computation.31 | convolution fusion | flops 1080029184 | bytes 13647872 | tf_op jit(solution)/shard_map/hqk,khd->qhd/dot_general | solution.py:37
  187.0 16.9 %fusion.6 = bf16[512,8192]{1,0:T(8,128)(2,1)} fusion(bf16[512,1024]{0,1:T(8,128)(2,1)S(1)} %bitcast.84, bf16[1,1024,8192]{2,1,0:T(8,128)(2,1)} %param.12), kind=kOutput, calls=%fused_computation.9 | convolution fusion | flops 8594128896 | bytes 26214400 | tf_op jit(solution)/shard_map/dot_general | solution.py:103
  203.9 1.5 collective-permute-start.3
  206.9 10.9 %multiply_convert_fusion = bf16[8,512,1024]{1,2,0:T(8,128)(2,1)} fusion(bf16[512,8,128]{0,2,1:T(8,128)(2,1)} %copy.45, f32[8,512]{1,0:T(8,128)S(1)} %get-tuple-element.23, f32[8,512,1024]{1,2,0:T(8,128)} %get-tuple-element.22, f32[8,512]{1,0:T(8,128)S(1)} %get-tuple-element.21, bf16[512,8,128]{2,0,1:T(8,128)(2,1)S(1)} %copy-done.10, ...), kind=kOutput, calls=%fused_computation.6 | convolution fusion | flops 1094713344 | bytes 28344320 | tf_op jit(solution)/shard_map/qhd,khd->hqk/dot_general | solution.py:43
  217.8 6.2 %multiply_bitcast_fusion = f32[1024,8,128]{0,2,1:T(8,128)S(1)} fusion(bf16[8,512,1024]{1,2,0:T(8,128)(2,1)} %multiply_convert_fusion, bf16[512,8,128]{0,2,1:T(8,128)(2,1)S(1)} %bitcast.74), kind=kOutput, calls=%fused_computation.18 | convolution fusion | flops 1074790400 | bytes 13631488 | tf_op jit(solution)/shard_map/hqk,qhd->khd/dot_general | solution.py:50
  224.1 2.1 copy-done.1
  227.3 6.3 %convolution_bitcast_fusion = f32[1024,8,128]{0,2,1:T(8,128)S(1)} fusion(bf16[512,8,128]{0,2,1:T(8,128)(2,1)S(1)} %copy-done.11, bf16[8,512,1024]{1,2,0:T(8,128)(2,1)} %fusion.13), kind=kOutput, calls=%fused_computation.19 | convolution fusion | flops 1073741824 | bytes 13631488 | tf_op jit(solution)/shard_map/hqk,qhd->khd/dot_general | solution.py:45
  233.6 1.9 copy-done
  239.1 107.7 %reduce-scatter.2.cloned.1.call-done = bf16[512,2048]{1,0:T(8,128)(2,1)} async-done(((bf16[512,8192]{1,0:T(8,128)(2,1)}), bf16[512,2048]{1,0:T(8,128)(2,1)}) %reduce-scatter.2.cloned.1.call-update) | async-done | bytes 2097168 | tf_op jit(solution)/shard_map/reduce_scatter | solution.py:106
  346.8 4.7 %fusion.15 = bf16[1,512,2048]{2,1,0:T(8,128)(2,1)} fusion(bf16[512,2048]{1,0:T(8,128)(2,1)} %reduce-scatter.2.cloned.1.call-done, bf16[1,512,2048]{2,1,0:T(8,128)(2,1)} %param.10), kind=kLoop, calls=%fused_computation.20 | loop fusion | flops 4194304 | bytes 6291456 | tf_op jit(solution)/shard_map/broadcast_in_dim | solution.py:110
  352.9 1.6 slice.36
  354.5 3.1 copy.49
  357.6 1.8 copy.50
  359.4 6.1 %multiply_convert_fusion.1 = bf16[8,128,512]{2,1,0:T(8,128)(2,1)} fusion(bf16[8,512,1024]{1,2,0:T(8,128)(2,1)} %multiply_convert_fusion, bf16[512,8,128]{2,0,1:T(8,128)(2,1)S(1)} %copy-done.8, bf16[512,8,128]{2,0,1:T(8,128)(2,1)} %copy-done.9), kind=kOutput, calls=%fused_computation.32 | convolution fusion | flops 1078984704 | bytes 11534336 | tf_op jit(solution)/shard_map/hqk,khd->qhd/dot_general | solution.py:47
  365.5 2.4 copy.51
  367.9 2.2 convert_element_type.55
  370.1 2.0 fusion.16
  372.1 26.8 %collective-permute-done.2 = bf16[1,512,2048]{2,1,0:T(8,128)(2,1)} collective-permute-done((bf16[1,512,2048]{2,1,0:T(8,128)(2,1)}, bf16[1,512,2048]{2,1,0:T(8,128)(2,1)}, u32[]{:S(2)}, u32[]{:S(2)}) %collective-permute-start.2) | collective-permute-done | bytes 2097184 | tf_op jit(solution)/shard_map/ppermute | solution.py:16
  399.0 3.2 copy.69
  402.1 3.2 copy.70
  (54 shorter events, 16.8 us)
Async XLA Ops:
  7.2 2.3 copy-start.12
  7.2 154.8 %all-gather.3.cloned.1.call-start = ((), (), s32[]{:S(2)}) async-start(), calls=%async_computation.2 | async-start | bytes 10485760 | tf_op jit(solution)/shard_map/all_gather | solution.py:64
  7.9 338.8 %reduce-scatter.2.cloned.1.call-start = ((), (), s32[]{:S(2)}) async-start(), calls=%async_computation.1 | async-start | bytes 10485760 | tf_op jit(solution)/shard_map/reduce_scatter | solution.py:106
  11.5 7.7 %copy-start.13 = (s32[1,2048]{1,0:T(1,128)S(1)}, s32[1,2048]{1,0:T(1,128)}, u32[]{:S(2)}) copy-start(s32[1,2048]{1,0:T(1,128)} %param.13) | copy-start | bytes 24580
  11.5 9.5 %collective-permute-start = (bf16[2,512,1024]{1,2,0:T(8,128)(2,1)}, bf16[2,512,1024]{1,2,0:T(8,128)(2,1)}, u32[]{:S(2)}, u32[]{:S(2)}) collective-permute-start(bf16[2,512,1024]{1,2,0:T(8,128)(2,1)} %pad_maximum_fusion), channel_id=1, source_target_pairs={{0,4},{4,8},{8,12},{1,5},{5,9},{9,13},{2,6},{6,10},{10,14},{3,7},{... | collective-permute-start | bytes 6291464 | tf_op jit(solution)/shard_map/ppermute | solution.py:22
  16.0 12.6 %copy-start.7 = (bf16[512,8,128]{2,0,1:T(8,128)(2,1)}, bf16[512,8,128]{2,0,1:T(8,128)(2,1)S(1)}, u32[]{:S(2)}) copy-start(bf16[512,8,128]{2,0,1:T(8,128)(2,1)S(1)} %copy.32) | copy-start | bytes 3145732
  25.9 10.7 %copy-start.9 = (bf16[512,8,128]{2,0,1:T(8,128)(2,1)}, bf16[512,8,128]{2,0,1:T(8,128)(2,1)S(1)}, u32[]{:S(2)}) copy-start(bf16[512,8,128]{2,0,1:T(8,128)(2,1)S(1)} %copy.31) | copy-start | bytes 3145732
  177.1 1.0 copy-start.3
  203.9 1.6 copy-start.4
  203.9 3.0 copy-start.10
  203.9 149.0 %collective-permute-start.3 = (bf16[1,512,2048]{2,1,0:T(8,128)(2,1)}, bf16[1,512,2048]{2,1,0:T(8,128)(2,1)}, u32[]{:S(2)}, u32[]{:S(2)}) collective-permute-start(bf16[1,512,2048]{2,1,0:T(8,128)(2,1)} %param.11), channel_id=1, source_target_pairs={{16,0},{0,16},{17,1},{1,17},{18,2},{2,18},{19,3},{3,19},{20,4},{4,... | collective-permute-start | bytes 6291464 | tf_op jit(solution)/shard_map/ppermute | solution.py:16
  224.1 2.1 copy-start.1
  226.1 1.2 copy-start.11
  233.6 1.9 copy-start
  237.8 130.1 %collective-permute-start.1 = (bf16[2,512,1024]{2,1,0:T(8,128)(2,1)}, bf16[2,512,1024]{2,1,0:T(8,128)(2,1)}, u32[]{:S(2)}, u32[]{:S(2)}) collective-permute-start(bf16[2,512,1024]{2,1,0:T(8,128)(2,1)} %pad_maximum_fusion.3), channel_id=1, source_target_pairs={{4,0},{8,4},{12,8},{5,1},{9,5},{13,9},{6,2},{10,6},{14,10},{7,3},{... | collective-permute-start | bytes 6291464 | tf_op jit(solution)/shard_map/ppermute | solution.py:22
  346.7 6.2 %copy-start.2 = (f32[1024,8,128]{0,2,1:T(8,128)S(1)}, f32[1024,8,128]{0,2,1:T(8,128)}, u32[]{:S(2)}) copy-start(f32[1024,8,128]{0,2,1:T(8,128)} %copy-done.1) | copy-start | bytes 12582916
  351.4 47.5 %collective-permute-start.2 = (bf16[1,512,2048]{2,1,0:T(8,128)(2,1)}, bf16[1,512,2048]{2,1,0:T(8,128)(2,1)}, u32[]{:S(2)}, u32[]{:S(2)}) collective-permute-start(bf16[1,512,2048]{2,1,0:T(8,128)(2,1)} %fusion.15), channel_id=1, source_target_pairs={{16,0},{0,16},{17,1},{1,17},{18,2},{2,18},{19,3},{3,19},{20,4},{4,... | collective-permute-start | bytes 6291464 | tf_op jit(solution)/shard_map/ppermute | solution.py:16
  354.5 3.1 slice-start
  354.5 4.9 %copy-start.8 = (bf16[512,8,128]{2,0,1:T(8,128)(2,1)S(1)}, bf16[512,8,128]{2,0,1:T(8,128)(2,1)}, u32[]{:S(2)}) copy-start(bf16[512,8,128]{2,0,1:T(8,128)(2,1)} %copy-done.7) | copy-start | bytes 3145732
  365.5 4.6 %copy-start.5 = (f32[1,512,1024]{2,1,0:T(8,128)S(1)}, f32[1,512,1024]{2,1,0:T(8,128)}, u32[]{:S(2)}) copy-start(f32[1,512,1024]{2,1,0:T(8,128)} %copy.49) | copy-start | bytes 6291460
  367.9 2.2 copy-start.6
Sparse Core Ops, SparseCore 0:
  9.6 152.3 all-gather.2
  204.1 142.6 reduce-scatter.1
where the time goes:
time: 413 us; the launch traced here: 412 us
  waiting for transfers between devices  233 us (56%)
  matrix products  74.8 us (18%)
  other arithmetic  42.9 us (10%)
  local copies, waits for them, and re-layouts  39.2 us (9%)
  between operations  14.3 us (3%)
  starting transfers between devices  8.21 us (2%)
    reduce_scatter x1, waiting for transfers between devices, body(): lax.psum_scatter(partial_value, 'tp', scatter_dimension=1, tiled=True)  108 us
    all_gather x1, waiting for transfers between devices, body(): lax.all_gather(grad_rows, 'tp', axis=1, tiled=True)  97.5 us
    ppermute x2, waiting for transfers between devices, shifted(): return lax.ppermute(block, axis, route)  26.9 us
    unnamed x35, local copies, waits for them, and re-layouts  18.5 us
    sub x1, other arithmetic, block_terms(): exponent = jnp.where(visible[None], jnp.exp(masked - row_max), 0.0)  18.4 us
    dot_general x1, matrix products, body(): jnp.dot(attended_flat, weight, preferred_element_type=jnp.float32)  16.9 us
    dot_general x1, matrix products, body(): lax.dot_general(lax.all_gather(grad_rows, 'tp', axis=1, tiled=True), weig...  14.8 us
    dot_general x1, matrix products, block_terms(): jnp.einsum('qhd,khd->hqk', dout_block, value_block, preferred_element_typ...  10.9 us
  transfers between devices with their start and end apart: 6, of which 3 were waited for; matrix products, arithmetic and copies ran while one was open for 25% of the time, Pallas kernels for 0%

commit v1 on v0

v1 whole, which is shorter than its diff:
```python
import functools

import jax
import jax.numpy as jnp
from jax import lax
from jax.experimental import pallas as pl
from jax.experimental.pallas import tpu as pltpu
from jax.sharding import PartitionSpec as P

HD = 128
WINDOW = 512
NEG = -1e30
HALF = 256
VMEM_LIMIT = 48 * 1024 * 1024

OUTER = [(0, 1), (1, 0), (2, 3), (3, 2)]
MIDDLE = [(1, 2), (2, 1)]
OUTER_INWARD = [(0, 1), (3, 2)]
OUTER_OUTWARD = [(1, 0), (2, 3)]


def params():
    return pltpu.CompilerParams(vmem_limit_bytes=VMEM_LIMIT)


def dot(a, b, contract):
    return lax.dot_general(a, b, ((contract[0], contract[1]), ((), ())), preferred_element_type=jnp.float32)


def nt(a, b):
    return dot(a, b, ((1,), (1,)))


def nn(a, b):
    return dot(a, b, ((1,), (0,)))


def tn(a, b):
    return dot(a, b, ((0,), (0,)))


def lower(size):
    row = lax.broadcasted_iota(jnp.int32, (size, size), 0)
    col = lax.broadcasted_iota(jnp.int32, (size, size), 1)
    return col <= row


def forward_kernel(index_ref, doc_ref, q_ref, k_ref, v_ref, kp_ref, vp_ref, att_ref, w_ref, bias_ref):
    rows = q_ref.shape[0]
    scaling = HD ** (-0.5)

    @pl.when(pl.program_id(0) == 0)
    def _():
        index = index_ref[0]
        own = doc_ref[:, pl.ds(pl.multiple_of(index * rows, rows), rows)]
        before = doc_ref[:, pl.ds(pl.multiple_of(jnp.maximum(index - 1, 0) * rows, rows), rows)]
        before = jnp.where(index > 0, before, -1)
        own = jnp.broadcast_to(own, (rows, rows))
        before = jnp.broadcast_to(before, (rows, rows))
        key_doc = jnp.where(lower(rows), own, before)
        bias_ref[...] = jnp.where(key_doc == own.T, 0.0, NEG)

    tri = lower(HALF)
    for qb in range(2):
        qs = pl.ds(qb * HALF, HALF)
        ks = pl.ds((1 - qb) * HALF, HALF)
        q = q_ref[qs, :]
        diagonal = jnp.where(tri, nt(q, k_ref[qs, :]), nt(q, kp_ref[qs, :]))
        if qb == 0:
            other = nt(q, kp_ref[ks, :])
            scores = jnp.concatenate([diagonal, other], 1)
        else:
            other = nt(q, k_ref[ks, :])
            scores = jnp.concatenate([other, diagonal], 1)
        scores = scores * scaling + bias_ref[qs, :]
        row_max = jnp.max(scores, axis=1, keepdims=True)
        exponent = jnp.exp(scores - row_max)
        row_sum = jnp.sum(exponent, axis=1, keepdims=True)
        prob = exponent * (1.0 / row_sum)
        w_ref[0, qs, :] = prob.astype(jnp.bfloat16)
        mine = prob[:, qb * HALF : (qb + 1) * HALF]
        rest = prob[:, (1 - qb) * HALF : (2 - qb) * HALF].astype(jnp.bfloat16)
        mine_own = jnp.where(tri, mine, 0.0).astype(jnp.bfloat16)
        mine_before = jnp.where(tri, 0.0, mine).astype(jnp.bfloat16)
        att = nn(mine_own, v_ref[qs, :]) + nn(mine_before, vp_ref[qs, :])
        att = att + nn(rest, (vp_ref if qb == 0 else v_ref)[ks, :])
        att_ref[qs, :] = att.astype(jnp.bfloat16)


def forward(index, doc, q, k, v, kp, vp):
    rows, feature = q.shape
    heads = feature // HD
    head = pl.BlockSpec((rows, HD), lambda h, *_: (0, h))
    return pl.pallas_call(
        forward_kernel,
        grid_spec=pltpu.PrefetchScalarGridSpec(
            num_scalar_prefetch=1,
            grid=(heads,),
            in_specs=[pl.BlockSpec(doc.shape, lambda h, *_: (0, 0))] + [head] * 5,
            out_specs=[head, pl.BlockSpec((1, rows, rows), lambda h, *_: (h, 0, 0))],
            scratch_shapes=[pltpu.VMEM((rows, rows), jnp.float32)],
        ),
        out_shape=[
            jax.ShapeDtypeStruct((rows, feature), jnp.bfloat16),
            jax.ShapeDtypeStruct((heads, rows, rows), jnp.bfloat16),
        ],
        compiler_params=params(),
        cost_estimate=pl.CostEstimate(flops=12 * 2 * 2**23 * heads, bytes_accessed=2**23, transcendentals=rows * rows * heads),
        name="attend",
    )(index, doc, q, k, v, kp, vp)


def project_kernel(counts, has_total, index_ref, *refs):
    w_refs = refs[: len(counts)]
    refs = refs[len(counts) :]
    out_ref = refs[-1]
    total = refs[-2][...] if has_total else None
    at = 0
    for w_ref, count in zip(w_refs, counts):
        x = refs[at][...]
        for other in refs[at + 1 : at + count]:
            x = x + other[...]
        at += count
        term = nt(x, w_ref[...])
        total = term if total is None else total + term
    out_ref[...] = total


def project(weight, index, groups, total, chunk):
    rows = HALF
    depth = groups[0][0].shape[1]
    heads_rows = weight.shape[0]
    block = 256
    counts = tuple(len(g) for g in groups)
    w_specs = [pl.BlockSpec((block, depth), lambda n, idx, j=j: (n, idx[j])) for j in range(len(groups))]
    flat, specs = [], []
    for g in groups:
        for x in g:
            flat.append(x)
            at = chunk if x.shape[0] > rows else 0
            specs.append(pl.BlockSpec((rows, depth), lambda n, idx, at=at: (at, 0)))
    if total is not None:
        flat.append(total)
        specs.append(pl.BlockSpec((rows, block), lambda n, idx: (0, n)))
    return pl.pallas_call(
        functools.partial(project_kernel, counts, total is not None),
        grid_spec=pltpu.PrefetchScalarGridSpec(
            num_scalar_prefetch=1,
            grid=(heads_rows // block,),
            in_specs=w_specs + specs,
            out_specs=pl.BlockSpec((rows, block), lambda n, idx: (0, n)),
        ),
        out_shape=jax.ShapeDtypeStruct((rows, heads_rows), jnp.float32),
        compiler_params=params(),
        cost_estimate=pl.CostEstimate(flops=2 * rows * depth * heads_rows * len(groups), bytes_accessed=4 * 2**20 * len(groups), transcendentals=0),
        name="project",
    )(index, *([weight] * len(groups)), *flat)


def part_kernel(received, has_stream, index_ref, x_ref, w_ref, *refs):
    out_ref = refs[-1]
    total = nn(x_ref[...], w_ref[...])
    for ref in refs[:received]:
        total = total + ref[...].astype(jnp.float32)
    if has_stream:
        total = refs[received][...].astype(jnp.float32) - total
    out_ref[...] = total.astype(jnp.bfloat16)


def part(weight, index, attended, received, stream, start, rows):
    depth = weight.shape[0]
    width = stream.shape[1] if stream is not None else weight.shape[1] // 4
    block = 512
    steps = width // block
    at = start // rows
    extra = []
    specs = []
    for x in received:
        extra.append(x)
        specs.append(pl.BlockSpec((rows, block), lambda n, idx: (0, n)))
    if stream is not None:
        extra.append(stream)
        specs.append(pl.BlockSpec((rows, block), lambda n, idx: (at, n)))
    return pl.pallas_call(
        functools.partial(part_kernel, len(received), stream is not None),
        grid_spec=pltpu.PrefetchScalarGridSpec(
            num_scalar_prefetch=1,
            grid=(steps,),
            in_specs=[
                pl.BlockSpec((rows, depth), lambda n, idx: (at, 0)),
                pl.BlockSpec((depth, block), lambda n, idx: (0, idx[0] * steps + n)),
            ]
            + specs,
            out_specs=pl.BlockSpec((rows, block), lambda n, idx: (0, n)),
        ),
        out_shape=jax.ShapeDtypeStruct((rows, width), jnp.bfloat16),
        compiler_params=params(),
        cost_estimate=pl.CostEstimate(flops=2 * rows * depth * width, bytes_accessed=6 * 2**20, transcendentals=0),
        name="part",
    )(index, attended, weight, *extra)


def backward_kernel(qb, index_ref, w_ref, total_ref, x_ref, y_ref, p_ref, att_ref, q_ref, k_ref, v_ref, kp_ref, vp_ref, *refs):
    scaling = HD ** (-0.5)
    qs = pl.ds(qb * HALF, HALF)
    ks = pl.ds((1 - qb) * HALF, HALF)
    tri = lower(HALF)
    bf = jnp.bfloat16
    d_out = (total_ref[...] + nt(x_ref[...] + y_ref[...], w_ref[...])).astype(bf)
    row_delta = jnp.sum(d_out.astype(jnp.float32) * att_ref[...].astype(jnp.float32), axis=1, keepdims=True)
    q = q_ref[...]
    k_diag, kp_diag = k_ref[qs, :], kp_ref[qs, :]
    k_rest, v_rest = ((kp_ref, vp_ref) if qb == 0 else (k_ref, v_ref))
    k_rest, v_rest = k_rest[ks, :], v_rest[ks, :]
    p_diag = p_ref[0, :, qb * HALF : (qb + 1) * HALF].astype(jnp.float32)
    p_rest = p_ref[0, :, (1 - qb) * HALF : (2 - qb) * HALF]
    dp_diag = jnp.where(tri, nt(d_out, v_ref[qs, :]), nt(d_out, vp_ref[qs, :]))
    dp_rest = nt(d_out, v_rest)
    ds_diag = p_diag * (dp_diag - row_delta)
    ds_rest = (p_rest.astype(jnp.float32) * (dp_rest - row_delta)).astype(bf)
    ds_own = jnp.where(tri, ds_diag, 0.0).astype(bf)
    ds_before = jnp.where(tri, 0.0, ds_diag).astype(bf)
    p_own = jnp.where(tri, p_diag, 0.0).astype(bf)
    p_before = jnp.where(tri, 0.0, p_diag).astype(bf)
    dq = nn(ds_own, k_diag) + nn(ds_before, kp_diag) + nn(ds_rest, k_rest)
    dk_own, dv_own = tn(ds_own, q) * scaling, tn(p_own, d_out)
    dk_before, dv_before = tn(ds_before, q) * scaling, tn(p_before, d_out)
    dk_rest, dv_rest = tn(ds_rest, q) * scaling, tn(p_rest, d_out)
    if qb == 0:
        dq_ref, dkb_ref, dvb_ref, dk0_ref, dv0_ref, dkr_ref, dvr_ref = refs
        dkb_ref[...] = dk_before.astype(bf)
        dvb_ref[...] = dv_before.astype(bf)
        dk0_ref[...] = dk_own
        dv0_ref[...] = dv_own
        dkr_ref[...] = dk_rest
        dvr_ref[...] = dv_rest
    else:
        dk0i, dv0i, dkri, dvri, dq_ref, dkb_ref, dvb_ref, dk0_ref, dv0_ref, dk1_ref, dv1_ref = refs
        dkb_ref[...] = (dk_before + dkri[...]).astype(bf)
        dvb_ref[...] = (dv_before + dvri[...]).astype(bf)
        dk0_ref[...] = dk_rest + dk0i[...]
        dv0_ref[...] = dv_rest + dv0i[...]
        dk1_ref[...] = dk_own
        dv1_ref[...] = dv_own
    dq_ref[...] = (dq * scaling).astype(bf)


def backward(qb, weight, index, total, x, y, probs, attended, q, k, v, kp, vp, carried):
    rows, feature = q.shape
    heads = feature // HD
    depth = x.shape[1]
    x_at = qb if x.shape[0] > HALF else 0
    y_at = qb if y.shape[0] > HALF else 0
    head = pl.BlockSpec((rows, HD), lambda h, *_: (0, h))
    half = pl.BlockSpec((HALF, HD), lambda h, *_: (0, h))
    mine = pl.BlockSpec((HALF, HD), lambda h, *_: (qb, h))
    bf16_out = jax.ShapeDtypeStruct((HALF, feature), jnp.bfloat16)
    f32_out = jax.ShapeDtypeStruct((HALF, feature), jnp.float32)
    return pl.pallas_call(
        functools.partial(backward_kernel, qb),
        grid_spec=pltpu.PrefetchScalarGridSpec(
            num_scalar_prefetch=1,
            grid=(heads,),
            in_specs=[
                pl.BlockSpec((HD, depth), lambda h, idx: (h, idx[0])),
                half,
                pl.BlockSpec((HALF, depth), lambda h, *_: (x_at, 0)),
                pl.BlockSpec((HALF, depth), lambda h, *_: (y_at, 0)),
                pl.BlockSpec((1, HALF, rows), lambda h, *_: (h, qb, 0)),
                mine,
                mine,
                head,
                head,
                head,
                head,
            ]
            + [half] * len(carried),
            out_specs=[half] * 7,
        ),
        out_shape=[bf16_out] * 3 + [f32_out] * 4,
        compiler_params=params(),
        cost_estimate=pl.CostEstimate(flops=2 * HALF * depth * feature * 3, bytes_accessed=16 * 2**20, transcendentals=0),
        name="backward",
    )(index, weight, total, x, y, probs, attended, q, k, v, kp, vp, *carried)


def from_behind(block, axis, distance):
    devices = range(lax.axis_size(axis))
    route = [(i - distance, i) for i in devices if i - distance in devices]
    return lax.ppermute(block, axis, route)


def shifted(block, axis, distance):
    count = lax.axis_size(axis)
    return lax.ppermute(block, axis, [((i - distance) % count, i) for i in range(count)])


def hop(block, pairs):
    return lax.ppermute(block, "tp", pairs)


def body(queries, keys, values, stream, grad_stream, out_proj, doc_ids):
    q, k, v, weight = queries[0], keys[0], values[0], out_proj[0]
    grad = grad_stream[0]
    rows, feature = q.shape
    chunks = rows // HALF
    me = lax.axis_index("tp").astype(jnp.int32)
    ctx = lax.axis_index("ctx").astype(jnp.int32)
    near, across, far = me ^ 1, me ^ 2, 3 - me
    one = lambda x: x.reshape(1)

    kp = from_behind(k, "ctx", 1)
    vp = from_behind(v, "ctx", 1)
    pieces = [grad[c * HALF : (c + 1) * HALF] for c in range(chunks)]
    o1 = [hop(x, OUTER) for x in pieces]
    m1 = [hop(x, MIDDLE) for x in pieces]
    grad_next = shifted(grad_stream, "pipe", -1)
    attended, probs = forward(one(ctx), doc_ids, q, k, v, kp, vp)
    m2 = [hop(x, MIDDLE) for x in o1]
    i2 = [hop(x, OUTER_OUTWARD) for x in m1]
    i3 = [hop(x, OUTER_OUTWARD) for x in m2]

    sa = [part(weight, one(far), attended, [], None, c * HALF, HALF) for c in range(chunks)]
    e2 = [hop(x, OUTER_INWARD) for x in sa]
    sb = [part(weight, one(across), attended, [e2[c]], None, c * HALF, HALF) for c in range(chunks)]
    n3 = [hop(x, MIDDLE) for x in sb]
    e3 = [hop(x, OUTER_INWARD) for x in sb]
    sc = [part(weight, one(near), attended, [n3[c]], None, c * HALF, HALF) for c in range(chunks)]
    sd = [part(weight, one(far), attended, [e3[c]], None, c * HALF, HALF) for c in range(chunks)]
    f4 = [hop(x, OUTER) for x in sc]
    n4 = [hop(x, MIDDLE) for x in sd]
    rebuilt = [
        part(weight, one(me), attended, [f4[c], n4[c]], stream[0], c * HALF, HALF) for c in range(chunks)
    ]
    stream_next = jnp.concatenate([shifted(x, "pipe", -1) for x in rebuilt], 0)[None]

    totals = [project(weight, jnp.stack([me, near]), [[grad], [o1[c]]], None, c) for c in range(chunks)]
    totals = [project(weight, one(across), [[m2[c], i2[c]]], totals[c], c) for c in range(chunks)]
    first = backward(0, weight, one(far), totals[0], m1[0], i3[0], probs, attended, q, k, v, kp, vp, ())
    dq0, dkb0, dvb0, dk0, dv0, dkr, dvr = first
    ret_k0, ret_v0 = from_behind(dkb0, "ctx", -1), from_behind(dvb0, "ctx", -1)
    second = backward(1, weight, one(far), totals[1], m1[1], i3[1], probs, attended, q, k, v, kp, vp, (dk0, dv0, dkr, dvr))
    dq1, dkb1, dvb1, dk0, dv0, dk1, dv1 = second
    ret_k1, ret_v1 = from_behind(dkb1, "ctx", -1), from_behind(dvb1, "ctx", -1)

    def finish(a0, a1, r0, r1):
        return jnp.concatenate([(a0 + r0).astype(jnp.bfloat16), (a1 + r1).astype(jnp.bfloat16)], 0)[None]

    grad_queries = jnp.concatenate([dq0, dq1], 0)[None]
    grad_keys = finish(dk0, dk1, ret_k0, ret_k1)
    grad_values = finish(dv0, dv1, ret_v0, ret_v1)
    return (grad_queries, grad_keys, grad_values, stream_next, grad_next)


def solution(mesh):
    cut = P("pipe", "ctx", "tp")
    in_specs = (cut, cut, cut, cut, cut, P("pipe", "tp", None), P("pipe", None))
    out_specs = (cut, cut, cut, cut, cut)
    return jax.shard_map(body, mesh=mesh, in_specs=in_specs, out_specs=out_specs, check_vma=False)
```

time: 413 us -> 290 us (0.70)
  the two profiles are of different devices: /device:TPU:0 before, /device:TPU:18 now
where the time goes in v1:
time: 290 us; the launch traced here: 288 us
  Pallas kernels  105 us (36%)
  waiting for transfers between devices  98.1 us (34%)
  starting transfers between devices  54.8 us (19%)
  local copies, waits for them, and re-layouts  22.5 us (8%)
  other arithmetic  6.52 us (2%)
    pallas_call x10, Pallas kernels, part(): pl.pallas_call(functools.partial(part_kernel, len(received), stream is no...  44.1 us
    ppermute x20, waiting for transfers between devices, hop(): return lax.ppermute(block, 'tp', pairs)  39 us
    ppermute x3, waiting for transfers between devices, shifted(): lax.ppermute(block, axis, [((i - distance) % count, i) for i in range(cou...  38.9 us
    ppermute x20, starting transfers between devices, hop(): return lax.ppermute(block, 'tp', pairs)  37.4 us
    pallas_call x2, Pallas kernels, backward(): pl.pallas_call(functools.partial(backward_kernel, qb), grid_spec=pltpu.Pr...  25.3 us
    pallas_call x4, Pallas kernels, project(): pl.pallas_call(functools.partial(project_kernel, counts, total is not Non...  22.2 us
    ppermute x6, waiting for transfers between devices, from_behind(): return lax.ppermute(block, axis, route)  20.1 us
    unnamed x61, local copies, waits for them, and re-layouts  19.4 us
  transfers between devices with their start and end apart: 29, of which 8 were waited for; matrix products, arithmetic and copies ran while one was open for 3% of the time, Pallas kernels for 36%

profile of v1, /device:TPU:18, one launch (start us, length us, event | category | flops | bytes accessed | tf_op | source)
XLA Modules:
  0.0 287.7 jit_solution(13981318063420340357)
XLA Ops:
  4.7 3.1 %slice_bitcast_fusion.1 = (bf16[256,2048]{1,0:T(8,128)(2,1)}, bf16[256,2048]{1,0:T(8,128)(2,1)}) fusion(bf16[1,512,2048]{2,1,0:T(8,128)(2,1)} %param.11), kind=kLoop, calls=%fused_computation.9 | loop fusion | bytes 4194304 | tf_op jit(solution)/shard_map/slice | solution.py:314
  11.5 5.4 %collective-permute-done.5.kp_ref = bf16[512,1024]{1,0:T(8,128)(2,1)S(1)} collective-permute-done((bf16[512,1024]{1,0:T(8,128)(2,1)}, bf16[512,1024]{1,0:T(8,128)(2,1)S(1)}, u32[]{:S(2)}, u32[]{:S(2)}) %collective-permute-start.5) | collective-permute-done | bytes 1048608 | tf_op jit(solution)/shard_map/ppermute | solution.py:290
  20.3 8.0 %collective-permute-done.6.vp_ref = bf16[512,1024]{1,0:T(8,128)(2,1)} collective-permute-done((bf16[512,1024]{1,0:T(8,128)(2,1)}, bf16[512,1024]{1,0:T(8,128)(2,1)}, u32[]{:S(2)}, u32[]{:S(2)}) %collective-permute-start.6) | collective-permute-done | bytes 1048608 | tf_op jit(solution)/shard_map/ppermute | solution.py:290
  30.8 13.1 %attend.1 = (bf16[512,1024]{1,0:T(8,128)(2,1)S(1)}, bf16[8,512,512]{2,1,0:T(8,128)(2,1)}) custom-call(s32[1]{0:T(128)} %bitcast.7.index_ref, s32[1,2048]{1,0:T(1,128)S(1)} %copy-done.28, bf16[512,1024]{1,0:T(8,128)(2,1)S(1)} %bitcast.27, bf16[512,1024]{1,0:T(8,128)(2,1)S(1)} %bitcast.31, bf16[512,1024]{1,0:T(8,128)(2,1)S(1)} %bitcast.35, ...), custom_call_target="tpu_custom_call" | custom-call | flops 1610612736 | bytes 8388608 | tf_op jit(solution)/shard_map/attend/pallas_call | solution.py:94
  43.8 4.3 %part.15 = bf16[256,2048]{1,0:T(8,128)(2,1)S(1)} custom-call(s32[1]{0:T(128)} %bitcast.index_ref, bf16[512,1024]{1,0:T(8,128)(2,1)S(1)} %get-tuple-element.22.att_ref.x_ref, bf16[1024,8192]{1,0:T(8,128)(2,1)} %bitcast.36), custom_call_target="tpu_custom_call" | custom-call | flops 1073741824 | bytes 6291456 | tf_op jit(solution)/shard_map/part/pallas_call | solution.py:184
  49.4 2.4 collective-permute-start.8
  51.8 4.9 %collective-permute-start.10 = (bf16[256,2048]{1,0:T(8,128)(2,1)}, bf16[256,2048]{1,0:T(8,128)(2,1)}, u32[]{:S(2)}, u32[]{:S(2)}) collective-permute-start(bf16[256,2048]{1,0:T(8,128)(2,1)} %collective-permute-done.9.x_ref), channel_id=1, source_target_pairs={{1,0},{2,3},{5,4},{6,7},{9,8},{10,11},{13,12},{14,15},{17,16},{18,... | collective-permute-start | bytes 3145736 | tf_op jit(solution)/shard_map/ppermute | solution.py:299
  56.7 4.8 %part.10 = bf16[256,2048]{1,0:T(8,128)(2,1)} custom-call(s32[1]{0:T(128)} %bitcast.index_ref, bf16[512,1024]{1,0:T(8,128)(2,1)S(1)} %get-tuple-element.22.att_ref.x_ref, bf16[1024,8192]{1,0:T(8,128)(2,1)} %bitcast.37), custom_call_target="tpu_custom_call" | custom-call | flops 1073741824 | bytes 6291456 | tf_op jit(solution)/shard_map/part/pallas_call | solution.py:184
  62.8 2.4 collective-permute-start.1
  65.1 13.9 %collective-permute-done.22.refs_0_ = bf16[256,2048]{1,0:T(8,128)(2,1)S(1)} collective-permute-done((bf16[256,2048]{1,0:T(8,128)(2,1)S(1)}, bf16[256,2048]{1,0:T(8,128)(2,1)S(1)}, u32[]{:S(2)}, u32[]{:S(2)}) %collective-permute-start.22) | collective-permute-done | bytes 1048608 | tf_op jit(solution)/shard_map/ppermute | solution.py:299
  82.7 5.0 %part.16 = bf16[256,2048]{1,0:T(8,128)(2,1)} custom-call(s32[1]{0:T(128)} %bitcast.2.index_ref, bf16[512,1024]{1,0:T(8,128)(2,1)S(1)} %get-tuple-element.22.att_ref.x_ref, bf16[1024,8192]{1,0:T(8,128)(2,1)} %bitcast.38, bf16[256,2048]{1,0:T(8,128)(2,1)S(1)} %copy-done.13), custom_call_target="tpu_custom_call" | custom-call | flops 1073741824 | bytes 6291456 | tf_op jit(solution)/shard_map/part/pallas_call | solution.py:184
  91.3 10.2 %collective-permute-done.16.refs_0_ = bf16[256,2048]{1,0:T(8,128)(2,1)} collective-permute-done((bf16[256,2048]{1,0:T(8,128)(2,1)}, bf16[256,2048]{1,0:T(8,128)(2,1)}, u32[]{:S(2)}, u32[]{:S(2)}) %collective-permute-start.16) | collective-permute-done | bytes 1048608 | tf_op jit(solution)/shard_map/ppermute | solution.py:299
  103.1 4.9 %part.11 = bf16[256,2048]{1,0:T(8,128)(2,1)} custom-call(s32[1]{0:T(128)} %bitcast.2.index_ref, bf16[512,1024]{1,0:T(8,128)(2,1)S(1)} %get-tuple-element.22.att_ref.x_ref, bf16[1024,8192]{1,0:T(8,128)(2,1)} %bitcast.39, bf16[256,2048]{1,0:T(8,128)(2,1)} %collective-permute-done.16.refs_0_), custom_call_target="tpu_custom_call" | custom-call | flops 1073741824 | bytes 6291456 | tf_op jit(solution)/shard_map/part/pallas_call | solution.py:184
  112.7 14.9 %collective-permute-done.23.refs_0_ = bf16[256,2048]{1,0:T(8,128)(2,1)} collective-permute-done((bf16[256,2048]{1,0:T(8,128)(2,1)}, bf16[256,2048]{1,0:T(8,128)(2,1)}, u32[]{:S(2)}, u32[]{:S(2)}) %collective-permute-start.23) | collective-permute-done | bytes 1048608 | tf_op jit(solution)/shard_map/ppermute | solution.py:299
  129.0 6.4 %project.6.refs_3_ = f32[256,1024]{1,0:T(8,128)S(1)} custom-call(s32[2]{0:T(128)S(1)} %pad_add_fusion.index_ref, bf16[1024,8192]{1,0:T(8,128)(2,1)} %bitcast.40, bf16[1024,8192]{1,0:T(8,128)(2,1)} %bitcast.41, bf16[512,2048]{1,0:T(8,128)(2,1)S(1)} %bitcast.23, bf16[256,2048]{1,0:T(8,128)(2,1)} %collective-permute-done.7.refs_3_), custom_call_target="tpu_custom_call" | custom-call | flops 2147483648 | bytes 8388608 | tf_op jit(solution)/shard_map/project/pallas_call | solution.py:145
  137.7 6.4 %project.4.refs_3_ = f32[256,1024]{1,0:T(8,128)S(1)} custom-call(s32[2]{0:T(128)S(1)} %pad_add_fusion.index_ref, bf16[1024,8192]{1,0:T(8,128)(2,1)} %bitcast.42, bf16[1024,8192]{1,0:T(8,128)(2,1)} %bitcast.43, bf16[512,2048]{1,0:T(8,128)(2,1)S(1)} %bitcast.24, bf16[256,2048]{1,0:T(8,128)(2,1)} %collective-permute-done.refs_3_), custom_call_target="tpu_custom_call" | custom-call | flops 2147483648 | bytes 8388608 | tf_op jit(solution)/shard_map/project/pallas_call | solution.py:145
  144.1 4.8 %project.7.total_ref = f32[256,1024]{1,0:T(8,128)S(1)} custom-call(s32[1]{0:T(128)} %bitcast.2.index_ref, bf16[1024,8192]{1,0:T(8,128)(2,1)} %bitcast.44, bf16[256,2048]{1,0:T(8,128)(2,1)} %collective-permute-done.8.refs_1_, bf16[256,2048]{1,0:T(8,128)(2,1)} %collective-permute-done.10.refs_2_, f32[256,1024]{1,0:T(8,128)S(1)} %project.6.refs_3_), custom_call_target="tpu_custom_call" | custom-call | flops 1073741824 | bytes 4194304 | tf_op jit(solution)/shard_map/project/pallas_call | solution.py:145
  149.9 4.5 %project.5.total_ref = f32[256,1024]{1,0:T(8,128)S(1)} custom-call(s32[1]{0:T(128)} %bitcast.2.index_ref, bf16[1024,8192]{1,0:T(8,128)(2,1)} %bitcast.45, bf16[256,2048]{1,0:T(8,128)(2,1)} %collective-permute-done.1.refs_1_, bf16[256,2048]{1,0:T(8,128)(2,1)S(1)} %copy-done.11, f32[256,1024]{1,0:T(8,128)S(1)} %project.4.refs_3_), custom_call_target="tpu_custom_call" | custom-call | flops 1073741824 | bytes 4194304 | tf_op jit(solution)/shard_map/project/pallas_call | solution.py:145
  154.5 4.4 %part.17 = bf16[256,2048]{1,0:T(8,128)(2,1)S(1)} custom-call(s32[1]{0:T(128)} %bitcast.5.index_ref, bf16[512,1024]{1,0:T(8,128)(2,1)S(1)} %get-tuple-element.22.att_ref.x_ref, bf16[1024,8192]{1,0:T(8,128)(2,1)} %bitcast.46, bf16[256,2048]{1,0:T(8,128)(2,1)} %collective-permute-done.23.refs_0_), custom_call_target="tpu_custom_call" | custom-call | flops 1073741824 | bytes 6291456 | tf_op jit(solution)/shard_map/part/pallas_call | solution.py:184
  158.9 4.1 %part.18 = bf16[256,2048]{1,0:T(8,128)(2,1)S(1)} custom-call(s32[1]{0:T(128)} %bitcast.index_ref, bf16[512,1024]{1,0:T(8,128)(2,1)S(1)} %get-tuple-element.22.att_ref.x_ref, bf16[1024,8192]{1,0:T(8,128)(2,1)} %bitcast.47, bf16[256,2048]{1,0:T(8,128)(2,1)} %collective-permute-done.25.refs_0_), custom_call_target="tpu_custom_call" | custom-call | flops 1073741824 | bytes 6291456 | tf_op jit(solution)/shard_map/part/pallas_call | solution.py:184
  163.1 4.1 %part.12 = bf16[256,2048]{1,0:T(8,128)(2,1)S(1)} custom-call(s32[1]{0:T(128)} %bitcast.5.index_ref, bf16[512,1024]{1,0:T(8,128)(2,1)S(1)} %get-tuple-element.22.att_ref.x_ref, bf16[1024,8192]{1,0:T(8,128)(2,1)} %bitcast.48, bf16[256,2048]{1,0:T(8,128)(2,1)} %collective-permute-done.17.refs_0_), custom_call_target="tpu_custom_call" | custom-call | flops 1073741824 | bytes 6291456 | tf_op jit(solution)/shard_map/part/pallas_call | solution.py:184
  169.1 4.1 %part.13 = bf16[256,2048]{1,0:T(8,128)(2,1)S(1)} custom-call(s32[1]{0:T(128)} %bitcast.index_ref, bf16[512,1024]{1,0:T(8,128)(2,1)S(1)} %get-tuple-element.22.att_ref.x_ref, bf16[1024,8192]{1,0:T(8,128)(2,1)} %bitcast.49, bf16[256,2048]{1,0:T(8,128)(2,1)} %collective-permute-done.19.refs_0_), custom_call_target="tpu_custom_call" | custom-call | flops 1073741824 | bytes 6291456 | tf_op jit(solution)/shard_map/part/pallas_call | solution.py:184
  174.1 12.3 %backward.2 = (bf16[256,1024]{1,0:T(8,128)(2,1)S(1)}, bf16[256,1024]{1,0:T(8,128)(2,1)S(1)}, bf16[256,1024]{1,0:T(8,128)(2,1)S(1)}, f32[256,1024]{1,0:T(8,128)S(...) custom-call(s32[1]{0:T(128)} %bitcast.index_ref, bf16[1024,8192]{1,0:T(8,128)(2,1)} %bitcast.50, ...), custom_call_target="tpu_custom_call" | custom-call | flops 3221225472 | bytes 16777216 | tf_op jit(solution)/shard_map/backward/pallas_call | solution.py:259
  192.8 3.9 %collective-permute-start.20 = (bf16[256,2048]{1,0:T(8,128)(2,1)S(1)}, bf16[256,2048]{1,0:T(8,128)(2,1)S(1)}, u32[]{:S(2)}, u32[]{:S(2)}) collective-permute-start(bf16[256,2048]{1,0:T(8,128)(2,1)S(1)} %part.13), channel_id=1, source_target_pairs={{1,2},{2,1},{5,6},{6,5},{9,10},{10,9},{13,14},{14,13},{17,18},{18,... | collective-permute-start | bytes 3145736 | tf_op jit(solution)/shard_map/ppermute | solution.py:299
  196.8 13.0 %backward.3 = (bf16[256,1024]{1,0:T(8,128)(2,1)S(1)}, bf16[256,1024]{1,0:T(8,128)(2,1)S(1)}, bf16[256,1024]{1,0:T(8,128)(2,1)S(1)}, f32[256,1024]{1,0:T(8,128)S(...) custom-call(s32[1]{0:T(128)} %bitcast.index_ref, bf16[1024,8192]{1,0:T(8,128)(2,1)} %bitcast.51, ...), custom_call_target="tpu_custom_call" | custom-call | flops 3221225472 | bytes 16777216 | tf_op jit(solution)/shard_map/backward/pallas_call | solution.py:259
  213.8 6.7 %collective-permute-done.13 = bf16[256,1024]{1,0:T(8,128)(2,1)S(1)} collective-permute-done((bf16[256,1024]{1,0:T(8,128)(2,1)S(1)}, bf16[256,1024]{1,0:T(8,128)(2,1)S(1)}, u32[]{:S(2)}, u32[]{:S(2)}) %collective-permute-start.13) | collective-permute-done | bytes 524320 | tf_op jit(solution)/shard_map/ppermute | solution.py:290
  220.4 3.8 %collective-permute-start.12 = (bf16[256,1024]{1,0:T(8,128)(2,1)}, bf16[256,1024]{1,0:T(8,128)(2,1)S(1)}, u32[]{:S(2)}, u32[]{:S(2)}) collective-permute-start(bf16[256,1024]{1,0:T(8,128)(2,1)} %copy-done.27), channel_id=1, source_target_pairs={{4,0},{8,4},{12,8},{5,1},{9,5},{13,9},{6,2},{10,6},{14,10},{7,3},{... | collective-permute-start | bytes 1572872 | tf_op jit(solution)/shard_map/ppermute | solution.py:290
  230.5 4.3 %part.19 = bf16[256,2048]{1,0:T(8,128)(2,1)S(1)} custom-call(s32[1]{0:T(128)} %bitcast.4.index_ref, bf16[512,1024]{1,0:T(8,128)(2,1)S(1)} %copy-done.1, bf16[1024,8192]{1,0:T(8,128)(2,1)} %bitcast.52, bf16[256,2048]{1,0:T(8,128)(2,1)S(1)} %collective-permute-done.24.refs_0_, bf16[256,2048]{1,0:T(8,128)(2,1)S(1)} %collective-permute-done.26.refs_1_, ...), custom_call_target="tpu_custom_call" | custom-call | flops 1073741824 | bytes 6291456 | tf_op jit(solution)/shard_map/part/pallas_call | solution.py:184
  236.4 4.2 %part.14 = bf16[256,2048]{1,0:T(8,128)(2,1)S(1)} custom-call(s32[1]{0:T(128)} %bitcast.4.index_ref, bf16[512,1024]{1,0:T(8,128)(2,1)S(1)} %copy-done.1, bf16[1024,8192]{1,0:T(8,128)(2,1)} %bitcast.53, bf16[256,2048]{1,0:T(8,128)(2,1)S(1)} %collective-permute-done.18.refs_0_, bf16[256,2048]{1,0:T(8,128)(2,1)S(1)} %collective-permute-done.20.refs_1_, ...), custom_call_target="tpu_custom_call" | custom-call | flops 1073741824 | bytes 6291456 | tf_op jit(solution)/shard_map/part/pallas_call | solution.py:184
  244.0 16.8 %collective-permute-done.27 = bf16[256,2048]{1,0:T(8,128)(2,1)S(1)} collective-permute-done((bf16[256,2048]{1,0:T(8,128)(2,1)S(1)}, bf16[256,2048]{1,0:T(8,128)(2,1)S(1)}, u32[]{:S(2)}, u32[]{:S(2)}) %collective-permute-start.27) | collective-permute-done | bytes 1048608 | tf_op jit(solution)/shard_map/ppermute | solution.py:295
  260.8 22.1 %collective-permute-done.21 = bf16[256,2048]{1,0:T(8,128)(2,1)S(1)} collective-permute-done((bf16[256,2048]{1,0:T(8,128)(2,1)S(1)}, bf16[256,2048]{1,0:T(8,128)(2,1)S(1)}, u32[]{:S(2)}, u32[]{:S(2)}) %collective-permute-start.21) | collective-permute-done | bytes 1048608 | tf_op jit(solution)/shard_map/ppermute | solution.py:295
  284.5 3.2 %copy.13 = bf16[1,512,2048]{2,1,0:T(8,128)(2,1)} copy(bf16[1,512,2048]{2,1,0:T(8,128)(2,1)} %collective-permute-done.28) | data formatting | bytes 4194304
  (114 shorter events, 60.3 us)
Async XLA Ops:
  0.6 16.3 %collective-permute-start.5 = (bf16[512,1024]{1,0:T(8,128)(2,1)}, bf16[512,1024]{1,0:T(8,128)(2,1)S(1)}, u32[]{:S(2)}, u32[]{:S(2)}) collective-permute-start(bf16[512,1024]{1,0:T(8,128)(2,1)} %bitcast.28), channel_id=1, source_target_pairs={{0,4},{4,8},{8,12},{1,5},{5,9},{9,13},{2,6},{6,10},{10,14},{3,7},{... | collective-permute-start | bytes 3145736 | tf_op jit(solution)/shard_map/ppermute | solution.py:290
  2.6 25.7 %copy-start.3 = (bf16[1,512,1024]{2,1,0:T(8,128)(2,1)S(1)}, bf16[1,512,1024]{2,1,0:T(8,128)(2,1)}, u32[]{:S(2)}) copy-start(bf16[1,512,1024]{2,1,0:T(8,128)(2,1)} %param.7) | copy-start | bytes 3145732
  2.6 25.7 %copy-start.4 = (bf16[1,512,1024]{2,1,0:T(8,128)(2,1)S(1)}, bf16[1,512,1024]{2,1,0:T(8,128)(2,1)}, u32[]{:S(2)}) copy-start(bf16[1,512,1024]{2,1,0:T(8,128)(2,1)} %param.8) | copy-start | bytes 3145732
  2.6 25.7 %collective-permute-start.6 = (bf16[512,1024]{1,0:T(8,128)(2,1)}, bf16[512,1024]{1,0:T(8,128)(2,1)}, u32[]{:S(2)}, u32[]{:S(2)}) collective-permute-start(bf16[512,1024]{1,0:T(8,128)(2,1)} %bitcast.32), channel_id=1, source_target_pairs={{0,4},{4,8},{8,12},{1,5},{5,9},{9,13},{2,6},{6,10},{10,14},{3,7},{... | collective-permute-start | bytes 3145736 | tf_op jit(solution)/shard_map/ppermute | solution.py:290
  7.8 41.7 %collective-permute-start.7 = (bf16[256,2048]{1,0:T(8,128)(2,1)}, bf16[256,2048]{1,0:T(8,128)(2,1)}, u32[]{:S(2)}, u32[]{:S(2)}) collective-permute-start(bf16[256,2048]{1,0:T(8,128)(2,1)} %get-tuple-element.38), channel_id=1, source_target_pairs={{0,1},{1,0},{2,3},{3,2},{4,5},{5,4},{6,7},{7,6},{8,9},{9,8},{10,11... | collective-permute-start | bytes 3145736 | tf_op jit(solution)/shard_map/ppermute | solution.py:299
  9.3 42.5 %collective-permute-start.9 = (bf16[256,2048]{1,0:T(8,128)(2,1)}, bf16[256,2048]{1,0:T(8,128)(2,1)}, u32[]{:S(2)}, u32[]{:S(2)}) collective-permute-start(bf16[256,2048]{1,0:T(8,128)(2,1)} %get-tuple-element.38), channel_id=1, source_target_pairs={{1,2},{2,1},{5,6},{6,5},{9,10},{10,9},{13,14},{14,13},{17,18},{18,... | collective-permute-start | bytes 3145736 | tf_op jit(solution)/shard_map/ppermute | solution.py:299
  11.3 50.2 %collective-permute-start = (bf16[256,2048]{1,0:T(8,128)(2,1)}, bf16[256,2048]{1,0:T(8,128)(2,1)}, u32[]{:S(2)}, u32[]{:S(2)}) collective-permute-start(bf16[256,2048]{1,0:T(8,128)(2,1)} %get-tuple-element.37), channel_id=1, source_target_pairs={{0,1},{1,0},{2,3},{3,2},{4,5},{5,4},{6,7},{7,6},{8,9},{9,8},{10,11... | collective-permute-start | bytes 3145736 | tf_op jit(solution)/shard_map/ppermute | solution.py:299
  17.9 44.8 %collective-permute-start.2 = (bf16[256,2048]{1,0:T(8,128)(2,1)}, bf16[256,2048]{1,0:T(8,128)(2,1)}, u32[]{:S(2)}, u32[]{:S(2)}) collective-permute-start(bf16[256,2048]{1,0:T(8,128)(2,1)} %get-tuple-element.37), channel_id=1, source_target_pairs={{1,2},{2,1},{5,6},{6,5},{9,10},{10,9},{13,14},{14,13},{17,18},{18,... | collective-permute-start | bytes 3145736 | tf_op jit(solution)/shard_map/ppermute | solution.py:299
  43.8 125.3 %copy-start = (bf16[512,1024]{1,0:T(8,128)(2,1)}, bf16[512,1024]{1,0:T(8,128)(2,1)S(1)}, u32[]{:S(2)}) copy-start(bf16[512,1024]{1,0:T(8,128)(2,1)S(1)} %get-tuple-element.22.att_ref.x_ref) | copy-start | bytes 3145732
  48.1 30.9 %collective-permute-start.22 = (bf16[256,2048]{1,0:T(8,128)(2,1)S(1)}, bf16[256,2048]{1,0:T(8,128)(2,1)S(1)}, u32[]{:S(2)}, u32[]{:S(2)}) collective-permute-start(bf16[256,2048]{1,0:T(8,128)(2,1)S(1)} %part.15), channel_id=1, source_target_pairs={{0,1},{3,2},{4,5},{7,6},{8,9},{11,10},{12,13},{15,14},{16,17},{19,... | collective-permute-start | bytes 3145736 | tf_op jit(solution)/shard_map/ppermute | solution.py:299
  49.4 38.3 %collective-permute-start.8 = (bf16[256,2048]{1,0:T(8,128)(2,1)}, bf16[256,2048]{1,0:T(8,128)(2,1)}, u32[]{:S(2)}, u32[]{:S(2)}) collective-permute-start(bf16[256,2048]{1,0:T(8,128)(2,1)} %collective-permute-done.7.refs_3_), channel_id=1, source_target_pairs={{1,2},{2,1},{5,6},{6,5},{9,10},{10,9},{13,14},{14,13},{17,18},{18,... | collective-permute-start | bytes 3145736 | tf_op jit(solution)/shard_map/ppermute | solution.py:299
  51.8 38.2 %collective-permute-start.10 = (bf16[256,2048]{1,0:T(8,128)(2,1)}, bf16[256,2048]{1,0:T(8,128)(2,1)}, u32[]{:S(2)}, u32[]{:S(2)}) collective-permute-start(bf16[256,2048]{1,0:T(8,128)(2,1)} %collective-permute-done.9.x_ref), channel_id=1, source_target_pairs={{1,0},{2,3},{5,4},{6,7},{9,8},{10,11},{13,12},{14,15},{17,16},{18,... | collective-permute-start | bytes 3145736 | tf_op jit(solution)/shard_map/ppermute | solution.py:299
  61.5 40.1 %collective-permute-start.16 = (bf16[256,2048]{1,0:T(8,128)(2,1)}, bf16[256,2048]{1,0:T(8,128)(2,1)}, u32[]{:S(2)}, u32[]{:S(2)}) collective-permute-start(bf16[256,2048]{1,0:T(8,128)(2,1)} %part.10), channel_id=1, source_target_pairs={{0,1},{3,2},{4,5},{7,6},{8,9},{11,10},{12,13},{15,14},{16,17},{19,... | collective-permute-start | bytes 3145736 | tf_op jit(solution)/shard_map/ppermute | solution.py:299
  62.8 45.3 %collective-permute-start.1 = (bf16[256,2048]{1,0:T(8,128)(2,1)}, bf16[256,2048]{1,0:T(8,128)(2,1)}, u32[]{:S(2)}, u32[]{:S(2)}) collective-permute-start(bf16[256,2048]{1,0:T(8,128)(2,1)} %collective-permute-done.refs_3_), channel_id=1, source_target_pairs={{1,2},{2,1},{5,6},{6,5},{9,10},{10,9},{13,14},{14,13},{17,18},{18,... | collective-permute-start | bytes 3145736 | tf_op jit(solution)/shard_map/ppermute | solution.py:299
  80.0 30.4 %collective-permute-start.3 = (bf16[256,2048]{1,0:T(8,128)(2,1)}, bf16[256,2048]{1,0:T(8,128)(2,1)S(1)}, u32[]{:S(2)}, u32[]{:S(2)}) collective-permute-start(bf16[256,2048]{1,0:T(8,128)(2,1)} %collective-permute-done.2.x_ref), channel_id=1, source_target_pairs={{1,0},{2,3},{5,4},{6,7},{9,8},{10,11},{13,12},{14,15},{17,16},{18,... | collective-permute-start | bytes 3145736 | tf_op jit(solution)/shard_map/ppermute | solution.py:299
  87.7 39.8 %collective-permute-start.23 = (bf16[256,2048]{1,0:T(8,128)(2,1)}, bf16[256,2048]{1,0:T(8,128)(2,1)}, u32[]{:S(2)}, u32[]{:S(2)}) collective-permute-start(bf16[256,2048]{1,0:T(8,128)(2,1)} %part.16), channel_id=1, source_target_pairs={{1,2},{2,1},{5,6},{6,5},{9,10},{10,9},{13,14},{14,13},{17,18},{18,... | collective-permute-start | bytes 3145736 | tf_op jit(solution)/shard_map/ppermute | solution.py:299
  90.0 45.4 %collective-permute-start.25 = (bf16[256,2048]{1,0:T(8,128)(2,1)}, bf16[256,2048]{1,0:T(8,128)(2,1)}, u32[]{:S(2)}, u32[]{:S(2)}) collective-permute-start(bf16[256,2048]{1,0:T(8,128)(2,1)} %part.16), channel_id=1, source_target_pairs={{0,1},{3,2},{4,5},{7,6},{8,9},{11,10},{12,13},{15,14},{16,17},{19,... | collective-permute-start | bytes 3145736 | tf_op jit(solution)/shard_map/ppermute | solution.py:299
  101.6 110.1 %collective-permute-start.28 = (bf16[1,512,2048]{2,1,0:T(8,128)(2,1)S(1)}, bf16[1,512,2048]{2,1,0:T(8,128)(2,1)}, u32[]{:S(2)}, u32[]{:S(2)}) collective-permute-start(bf16[1,512,2048]{2,1,0:T(8,128)(2,1)S(1)} %copy-done.2), channel_id=1, source_target_pairs={{16,0},{0,16},{17,1},{1,17},{18,2},{2,18},{19,3},{3,19},{20,4},{4,... | collective-permute-start | bytes 6291464 | tf_op jit(solution)/shard_map/ppermute | solution.py:295
  108.0 55.0 %collective-permute-start.17 = (bf16[256,2048]{1,0:T(8,128)(2,1)}, bf16[256,2048]{1,0:T(8,128)(2,1)}, u32[]{:S(2)}, u32[]{:S(2)}) collective-permute-start(bf16[256,2048]{1,0:T(8,128)(2,1)} %part.11), channel_id=1, source_target_pairs={{1,2},{2,1},{5,6},{6,5},{9,10},{10,9},{13,14},{14,13},{17,18},{18,... | collective-permute-start | bytes 3145736 | tf_op jit(solution)/shard_map/ppermute | solution.py:299
  111.4 55.8 %collective-permute-start.19 = (bf16[256,2048]{1,0:T(8,128)(2,1)}, bf16[256,2048]{1,0:T(8,128)(2,1)}, u32[]{:S(2)}, u32[]{:S(2)}) collective-permute-start(bf16[256,2048]{1,0:T(8,128)(2,1)} %part.11), channel_id=1, source_target_pairs={{0,1},{3,2},{4,5},{7,6},{8,9},{11,10},{12,13},{15,14},{16,17},{19,... | collective-permute-start | bytes 3145736 | tf_op jit(solution)/shard_map/ppermute | solution.py:299
  127.5 45.6 %collective-permute-start.4 = (bf16[256,2048]{1,0:T(8,128)(2,1)}, bf16[256,2048]{1,0:T(8,128)(2,1)S(1)}, u32[]{:S(2)}, u32[]{:S(2)}) collective-permute-start(bf16[256,2048]{1,0:T(8,128)(2,1)} %collective-permute-done.1.refs_1_), channel_id=1, source_target_pairs={{1,0},{2,3},{5,4},{6,7},{9,8},{10,11},{13,12},{14,15},{17,16},{18,... | collective-permute-start | bytes 3145736 | tf_op jit(solution)/shard_map/ppermute | solution.py:299
  135.4 57.4 %collective-permute-start.11 = (bf16[256,2048]{1,0:T(8,128)(2,1)}, bf16[256,2048]{1,0:T(8,128)(2,1)}, u32[]{:S(2)}, u32[]{:S(2)}) collective-permute-start(bf16[256,2048]{1,0:T(8,128)(2,1)} %collective-permute-done.8.refs_1_), channel_id=1, source_target_pairs={{1,0},{2,3},{5,4},{6,7},{9,8},{10,11},{13,12},{14,15},{17,16},{18,... | collective-permute-start | bytes 3145736 | tf_op jit(solution)/shard_map/ppermute | solution.py:299
  163.0 63.6 %collective-permute-start.24 = (bf16[256,2048]{1,0:T(8,128)(2,1)S(1)}, bf16[256,2048]{1,0:T(8,128)(2,1)S(1)}, u32[]{:S(2)}, u32[]{:S(2)}) collective-permute-start(bf16[256,2048]{1,0:T(8,128)(2,1)S(1)} %part.17), channel_id=1, source_target_pairs={{0,1},{1,0},{2,3},{3,2},{4,5},{5,4},{6,7},{7,6},{8,9},{9,8},{10,11... | collective-permute-start | bytes 3145736 | tf_op jit(solution)/shard_map/ppermute | solution.py:299
  167.2 61.4 %collective-permute-start.26 = (bf16[256,2048]{1,0:T(8,128)(2,1)S(1)}, bf16[256,2048]{1,0:T(8,128)(2,1)S(1)}, u32[]{:S(2)}, u32[]{:S(2)}) collective-permute-start(bf16[256,2048]{1,0:T(8,128)(2,1)S(1)} %part.18), channel_id=1, source_target_pairs={{1,2},{2,1},{5,6},{6,5},{9,10},{10,9},{13,14},{14,13},{17,18},{18,... | collective-permute-start | bytes 3145736 | tf_op jit(solution)/shard_map/ppermute | solution.py:299
  173.2 61.6 %collective-permute-start.18 = (bf16[256,2048]{1,0:T(8,128)(2,1)S(1)}, bf16[256,2048]{1,0:T(8,128)(2,1)S(1)}, u32[]{:S(2)}, u32[]{:S(2)}) collective-permute-start(bf16[256,2048]{1,0:T(8,128)(2,1)S(1)} %part.12), channel_id=1, source_target_pairs={{0,1},{1,0},{2,3},{3,2},{4,5},{5,4},{6,7},{7,6},{8,9},{9,8},{10,11... | collective-permute-start | bytes 3145736 | tf_op jit(solution)/shard_map/ppermute | solution.py:299
  192.8 43.6 %collective-permute-start.20 = (bf16[256,2048]{1,0:T(8,128)(2,1)S(1)}, bf16[256,2048]{1,0:T(8,128)(2,1)S(1)}, u32[]{:S(2)}, u32[]{:S(2)}) collective-permute-start(bf16[256,2048]{1,0:T(8,128)(2,1)S(1)} %part.13), channel_id=1, source_target_pairs={{1,2},{2,1},{5,6},{6,5},{9,10},{10,9},{13,14},{14,13},{17,18},{18,... | collective-permute-start | bytes 3145736 | tf_op jit(solution)/shard_map/ppermute | solution.py:299
  211.7 8.7 %collective-permute-start.13 = (bf16[256,1024]{1,0:T(8,128)(2,1)S(1)}, bf16[256,1024]{1,0:T(8,128)(2,1)S(1)}, u32[]{:S(2)}, u32[]{:S(2)}) collective-permute-start(bf16[256,1024]{1,0:T(8,128)(2,1)S(1)} %get-tuple-element.32), channel_id=1, source_target_pairs={{4,0},{8,4},{12,8},{5,1},{9,5},{13,9},{6,2},{10,6},{14,10},{7,3},{... | collective-permute-start | bytes 1572872 | tf_op jit(solution)/shard_map/ppermute | solution.py:290
  220.4 20.8 %collective-permute-start.12 = (bf16[256,1024]{1,0:T(8,128)(2,1)}, bf16[256,1024]{1,0:T(8,128)(2,1)S(1)}, u32[]{:S(2)}, u32[]{:S(2)}) collective-permute-start(bf16[256,1024]{1,0:T(8,128)(2,1)} %copy-done.27), channel_id=1, source_target_pairs={{4,0},{8,4},{12,8},{5,1},{9,5},{13,9},{6,2},{10,6},{14,10},{7,3},{... | collective-permute-start | bytes 1572872 | tf_op jit(solution)/shard_map/ppermute | solution.py:290
  226.6 15.8 %collective-permute-start.15 = (bf16[256,1024]{1,0:T(8,128)(2,1)S(1)}, bf16[256,1024]{1,0:T(8,128)(2,1)S(1)}, u32[]{:S(2)}, u32[]{:S(2)}) collective-permute-start(bf16[256,1024]{1,0:T(8,128)(2,1)S(1)} %get-tuple-element.36), channel_id=1, source_target_pairs={{4,0},{8,4},{12,8},{5,1},{9,5},{13,9},{6,2},{10,6},{14,10},{7,3},{... | collective-permute-start | bytes 1572872 | tf_op jit(solution)/shard_map/ppermute | solution.py:290
  228.6 14.2 %collective-permute-start.14 = (bf16[256,1024]{1,0:T(8,128)(2,1)S(1)}, bf16[256,1024]{1,0:T(8,128)(2,1)S(1)}, u32[]{:S(2)}, u32[]{:S(2)}) collective-permute-start(bf16[256,1024]{1,0:T(8,128)(2,1)S(1)} %copy-done.26), channel_id=1, source_target_pairs={{4,0},{8,4},{12,8},{5,1},{9,5},{13,9},{6,2},{10,6},{14,10},{7,3},{... | collective-permute-start | bytes 1572872 | tf_op jit(solution)/shard_map/ppermute | solution.py:290
  234.8 26.0 %collective-permute-start.27 = (bf16[256,2048]{1,0:T(8,128)(2,1)S(1)}, bf16[256,2048]{1,0:T(8,128)(2,1)S(1)}, u32[]{:S(2)}, u32[]{:S(2)}) collective-permute-start(bf16[256,2048]{1,0:T(8,128)(2,1)S(1)} %part.19), channel_id=1, source_target_pairs={{16,0},{0,16},{17,1},{1,17},{18,2},{2,18},{19,3},{3,19},{20,4},{4,... | collective-permute-start | bytes 3145736 | tf_op jit(solution)/shard_map/ppermute | solution.py:295
  240.7 42.3 %collective-permute-start.21 = (bf16[256,2048]{1,0:T(8,128)(2,1)S(1)}, bf16[256,2048]{1,0:T(8,128)(2,1)S(1)}, u32[]{:S(2)}, u32[]{:S(2)}) collective-permute-start(bf16[256,2048]{1,0:T(8,128)(2,1)S(1)} %part.14), channel_id=1, source_target_pairs={{16,0},{0,16},{17,1},{1,17},{18,2},{2,18},{19,3},{3,19},{20,4},{4,... | collective-permute-start | bytes 3145736 | tf_op jit(solution)/shard_map/ppermute | solution.py:295
  (27 other events, 119.9 us)

commit v2 on v0

v2 whole, which is shorter than its diff:
```python
import functools

import jax
import jax.numpy as jnp
from jax import lax
from jax.experimental import pallas as pl
from jax.experimental.pallas import tpu as pltpu
from jax.sharding import PartitionSpec as P

HD = 128
WINDOW = 512
NEG = -1e30
HALF = 256
PIECES = [(0, 256), (256, 128), (384, 128)]
PAIR = 2
VMEM_LIMIT = 50 * 1024 * 1024
COST = 1.0

OUTER = [(0, 1), (1, 0), (2, 3), (3, 2)]
MIDDLE = [(1, 2), (2, 1)]
OUTER_INWARD = [(0, 1), (3, 2)]
OUTER_OUTWARD = [(1, 0), (2, 3)]


def params():
    return pltpu.CompilerParams(vmem_limit_bytes=VMEM_LIMIT)


def dot(a, b, contract):
    return lax.dot_general(a, b, ((contract[0], contract[1]), ((), ())), preferred_element_type=jnp.float32)


def nt(a, b):
    return dot(a, b, ((1,), (1,)))


def nn(a, b):
    return dot(a, b, ((1,), (0,)))


def tn(a, b):
    return dot(a, b, ((0,), (0,)))


def lower(size):
    row = lax.broadcasted_iota(jnp.int32, (size, size), 0)
    col = lax.broadcasted_iota(jnp.int32, (size, size), 1)
    return col <= row


def forward_kernel(index_ref, doc_ref, q_ref, k_ref, v_ref, kp_ref, vp_ref, att_ref, w_ref, bias_ref):
    rows = q_ref.shape[0]
    scaling = HD ** (-0.5)

    @pl.when(pl.program_id(0) == 0)
    def _():
        index = index_ref[0]
        own = doc_ref[:, pl.ds(pl.multiple_of(index * rows, rows), rows)]
        before = doc_ref[:, pl.ds(pl.multiple_of(jnp.maximum(index - 1, 0) * rows, rows), rows)]
        before = jnp.where(index > 0, before, -1)
        own = jnp.broadcast_to(own, (rows, rows))
        before = jnp.broadcast_to(before, (rows, rows))
        key_doc = jnp.where(lower(rows), own, before)
        bias_ref[...] = jnp.where(key_doc == own.T, 0.0, NEG)

    tri = lower(HALF)
    for head in range(q_ref.shape[1] // HD):
        cols = pl.ds(head * HD, HD)
        for qb in range(2):
            qs = pl.ds(qb * HALF, HALF)
            ks = pl.ds((1 - qb) * HALF, HALF)
            q = q_ref[qs, cols]
            diagonal = jnp.where(tri, nt(q, k_ref[qs, cols]), nt(q, kp_ref[qs, cols]))
            if qb == 0:
                scores = jnp.concatenate([diagonal, nt(q, kp_ref[ks, cols])], 1)
            else:
                scores = jnp.concatenate([nt(q, k_ref[ks, cols]), diagonal], 1)
            scores = scores * scaling + bias_ref[qs, :]
            row_max = jnp.max(scores, axis=1, keepdims=True)
            exponent = jnp.exp(scores - row_max)
            row_sum = jnp.sum(exponent, axis=1, keepdims=True)
            prob = exponent * (1.0 / row_sum)
            w_ref[head, qs, :] = prob.astype(jnp.bfloat16)
            mine = prob[:, qb * HALF : (qb + 1) * HALF]
            rest = prob[:, (1 - qb) * HALF : (2 - qb) * HALF].astype(jnp.bfloat16)
            mine_own = jnp.where(tri, mine, 0.0).astype(jnp.bfloat16)
            mine_before = jnp.where(tri, 0.0, mine).astype(jnp.bfloat16)
            att = nn(mine_own, v_ref[qs, cols]) + nn(mine_before, vp_ref[qs, cols])
            att = att + nn(rest, (vp_ref if qb == 0 else v_ref)[ks, cols])
            att_ref[qs, cols] = att.astype(jnp.bfloat16)


def cost(flops, moved, transcendentals=0):
    return pl.CostEstimate(flops=int(flops * COST), bytes_accessed=int(moved * COST), transcendentals=int(transcendentals * COST))


ANY = pl.BlockSpec(memory_space=pl.ANY)


def call(kernel, index, grid, blocked, after, out_specs, out_shape, moved, flops, name, scratch=(), aliases=None):
    count = len(blocked)
    waits = len(after)
    outs = len(out_shape)

    def run(index_ref, *refs):
        kernel(index_ref, *refs[:count], *refs[count + waits : count + waits + outs], *refs[count + waits + outs + 1 :])
        refs[count + waits + outs][0, 0] = jnp.float32(0.0)

    result = pl.pallas_call(
        run,
        grid_spec=pltpu.PrefetchScalarGridSpec(
            num_scalar_prefetch=1,
            grid=grid,
            in_specs=[spec for _, spec in blocked] + [ANY] * waits,
            out_specs=list(out_specs) + [pl.BlockSpec((1, 1), lambda *_: (0, 0), memory_space=pltpu.SMEM)],
            scratch_shapes=list(scratch),
        ),
        out_shape=list(out_shape) + [jax.ShapeDtypeStruct((1, 1), jnp.float32)],
        input_output_aliases=aliases or {},
        compiler_params=params(),
        cost_estimate=cost(flops, moved),
        name=name,
    )(index, *[x for x, _ in blocked], *after)
    return result[:-1], result[-1].reshape(())


def tie(index, after):
    _, zero = call(lambda index_ref: None, index, (1,), [], after, [], [], 8192, 0, "tie")
    return zero


def forward(index, doc, q, k, v, kp, vp):
    rows, feature = q.shape
    heads = feature // HD
    head = pl.BlockSpec((rows, PAIR * HD), lambda h, *_: (0, h))
    return call(
        forward_kernel, index, (heads // PAIR,),
        [(doc, pl.BlockSpec(doc.shape, lambda h, *_: (0, 0)))] + [(x, head) for x in (q, k, v, kp, vp)], [],
        [head, pl.BlockSpec((PAIR, rows, rows), lambda h, *_: (h, 0, 0))],
        [jax.ShapeDtypeStruct((rows, feature), jnp.bfloat16), jax.ShapeDtypeStruct((heads, rows, rows), jnp.bfloat16)],
        2**23, 12 * 2 * 2**23 * heads, "attend", scratch=[pltpu.VMEM((rows, rows), jnp.float32)],
    )


def project(weight, index, groups, total, after):
    rows = sum(piece[0].shape[0] for piece in groups[0])
    depth = groups[0][0][0].shape[1]
    out_rows = weight.shape[0]
    block = 256
    shape = [[(len(piece), piece[0].shape[0]) for piece in g] for g in groups]
    has_total = total is not None

    def kernel(index_ref, *refs):
        refs = list(refs)
        w = [refs.pop(0)[...] for _ in groups]
        out_ref = refs[-1]
        start = 0
        base = refs[-2] if has_total else None
        sums = {}
        for j, pieces in enumerate(shape):
            start = 0
            for many, height in pieces:
                x = refs.pop(0)[...]
                for _ in range(many - 1):
                    x = x + refs.pop(0)[...]
                term = nt(x, w[j])
                key = (start, height)
                at = pl.ds(start, height)
                if j == 0:
                    out_ref[at, :] = term + base[at, :] if has_total else term
                else:
                    out_ref[at, :] += term
                start += height

    blocked = [(weight, pl.BlockSpec((block, depth), lambda n, idx, j=j: (n, idx[j]))) for j in range(len(groups))]
    for g in groups:
        for piece in g:
            for x in piece:
                blocked.append((x, pl.BlockSpec(x.shape, lambda n, idx: (0, 0))))
    if has_total:
        blocked.append((total, pl.BlockSpec((rows, block), lambda n, idx: (0, n))))
    return call(
        kernel, index, (out_rows // block,), blocked, after,
        [pl.BlockSpec((rows, block), lambda n, idx: (0, n))],
        [jax.ShapeDtypeStruct((rows, out_rows), jnp.float32)],
        2 * out_rows * depth * len(groups), 2 * rows * depth * out_rows * len(groups), "project",
    )


def parts(weight, index, attended, count, after, stream=None):
    rows, depth = attended.shape
    width = weight.shape[1] // 4
    block = 512
    steps = width // block

    def kernel(index_ref, x_ref, *refs):
        base = count + (stream is not None)
        for j in range(count):
            out = nn(x_ref[...], refs[j][...])
            if stream is not None and j == count - 1:
                out = refs[count][...].astype(jnp.float32) - out
            out = out.astype(jnp.bfloat16)
            refs[base + 2 * j][...] = out[:HALF]
            refs[base + 2 * j + 1][...] = out[HALF:]

    blocked = [(attended, pl.BlockSpec((rows, depth), lambda n, idx: (0, 0)))]
    for j in range(count):
        blocked.append((weight, pl.BlockSpec((depth, block), lambda n, idx, j=j: (0, idx[j] * steps + n))))
    if stream is not None:
        blocked.append((stream, pl.BlockSpec((rows, block), lambda n, idx: (0, n))))
    return call(
        kernel, index, (steps,), blocked, after,
        [pl.BlockSpec((HALF, block), lambda n, idx: (0, n))] * (2 * count),
        [jax.ShapeDtypeStruct((HALF, width), jnp.bfloat16)] * (2 * count),
        count * 2 * depth * width, 2 * rows * depth * width * count, "parts",
    )


def place(index, whole, rows, piece, start, after):
    height, width = piece.shape
    extra = list(after)
    aliases = None
    if whole is not None:
        extra = [whole] + extra
        aliases = {2: 0}

    def kernel(index_ref, x_ref, out_ref):
        out_ref[...] = x_ref[...]

    (out,), zero = call(
        kernel, index, (1,), [(piece, pl.BlockSpec((height, width), lambda n, idx: (0, 0)))], extra,
        [pl.BlockSpec((height, width), lambda n, idx: (start // height, 0))],
        [jax.ShapeDtypeStruct((rows, width), piece.dtype)],
        4 * height * width, 0, "place", aliases=aliases,
    )
    return out, zero


def settle(index, grad_keys, grad_values, k1, v1, back, after):
    height, width = k1.shape
    rows = grad_keys.shape[0]
    wide = 512

    def kernel(index_ref, k_ref, v_ref, back_ref, *refs):
        gk_ref, gv_ref = refs[-2:]
        gk_ref[...] = (k_ref[...] + back_ref[0].astype(jnp.float32)).astype(jnp.bfloat16)
        gv_ref[...] = (v_ref[...] + back_ref[1].astype(jnp.float32)).astype(jnp.bfloat16)

    flat = pl.BlockSpec((height, wide), lambda n, idx: (0, n))
    late = pl.BlockSpec((height, wide), lambda n, idx: (rows // height - 1, n))
    out = jax.ShapeDtypeStruct((rows, width), jnp.bfloat16)
    return call(
        kernel, index, (width // wide,),
        [(k1, flat), (v1, flat), (back, pl.BlockSpec((2, height, wide), lambda n, idx: (0, 0, n)))],
        [grad_keys, grad_values] + list(after), [late, late], [out, out],
        16 * height * width, 0, "settle", aliases={4: 0, 5: 1},
    )


def total_of(*terms):
    result = terms[0].astype(jnp.float32)
    for x in terms[1:]:
        result = result + x.astype(jnp.float32)
    return result


def backward(qb, weight, index, total, outer, middle, probs, attended, q, k, v, kp, vp, carried, after):
    rows, feature = q.shape
    heads = feature // HD
    depth = outer.shape[1]
    wide = PAIR * HD
    scaling = HD ** (-0.5)
    bf = jnp.bfloat16
    skip = len(after) + (1 if qb else 0)

    def kernel(index_ref, w_ref, total_ref, outer_ref, middle_ref, p_ref, att_ref, q_ref, k_ref, v_ref, kp_ref, vp_ref, *refs):
        refs = refs[skip:]
        carry = refs[:5] if qb else ()
        dq_ref, send_ref, k0_ref, v0_ref, k1_ref, v1_ref, x_ref = refs[len(carry) :]

        @pl.when((pl.program_id(0) == 0) & (index_ref[1] == 1))
        def _():
            x_ref[...] = outer_ref[...]

        @pl.when((pl.program_id(0) == 0) & (index_ref[1] == 0))
        def _():
            x_ref[...] = middle_ref[...]

        qs = pl.ds(qb * HALF, HALF)
        ks = pl.ds((1 - qb) * HALF, HALF)
        tri = lower(HALF)
        d_out_pair = (total_ref[...] + nt(x_ref[...], w_ref[...])).astype(bf)
        for head in range(PAIR):
            cols = pl.ds(head * HD, HD)
            d_out = d_out_pair[:, head * HD : (head + 1) * HD]
            row_delta = jnp.sum(
                d_out.astype(jnp.float32) * att_ref[:, cols].astype(jnp.float32), axis=1, keepdims=True
            )
            qh = q_ref[:, cols]
            k_rest_ref, v_rest_ref = (k_ref, v_ref) if qb else (kp_ref, vp_ref)
            k_rest, v_rest = k_rest_ref[ks, cols], v_rest_ref[ks, cols]
            p_diag = p_ref[head, :, qb * HALF : (qb + 1) * HALF].astype(jnp.float32)
            p_rest = p_ref[head, :, (1 - qb) * HALF : (2 - qb) * HALF]
            dp_diag = jnp.where(tri, nt(d_out, v_ref[qs, cols]), nt(d_out, vp_ref[qs, cols]))
            dp_rest = nt(d_out, v_rest)
            ds_diag = p_diag * (dp_diag - row_delta)
            ds_rest = (p_rest.astype(jnp.float32) * (dp_rest - row_delta)).astype(bf)
            ds_own = jnp.where(tri, ds_diag, 0.0).astype(bf)
            ds_before = jnp.where(tri, 0.0, ds_diag).astype(bf)
            p_own = jnp.where(tri, p_diag, 0.0).astype(bf)
            p_before = jnp.where(tri, 0.0, p_diag).astype(bf)
            dq = nn(ds_own, k_ref[qs, cols]) + nn(ds_before, kp_ref[qs, cols]) + nn(ds_rest, k_rest)
            dq_ref[:, cols] = (dq * scaling).astype(bf)
            dk_own, dv_own = tn(ds_own, qh) * scaling, tn(p_own, d_out)
            dk_before, dv_before = tn(ds_before, qh) * scaling, tn(p_before, d_out)
            dk_rest, dv_rest = tn(ds_rest, qh) * scaling, tn(p_rest, d_out)
            if qb == 0:
                send_ref[0, :, cols] = dk_before.astype(bf)
                send_ref[1, :, cols] = dv_before.astype(bf)
                k0_ref[:, cols], v0_ref[:, cols] = dk_own, dv_own
                k1_ref[:, cols], v1_ref[:, cols] = dk_rest, dv_rest
            else:
                k0i, v0i, kri, vri, back = carry
                send_ref[0, :, cols] = (dk_before + kri[:, cols]).astype(bf)
                send_ref[1, :, cols] = (dv_before + vri[:, cols]).astype(bf)
                k0_ref[:, cols] = (dk_rest + k0i[:, cols] + back[0, :, cols].astype(jnp.float32)).astype(bf)
                v0_ref[:, cols] = (dv_rest + v0i[:, cols] + back[1, :, cols].astype(jnp.float32)).astype(bf)
                k1_ref[:, cols], v1_ref[:, cols] = dk_own, dv_own

    whole = pl.BlockSpec((rows, wide), lambda h, *_: (0, h))
    half = pl.BlockSpec((HALF, wide), lambda h, *_: (0, h))
    mine = pl.BlockSpec((HALF, wide), lambda h, *_: (qb, h))
    blocked = [
        (weight, pl.BlockSpec((wide, depth), lambda h, idx: (h, idx[0]))),
        (total, mine),
        (outer, pl.BlockSpec((HALF, depth), lambda h, *_: (0, 0))),
        (middle, pl.BlockSpec((HALF, depth), lambda h, *_: (qb, 0))),
        (probs, pl.BlockSpec((PAIR, HALF, rows), lambda h, *_: (h, qb, 0))),
        (attended, mine),
        (q, mine),
        (k, whole),
        (v, whole),
        (kp, whole),
        (vp, whole),
    ]
    aliases = {}
    extra = list(after)
    if qb:
        extra = [carried[0]] + extra
        aliases = {1 + len(blocked): 0}
    pair = pl.BlockSpec((2, HALF, wide), lambda h, *_: (0, 0, h))
    blocked += [(x, ANY) for x in extra] + [(x, half) for x in carried[1:5]] + [(x, pair) for x in carried[5:]]
    f32_out = jax.ShapeDtypeStruct((HALF, feature), jnp.float32)
    whole_out = jax.ShapeDtypeStruct((rows, feature), bf)
    return call(
        kernel, index, (heads // PAIR,), blocked, [],
        [mine, pair] + [half] * 4,
        [whole_out, jax.ShapeDtypeStruct((2, HALF, feature), bf)] + [whole_out if qb else f32_out] * 2 + [f32_out] * 2,
        16 * 2**20, 2 * HALF * depth * feature * 3, "backward", aliases=aliases,
        scratch=[pltpu.VMEM((HALF, depth), bf)],
    )


def from_behind(block, axis, distance):
    devices = range(lax.axis_size(axis))
    route = [(i - distance, i) for i in devices if i - distance in devices]
    return lax.ppermute(block, axis, route)


def shifted(block, axis, distance):
    count = lax.axis_size(axis)
    return lax.ppermute(block, axis, [((i - distance) % count, i) for i in range(count)])


def hop(block, pairs):
    return lax.ppermute(block, "tp", pairs)


def body(queries, keys, values, stream, grad_stream, out_proj, doc_ids):
    q, k, v, weight = queries[0], keys[0], values[0], out_proj[0]
    grad = grad_stream[0]
    rows, feature = q.shape
    chunks = rows // HALF
    me = lax.axis_index("tp").astype(jnp.int32)
    ctx = lax.axis_index("ctx").astype(jnp.int32)
    near, across, far = me ^ 1, me ^ 2, 3 - me
    one = lambda x: x.reshape(1)

    idx = one(me)
    end = (me == 0) | (me == 3)
    bf = jnp.bfloat16
    half = lambda x, c: x[c * HALF : (c + 1) * HALF]
    both = range(chunks)

    kp = from_behind(k, "ctx", 1)
    vp = from_behind(v, "ctx", 1)
    o1 = hop(grad, OUTER)
    m1 = hop(grad, MIDDLE)
    grad_next = shifted(grad, "pipe", -1)
    (attended, probs), _ = forward(one(ctx), doc_ids, q, k, v, kp, vp)
    pa, zero = parts(weight, one(far), attended, 1, [])
    to_m2, to_x2 = [], []
    for c in both:
        to_x2.append(total_of(jnp.where(end, pa[c], half(m1, c)), zero).astype(bf))
        to_m2.append(total_of(half(o1, c), zero).astype(bf))
        zero = tie(idx, [to_m2[c], to_x2[c]])
    m2 = [hop(x, MIDDLE) for x in to_m2]
    x2 = [hop(x, OUTER) for x in to_x2]
    (pb0, pb1, pc0, pc1, pd0, pd1), _ = parts(weight, jnp.stack([across, near, me]), attended, 3, to_m2 + to_x2, stream[0])
    pb, pc, pd = (pb0, pb1), (pc0, pc1), (pd0, pd1)
    (total,), zero = project(weight, jnp.stack([me, near]), [[(grad,)], [(o1,)]], None, [pb0])
    n3, x3 = [], []
    for c in both:
        to_n3 = total_of(pb[c], x2[c], zero).astype(bf)
        to_x3 = total_of(jnp.where(end, pb[c], m2[c]), zero).astype(bf)
        n3.append(hop(to_n3, MIDDLE))
        x3.append(hop(to_x3, OUTER))
        if c == 0:
            zero = tie(idx, [to_n3, to_x3])
    (total,), zero = project(
        weight, one(across), [[(jnp.where(end, x2[c], m2[c]),) for c in both]], total, [to_n3, to_x3]
    )
    next_grad, zero = place(idx, None, 2 * HALF, grad_next, 0, [total])
    far_and_end = jnp.stack([far, end.astype(jnp.int32)])
    hops = {}

    def launch(p, zero):
        at, height = PIECES[p]
        c = at // HALF
        piece = slice(at - c * HALF, at - c * HALF + height)
        to_f4 = total_of(pc[c][piece], n3[c][piece], zero).astype(bf)
        to_n4 = total_of(pa[c][piece], x3[c][piece], zero).astype(bf)
        hops[p] = (hop(to_f4, OUTER), hop(to_n4, MIDDLE))
        return [to_f4, to_n4]

    arrived, done = [], []

    def finish(p, zero):
        at, height = PIECES[p]
        c = at // HALF
        own = pd[c][at - c * HALF : at - c * HALF + height]
        rebuilt = (own.astype(jnp.float32) - total_of(*hops[p], zero)).astype(bf)
        arrived.append(shifted(rebuilt, "pipe", -1))
        done.append(rebuilt)
        return tie(idx, [rebuilt])

    sends = launch(0, zero)
    (dq, send0, k0, v0, k1, v1), zero = backward(
        0, weight, far_and_end, total, x3[0], m1, probs, attended, q, k, v, kp, vp, (), sends
    )
    back0 = from_behind(send0, "ctx", -1)
    sends = launch(1, zero) + launch(2, zero)
    zero = tie(idx, sends)
    finish(0, zero)
    (dq, send1, grad_keys, grad_values, k1, v1), zero = backward(
        1, weight, far_and_end, total, x3[1], m1, probs, attended, q, k, v, kp, vp, (dq, k0, v0, k1, v1, back0), [done[0]]
    )
    back1 = from_behind(send1, "ctx", -1)
    zero = finish(1, zero)
    finish(2, zero)
    (grad_keys, grad_values), _ = settle(idx, grad_keys, grad_values, k1, v1, back1, [done[2]])
    stream_next, after = None, [grad_keys]
    for (at, height), piece in zip(PIECES, arrived):
        stream_next, _ = place(idx, stream_next, 2 * HALF, piece, at, after)
        after = []
    return tuple(x[None] for x in (dq, grad_keys, grad_values, stream_next, next_grad))


def solution(mesh):
    cut = P("pipe", "ctx", "tp")
    in_specs = (cut, cut, cut, cut, cut, P("pipe", "tp", None), P("pipe", None))
    out_specs = (cut, cut, cut, cut, cut)
    return jax.shard_map(body, mesh=mesh, in_specs=in_specs, out_specs=out_specs, check_vma=False)
```

time: 413 us -> 231 us (0.56)
  waiting for transfers between devices: 233 us -> 39.7 us
  Pallas kernels: 0 us -> 77.9 us
  matrix products: 74.8 us -> 0 us
  starting transfers between devices: 8.21 us -> 76.8 us
  local copies, waits for them, and re-layouts: 39.2 us -> 5.41 us
  other arithmetic: 42.9 us -> 28.2 us
  between operations: 14.3 us -> 1.28 us
    reduce_scatter x1 -> x0, waiting for transfers between devices: 108 us -> none  [body(): lax.psum_scatter(partial_value, 'tp', scatter_dimension=1, tiled=True)]
    all_gather x1 -> x0, waiting for transfers between devices: 97.5 us -> none  [body(): lax.all_gather(grad_rows, 'tp', axis=1, tiled=True)]
    pallas_call x0 -> x16, Pallas kernels: none -> 77.9 us  [call(): pl.pallas_call(run, grid_spec=pltpu.PrefetchScalarGridSpec(num_scalar_pre...]
    dot_general x8 -> x0, matrix products: 74.8 us -> none  [the longest x1 16.9 us: body(): jnp.dot(attended_flat, weight, preferred_element_type=jnp.float32)]
    ppermute x2 -> x20, starting transfers between devices: 3.03 us -> 67.6 us  [the longest x16 62.3 us: hop(): return lax.ppermute(block, 'tp', pairs)]
    sub x1 -> x0, other arithmetic: 18.4 us -> none  [block_terms(): exponent = jnp.where(visible[None], jnp.exp(masked - row_max), 0.0)]
    unnamed x35 -> x40, local copies, waits for them, and re-layouts: 18.5 us -> 5.41 us
    ppermute x2 -> x20, waiting for transfers between devices: 26.9 us -> 39.6 us  [the longest x4 23.7 us: shifted(): lax.ppermute(block, axis, [((i - distance) % count, i) for i in range(cou...]
  transfers between devices with their start and end apart: 6 -> 24, of which waited for: 3 -> 6; matrix products, arithmetic and copies ran while one was open for 25% -> 12% of each run, Pallas kernels for 0% -> 34%
where the time goes in v2:
time: 231 us; the launch traced here: 229 us
  Pallas kernels  77.9 us (34%)
  starting transfers between devices  76.8 us (33%)
  waiting for transfers between devices  39.7 us (17%)
  other arithmetic  28.2 us (12%)
  local copies, waits for them, and re-layouts  5.41 us (2%)
    pallas_call x16, Pallas kernels, call(): pl.pallas_call(run, grid_spec=pltpu.PrefetchScalarGridSpec(num_scalar_pre...  77.9 us
    ppermute x16, starting transfers between devices, hop(): return lax.ppermute(block, 'tp', pairs)  62.3 us
    ppermute x4, waiting for transfers between devices, shifted(): lax.ppermute(block, axis, [((i - distance) % count, i) for i in range(cou...  23.7 us
    ppermute x16, waiting for transfers between devices, hop(): return lax.ppermute(block, 'tp', pairs)  15.9 us
    ppermute x4, starting transfers between devices, from_behind(): return lax.ppermute(block, axis, route)  9.23 us
    convert_element_type x2, other arithmetic, body(): to_x3 = total_of(jnp.where(end, pb[c], m2[c]), zero).astype(bf)  6.03 us
    convert_element_type x2, other arithmetic, body(): to_x2.append(total_of(jnp.where(end, pa[c], half(m1, c)), zero).astype(bf))  5.51 us
    unnamed x40, local copies, waits for them, and re-layouts  5.41 us
  transfers between devices with their start and end apart: 24, of which 6 were waited for; matrix products, arithmetic and copies ran while one was open for 12% of the time, Pallas kernels for 34%

profile of v2, /device:TPU:0, one launch (start us, length us, event | category | flops | bytes accessed | tf_op | source)
XLA Modules:
  0.0 229.3 jit_solution(5430960804765371444)
XLA Ops:
  0.6 2.0 collective-permute-start.2
  2.6 4.6 %collective-permute-start.4 = (bf16[512,2048]{1,0:T(8,128)(2,1)}, bf16[512,2048]{1,0:T(8,128)(2,1)}, u32[]{:S(2)}, u32[]{:S(2)}) collective-permute-start(bf16[512,2048]{1,0:T(8,128)(2,1)} %bitcast.50), channel_id=1, source_target_pairs={{0,1},{1,0},{2,3},{3,2},{4,5},{5,4},{6,7},{7,6},{8,9},{9,8},{10,11... | collective-permute-start | bytes 6291464 | tf_op jit(solution)/shard_map/ppermute | solution.py:376
  8.6 5.0 %collective-permute-start.1 = (bf16[512,1024]{1,0:T(8,128)(2,1)}, bf16[512,1024]{1,0:T(8,128)(2,1)}, u32[]{:S(2)}, u32[]{:S(2)}) collective-permute-start(bf16[512,1024]{1,0:T(8,128)(2,1)} %bitcast.44), channel_id=1, source_target_pairs={{0,4},{4,8},{8,12},{1,5},{5,9},{9,13},{2,6},{6,10},{10,14},{3,7},{... | collective-permute-start | bytes 3145736 | tf_op jit(solution)/shard_map/ppermute | solution.py:367
  19.5 11.6 %attend.1 = (bf16[512,1024]{1,0:T(8,128)(2,1)S(1)}, bf16[8,512,512]{2,1,0:T(8,128)(2,1)}, f32[1,1]{1,0:T(1,128)}) custom-call(s32[1]{0:T(128)} %bitcast.4.index_ref, s32[1,2048]{1,0:T(1,128)S(1)} %copy-done.9, bf16[512,1024]{1,0:T(8,128)(2,1)S(1)} %bitcast.29, bf16[512,1024]{1,0:T(8,128)(2,1)S(1)} %bitcast.33, bf16[512,1024]{1,0:T(8,128)(2,1)} %bitcast.45, ...), custom_call_target="tpu_custom_call" | custom-call | flops 1610612736 | bytes 8388608 | tf_op jit(solution)/shard_map/attend/pallas_call | solution.py:109
  31.1 5.7 %parts.2 = (bf16[256,2048]{1,0:T(8,128)(2,1)S(1)}, bf16[256,2048]{1,0:T(8,128)(2,1)S(1)}, f32[1,1]{1,0:T(1,128)}) custom-call(s32[1]{0:T(128)} %bitcast.index_ref, bf16[512,1024]{1,0:T(8,128)(2,1)S(1)} %get-tuple-element.40.refs_0_.refs_5_, bf16[1024,8192]{1,0:T(8,128)(2,1)} %bitcast.34), custom_call_target="tpu_custom_call" | custom-call | flops 2147483648 | bytes 4194304 | tf_op jit(solution)/shard_map/parts/pallas_call | solution.py:109
  36.8 2.3 add_convert_fusion.9.refs_1_.refs_7_
  39.1 16.5 %collective-permute-start.3 = (bf16[256,2048]{1,0:T(8,128)(2,1)S(1)}, bf16[256,2048]{1,0:T(8,128)(2,1)}, u32[]{:S(2)}, u32[]{:S(2)}) collective-permute-start(bf16[256,2048]{1,0:T(8,128)(2,1)S(1)} %add_convert_fusion.9.refs_1_.refs_7_), channel_id=1, source_target_pairs={{0,1},{1,0},{2,3},{3,2},{4,5},{5,4},{6,7},{7,6},{8,9},{9,8},{10,11... | collective-permute-start | bytes 3145736 | tf_op jit(solution)/shard_map/ppermute | solution.py:376
  55.6 2.1 add_convert_fusion.8.refs_0_.refs_5_
  58.2 1.6 collective-permute-start.5
  59.9 3.2 %add_convert_fusion.7.refs_8_ = bf16[256,2048]{1,0:T(8,128)(2,1)} fusion(bf16[256,2048]{1,0:T(8,128)(2,1)S(1)} %get-tuple-element.43, bf16[512,2048]{1,0:T(8,128)(2,1)} %collective-permute-done.2.refs_3_, f32[]{:T(128)} %bitcast.11, pred[]{:T(512)S(6)} %or.3), kind=kLoop, calls=%fused_computation.8 | loop fusion | flops 2097152 | bytes 3145733 | tf_op jit(solution)/shard_map/convert_element_type | solution.py:404
  63.1 1.9 collective-permute-start.6
  65.0 2.1 add_convert_fusion.6.refs_6_
  67.2 1.7 collective-permute-start.7
  68.8 12.2 %parts.3 = (bf16[256,2048]{1,0:T(8,128)(2,1)S(1)}, bf16[256,2048]{1,0:T(8,128)(2,1)S(1)}, bf16[256,2048]{1,0:T(8,128)(2,1)S(1)}, bf16[256,2048]{1,0:T(8,128)(2,1...) custom-call(s32[3]{0:T(128)S(1)} %pad_add_fusion.2.index_ref, bf16[512,1024]{1,0:T(8,128)(2,1)} %copy-done, ...), custom_call_target="tpu_custom_call" | custom-call | flops 6442450944 | bytes 12582912 | tf_op jit(solution)/shard_map/parts/pallas_call | solution.py:109
  81.0 9.6 %project.2 = (f32[512,1024]{1,0:T(8,128)S(1)}, f32[1,1]{1,0:T(1,128)}) custom-call(s32[2]{0:T(128)S(1)} %pad_add_fusion.1.index_ref, bf16[1024,8192]{1,0:T(8,128)(2,1)} %bitcast.38, bf16[1024,8192]{1,0:T(8,128)(2,1)} %bitcast.39, bf16[512,2048]{1,0:T(8,128)(2,1)} %bitcast.52, bf16[512,2048]{1,0:T(8,128)(2,1)} %collective-permute-done.4.refs_3_, ...), custom_call_target="tpu_custom_call" | custom-call | flops 4294967296 | bytes 8388608 | tf_op jit(solution)/shard_map/project/pallas_call | solution.py:109
  90.6 2.6 %add_convert_fusion.4 = (bf16[256,2048]{1,0:T(8,128)(2,1)S(1)}, bf16[256,2048]{1,0:T(8,128)(2,1)S(1)}) fusion(bf16[256,2048]{1,0:T(8,128)(2,1)S(1)} %get-tuple-element.44.refs_4_, bf16[256,2048]{1,0:T(8,128)(2,1)} %collective-permute-done.5, f32[]{:T(128)} %bitcast.14, pred[]{:T(512)S(6)} %or.3, bf16[256,2048]{1,0:T(8,128)(2,1)} %collective-permute-done.3), kind=kLoop, calls=%fused_computation.5 | loop fusion | flops 4718592 | bytes 5242885 | tf_op jit(solution)/shard_map/convert_element_type | solution.py:415
  93.2 2.4 %collective-permute-start.9 = (bf16[256,2048]{1,0:T(8,128)(2,1)S(1)}, bf16[256,2048]{1,0:T(8,128)(2,1)S(1)}, u32[]{:S(2)}, u32[]{:S(2)}) collective-permute-start(bf16[256,2048]{1,0:T(8,128)(2,1)S(1)} %get-tuple-element.81.refs_1_), channel_id=1, source_target_pairs={{0,1},{1,0},{2,3},{3,2},{4,5},{5,4},{6,7},{7,6},{8,9},{9,8},{10,11... | collective-permute-start | bytes 3145736 | tf_op jit(solution)/shard_map/ppermute | solution.py:376
  97.8 3.4 %collective-permute-done.6 = bf16[256,2048]{1,0:T(8,128)(2,1)} collective-permute-done((bf16[256,2048]{1,0:T(8,128)(2,1)}, bf16[256,2048]{1,0:T(8,128)(2,1)}, u32[]{:S(2)}, u32[]{:S(2)}) %collective-permute-start.6) | collective-permute-done | bytes 1048608 | tf_op jit(solution)/shard_map/ppermute | solution.py:376
  101.2 3.4 %add_convert_fusion.2 = (bf16[256,2048]{1,0:T(8,128)(2,1)}, bf16[256,2048]{1,0:T(8,128)(2,1)S(1)}) fusion(bf16[256,2048]{1,0:T(8,128)(2,1)S(1)} %get-tuple-element.46, bf16[256,2048]{1,0:T(8,128)(2,1)} %collective-permute-done.7, f32[]{:T(128)} %bitcast.15, pred[]{:T(512)S(6)} %or.3, bf16[256,2048]{1,0:T(8,128)(2,1)} %collective-permute-done.6), kind=kLoop, calls=%fused_computation.3 | loop fusion | flops 4718592 | bytes 5242885 | tf_op jit(solution)/shard_map/convert_element_type | solution.py:415
  104.6 6.0 %collective-permute-start.8 = (bf16[256,2048]{1,0:T(8,128)(2,1)}, bf16[256,2048]{1,0:T(8,128)(2,1)S(1)}, u32[]{:S(2)}, u32[]{:S(2)}) collective-permute-start(bf16[256,2048]{1,0:T(8,128)(2,1)} %get-tuple-element.79.refs_5_), channel_id=1, source_target_pairs={{0,1},{1,0},{2,3},{3,2},{4,5},{5,4},{6,7},{7,6},{8,9},{9,8},{10,11... | collective-permute-start | bytes 3145736 | tf_op jit(solution)/shard_map/ppermute | solution.py:376
  115.0 6.2 %project.3 = (f32[512,1024]{1,0:T(8,128)}, f32[1,1]{1,0:T(1,128)}) custom-call(s32[1]{0:T(128)} %bitcast.3.index_ref, bf16[1024,8192]{1,0:T(8,128)(2,1)} %bitcast.40, bf16[256,2048]{1,0:T(8,128)(2,1)S(1)} %broadcast_select_fusion.1.refs_1_, bf16[256,2048]{1,0:T(8,128)(2,1)S(1)} %broadcast_select_fusion.refs_2_, f32[512,1024]{1,0:T(8,128)} %copy-done.6, ...), custom_call_target="tpu_custom_call" | custom-call | flops 2147483648 | bytes 4194304 | tf_op jit(solution)/shard_map/project/pallas_call | solution.py:109
  125.5 2.3 add_convert_fusion.1.refs_11_
  127.8 5.5 %collective-permute-start.12 = (bf16[256,2048]{1,0:T(8,128)(2,1)S(1)}, bf16[256,2048]{1,0:T(8,128)(2,1)S(1)}, u32[]{:S(2)}, u32[]{:S(2)}) collective-permute-start(bf16[256,2048]{1,0:T(8,128)(2,1)S(1)} %add_convert_fusion.1.refs_11_), channel_id=1, source_target_pairs={{0,1},{1,0},{2,3},{3,2},{4,5},{5,4},{6,7},{7,6},{8,9},{9,8},{10,11... | collective-permute-start | bytes 3145736 | tf_op jit(solution)/shard_map/ppermute | solution.py:376
  133.3 12.3 %backward.2 = (bf16[512,1024]{1,0:T(8,128)(2,1)}, bf16[2,256,1024]{2,1,0:T(8,128)(2,1)S(1)}, f32[256,1024]{1,0:T(8,128)S(1)}, f32[256,1024]{1,0:T(8,128)S(1)}, f...) custom-call(s32[2]{0:T(128)S(1)} %pad_add_fusion.index_ref, bf16[1024,8192]{1,0:T(8,128)(2,1)} %bitcast.41, ...), custom_call_target="tpu_custom_call" | custom-call | flops 3221225472 | bytes 16777216 | tf_op jit(solution)/shard_map/backward/pallas_call | solution.py:109
  149.0 2.3 add_convert_fusion.11
  151.4 4.3 %collective-permute-start.19 = (bf16[128,2048]{1,0:T(8,128)(2,1)S(1)}, bf16[128,2048]{1,0:T(8,128)(2,1)S(1)}, u32[]{:S(2)}, u32[]{:S(2)}) collective-permute-start(bf16[128,2048]{1,0:T(8,128)(2,1)S(1)} %get-tuple-element.78.refs_0_), channel_id=1, source_target_pairs={{0,1},{1,0},{2,3},{3,2},{4,5},{5,4},{6,7},{7,6},{8,9},{9,8},{10,11... | collective-permute-start | bytes 1572872 | tf_op jit(solution)/shard_map/ppermute | solution.py:376
  156.9 11.6 %collective-permute-done.12 = bf16[256,2048]{1,0:T(8,128)(2,1)S(1)} collective-permute-done((bf16[256,2048]{1,0:T(8,128)(2,1)S(1)}, bf16[256,2048]{1,0:T(8,128)(2,1)S(1)}, u32[]{:S(2)}, u32[]{:S(2)}) %collective-permute-start.12) | collective-permute-done | bytes 1048608 | tf_op jit(solution)/shard_map/ppermute | solution.py:376
  168.5 10.3 %collective-permute-start.17 = (bf16[128,2048]{1,0:T(8,128)(2,1)S(1)}, bf16[128,2048]{1,0:T(8,128)(2,1)S(1)}, u32[]{:S(2)}, u32[]{:S(2)}) collective-permute-start(bf16[128,2048]{1,0:T(8,128)(2,1)S(1)} %get-tuple-element.77.refs_2_), channel_id=1, source_target_pairs={{0,1},{1,0},{2,3},{3,2},{4,5},{5,4},{6,7},{7,6},{8,9},{9,8},{10,11... | collective-permute-start | bytes 1572872 | tf_op jit(solution)/shard_map/ppermute | solution.py:376
  181.6 12.8 %backward.3 = (bf16[512,1024]{1,0:T(8,128)(2,1)}, bf16[2,256,1024]{2,1,0:T(8,128)(2,1)S(1)}, bf16[512,1024]{1,0:T(8,128)(2,1)}, bf16[512,1024]{1,0:T(8,128)(2,1)...) custom-call(s32[2]{0:T(128)S(1)} %pad_add_fusion.index_ref, ...), custom_call_target="tpu_custom_call", output_to_operand_aliasing={{0}: (12, {})} | custom-call | flops 3221225472 | bytes 16777216 | tf_op jit(solution)/shard_map/backward/pallas_call | solution.py:109
  201.5 4.4 %collective-permute-done.23.refs_0_ = bf16[256,2048]{1,0:T(8,128)(2,1)S(1)} collective-permute-done((bf16[256,2048]{1,0:T(8,128)(2,1)S(1)}, bf16[256,2048]{1,0:T(8,128)(2,1)S(1)}, u32[]{:S(2)}, u32[]{:S(2)}) %collective-permute-start.23) | collective-permute-done | bytes 1048608 | tf_op jit(solution)/shard_map/ppermute | solution.py:372
  208.1 9.0 %collective-permute-done.22.refs_0_ = bf16[128,2048]{1,0:T(8,128)(2,1)S(1)} collective-permute-done((bf16[128,2048]{1,0:T(8,128)(2,1)S(1)}, bf16[128,2048]{1,0:T(8,128)(2,1)S(1)}, u32[]{:S(2)}, u32[]{:S(2)}) %collective-permute-start.22) | collective-permute-done | bytes 524320 | tf_op jit(solution)/shard_map/ppermute | solution.py:372
  217.9 10.4 %collective-permute-done.21.refs_0_ = bf16[128,2048]{1,0:T(8,128)(2,1)S(1)} collective-permute-done((bf16[128,2048]{1,0:T(8,128)(2,1)S(1)}, bf16[128,2048]{1,0:T(8,128)(2,1)S(1)}, u32[]{:S(2)}, u32[]{:S(2)}) %collective-permute-start.21) | collective-permute-done | bytes 524320 | tf_op jit(solution)/shard_map/ppermute | solution.py:372
  (90 shorter events, 36.8 us)
Async XLA Ops:
  0.6 36.2 %collective-permute-start.2 = (bf16[512,2048]{1,0:T(8,128)(2,1)}, bf16[512,2048]{1,0:T(8,128)(2,1)}, u32[]{:S(2)}, u32[]{:S(2)}) collective-permute-start(bf16[512,2048]{1,0:T(8,128)(2,1)} %bitcast.49), channel_id=1, source_target_pairs={{1,2},{2,1},{5,6},{6,5},{9,10},{10,9},{13,14},{14,13},{17,18},{18,... | collective-permute-start | bytes 6291464 | tf_op jit(solution)/shard_map/ppermute | solution.py:376
  2.6 52.9 %collective-permute-start.4 = (bf16[512,2048]{1,0:T(8,128)(2,1)}, bf16[512,2048]{1,0:T(8,128)(2,1)}, u32[]{:S(2)}, u32[]{:S(2)}) collective-permute-start(bf16[512,2048]{1,0:T(8,128)(2,1)} %bitcast.50), channel_id=1, source_target_pairs={{0,1},{1,0},{2,3},{3,2},{4,5},{5,4},{6,7},{7,6},{8,9},{9,8},{10,11... | collective-permute-start | bytes 6291464 | tf_op jit(solution)/shard_map/ppermute | solution.py:376
  7.2 8.1 %collective-permute-start = (bf16[512,1024]{1,0:T(8,128)(2,1)}, bf16[512,1024]{1,0:T(8,128)(2,1)S(1)}, u32[]{:S(2)}, u32[]{:S(2)}) collective-permute-start(bf16[512,1024]{1,0:T(8,128)(2,1)} %bitcast.30), channel_id=1, source_target_pairs={{0,4},{4,8},{8,12},{1,5},{5,9},{9,13},{2,6},{6,10},{10,14},{3,7},{... | collective-permute-start | bytes 3145736 | tf_op jit(solution)/shard_map/ppermute | solution.py:367
  8.6 6.8 %collective-permute-start.1 = (bf16[512,1024]{1,0:T(8,128)(2,1)}, bf16[512,1024]{1,0:T(8,128)(2,1)}, u32[]{:S(2)}, u32[]{:S(2)}) collective-permute-start(bf16[512,1024]{1,0:T(8,128)(2,1)} %bitcast.44), channel_id=1, source_target_pairs={{0,4},{4,8},{8,12},{1,5},{5,9},{9,13},{2,6},{6,10},{10,14},{3,7},{... | collective-permute-start | bytes 3145736 | tf_op jit(solution)/shard_map/ppermute | solution.py:367
  13.6 107.6 %collective-permute-start.11 = (bf16[512,2048]{1,0:T(8,128)(2,1)}, bf16[512,2048]{1,0:T(8,128)(2,1)S(1)}, u32[]{:S(2)}, u32[]{:S(2)}) collective-permute-start(bf16[512,2048]{1,0:T(8,128)(2,1)} %bitcast.51), channel_id=1, source_target_pairs={{16,0},{0,16},{17,1},{1,17},{18,2},{2,18},{19,3},{3,19},{20,4},{4,... | collective-permute-start | bytes 6291464 | tf_op jit(solution)/shard_map/ppermute | solution.py:372
  31.1 5.7 %copy-start = (bf16[512,1024]{1,0:T(8,128)(2,1)}, bf16[512,1024]{1,0:T(8,128)(2,1)S(1)}, u32[]{:S(2)}) copy-start(bf16[512,1024]{1,0:T(8,128)(2,1)S(1)} %get-tuple-element.40.refs_0_.refs_5_) | copy-start | bytes 3145732
  39.1 19.1 %copy-start.1 = (bf16[256,2048]{1,0:T(8,128)(2,1)}, bf16[256,2048]{1,0:T(8,128)(2,1)S(1)}, u32[]{:S(2)}) copy-start(bf16[256,2048]{1,0:T(8,128)(2,1)S(1)} %add_convert_fusion.9.refs_1_.refs_7_) | copy-start | bytes 3145732
  39.1 51.5 %collective-permute-start.3 = (bf16[256,2048]{1,0:T(8,128)(2,1)S(1)}, bf16[256,2048]{1,0:T(8,128)(2,1)}, u32[]{:S(2)}, u32[]{:S(2)}) collective-permute-start(bf16[256,2048]{1,0:T(8,128)(2,1)S(1)} %add_convert_fusion.9.refs_1_.refs_7_), channel_id=1, source_target_pairs={{0,1},{1,0},{2,3},{3,2},{4,5},{5,4},{6,7},{7,6},{8,9},{9,8},{10,11... | collective-permute-start | bytes 3145736 | tf_op jit(solution)/shard_map/ppermute | solution.py:376
  58.2 32.4 %collective-permute-start.5 = (bf16[256,2048]{1,0:T(8,128)(2,1)S(1)}, bf16[256,2048]{1,0:T(8,128)(2,1)}, u32[]{:S(2)}, u32[]{:S(2)}) collective-permute-start(bf16[256,2048]{1,0:T(8,128)(2,1)S(1)} %add_convert_fusion.8.refs_0_.refs_5_), channel_id=1, source_target_pairs={{1,2},{2,1},{5,6},{6,5},{9,10},{10,9},{13,14},{14,13},{17,18},{18,... | collective-permute-start | bytes 3145736 | tf_op jit(solution)/shard_map/ppermute | solution.py:376
  63.1 38.1 %collective-permute-start.6 = (bf16[256,2048]{1,0:T(8,128)(2,1)}, bf16[256,2048]{1,0:T(8,128)(2,1)}, u32[]{:S(2)}, u32[]{:S(2)}) collective-permute-start(bf16[256,2048]{1,0:T(8,128)(2,1)} %add_convert_fusion.7.refs_8_), channel_id=1, source_target_pairs={{0,1},{1,0},{2,3},{3,2},{4,5},{5,4},{6,7},{7,6},{8,9},{9,8},{10,11... | collective-permute-start | bytes 3145736 | tf_op jit(solution)/shard_map/ppermute | solution.py:376
  67.2 34.0 %collective-permute-start.7 = (bf16[256,2048]{1,0:T(8,128)(2,1)S(1)}, bf16[256,2048]{1,0:T(8,128)(2,1)}, u32[]{:S(2)}, u32[]{:S(2)}) collective-permute-start(bf16[256,2048]{1,0:T(8,128)(2,1)S(1)} %add_convert_fusion.6.refs_6_), channel_id=1, source_target_pairs={{1,2},{2,1},{5,6},{6,5},{9,10},{10,9},{13,14},{14,13},{17,18},{18,... | collective-permute-start | bytes 3145736 | tf_op jit(solution)/shard_map/ppermute | solution.py:376
  93.2 30.3 %collective-permute-start.9 = (bf16[256,2048]{1,0:T(8,128)(2,1)S(1)}, bf16[256,2048]{1,0:T(8,128)(2,1)S(1)}, u32[]{:S(2)}, u32[]{:S(2)}) collective-permute-start(bf16[256,2048]{1,0:T(8,128)(2,1)S(1)} %get-tuple-element.81.refs_1_), channel_id=1, source_target_pairs={{0,1},{1,0},{2,3},{3,2},{4,5},{5,4},{6,7},{7,6},{8,9},{9,8},{10,11... | collective-permute-start | bytes 3145736 | tf_op jit(solution)/shard_map/ppermute | solution.py:376
  96.1 29.4 %collective-permute-start.10 = (bf16[256,2048]{1,0:T(8,128)(2,1)S(1)}, bf16[256,2048]{1,0:T(8,128)(2,1)}, u32[]{:S(2)}, u32[]{:S(2)}) collective-permute-start(bf16[256,2048]{1,0:T(8,128)(2,1)S(1)} %get-tuple-element.82.refs_0_), channel_id=1, source_target_pairs={{1,2},{2,1},{5,6},{6,5},{9,10},{10,9},{13,14},{14,13},{17,18},{18,... | collective-permute-start | bytes 3145736 | tf_op jit(solution)/shard_map/ppermute | solution.py:376
  104.6 42.6 %collective-permute-start.8 = (bf16[256,2048]{1,0:T(8,128)(2,1)}, bf16[256,2048]{1,0:T(8,128)(2,1)S(1)}, u32[]{:S(2)}, u32[]{:S(2)}) collective-permute-start(bf16[256,2048]{1,0:T(8,128)(2,1)} %get-tuple-element.79.refs_5_), channel_id=1, source_target_pairs={{0,1},{1,0},{2,3},{3,2},{4,5},{5,4},{6,7},{7,6},{8,9},{9,8},{10,11... | collective-permute-start | bytes 3145736 | tf_op jit(solution)/shard_map/ppermute | solution.py:376
  110.7 38.3 %collective-permute-start.14 = (bf16[256,2048]{1,0:T(8,128)(2,1)S(1)}, bf16[256,2048]{1,0:T(8,128)(2,1)}, u32[]{:S(2)}, u32[]{:S(2)}) collective-permute-start(bf16[256,2048]{1,0:T(8,128)(2,1)S(1)} %get-tuple-element.80.refs_4_), channel_id=1, source_target_pairs={{1,2},{2,1},{5,6},{6,5},{9,10},{10,9},{13,14},{14,13},{17,18},{18,... | collective-permute-start | bytes 3145736 | tf_op jit(solution)/shard_map/ppermute | solution.py:376
  124.6 8.7 %copy-start.12 = (bf16[256,2048]{1,0:T(8,128)(2,1)}, bf16[256,2048]{1,0:T(8,128)(2,1)S(1)}, u32[]{:S(2)}) copy-start(bf16[256,2048]{1,0:T(8,128)(2,1)S(1)} %add_convert_fusion.refs_12_) | copy-start | bytes 3145732
  124.6 31.6 %collective-permute-start.13 = (bf16[256,2048]{1,0:T(8,128)(2,1)S(1)}, bf16[256,2048]{1,0:T(8,128)(2,1)S(1)}, u32[]{:S(2)}, u32[]{:S(2)}) collective-permute-start(bf16[256,2048]{1,0:T(8,128)(2,1)S(1)} %add_convert_fusion.refs_12_), channel_id=1, source_target_pairs={{1,2},{2,1},{5,6},{6,5},{9,10},{10,9},{13,14},{14,13},{17,18},{18,... | collective-permute-start | bytes 3145736 | tf_op jit(solution)/shard_map/ppermute | solution.py:376
  127.8 5.5 %copy-start.13 = (bf16[256,2048]{1,0:T(8,128)(2,1)}, bf16[256,2048]{1,0:T(8,128)(2,1)S(1)}, u32[]{:S(2)}) copy-start(bf16[256,2048]{1,0:T(8,128)(2,1)S(1)} %add_convert_fusion.1.refs_11_) | copy-start | bytes 3145732
  127.8 40.7 %collective-permute-start.12 = (bf16[256,2048]{1,0:T(8,128)(2,1)S(1)}, bf16[256,2048]{1,0:T(8,128)(2,1)S(1)}, u32[]{:S(2)}, u32[]{:S(2)}) collective-permute-start(bf16[256,2048]{1,0:T(8,128)(2,1)S(1)} %add_convert_fusion.1.refs_11_), channel_id=1, source_target_pairs={{0,1},{1,0},{2,3},{3,2},{4,5},{5,4},{6,7},{7,6},{8,9},{9,8},{10,11... | collective-permute-start | bytes 3145736 | tf_op jit(solution)/shard_map/ppermute | solution.py:376
  145.7 5.7 %copy-start.7 = (f32[256,1024]{1,0:T(8,128)}, f32[256,1024]{1,0:T(8,128)S(1)}, u32[]{:S(2)}) copy-start(f32[256,1024]{1,0:T(8,128)S(1)} %get-tuple-element.56.refs_13_) | copy-start | bytes 3145732
  145.7 5.7 %copy-start.8 = (f32[256,1024]{1,0:T(8,128)}, f32[256,1024]{1,0:T(8,128)S(1)}, u32[]{:S(2)}) copy-start(f32[256,1024]{1,0:T(8,128)S(1)} %get-tuple-element.57.refs_14_) | copy-start | bytes 3145732
  145.7 34.3 %collective-permute-start.15 = (bf16[2,256,1024]{2,1,0:T(8,128)(2,1)S(1)}, bf16[2,256,1024]{2,1,0:T(8,128)(2,1)}, u32[]{:S(2)}, u32[]{:S(2)}) collective-permute-start(bf16[2,256,1024]{2,1,0:T(8,128)(2,1)S(1)} %get-tuple-element.60), channel_id=1, source_target_pairs={{4,0},{8,4},{12,8},{5,1},{9,5},{13,9},{6,2},{10,6},{14,10},{7,3},{... | collective-permute-start | bytes 3145736 | tf_op jit(solution)/shard_map/ppermute | solution.py:367
  148.3 46.1 %collective-permute-start.20 = (bf16[128,2048]{1,0:T(8,128)(2,1)S(1)}, bf16[128,2048]{1,0:T(8,128)(2,1)S(1)}, u32[]{:S(2)}, u32[]{:S(2)}) collective-permute-start(bf16[128,2048]{1,0:T(8,128)(2,1)S(1)} %get-tuple-element.76.refs_1_), channel_id=1, source_target_pairs={{1,2},{2,1},{5,6},{6,5},{9,10},{10,9},{13,14},{14,13},{17,18},{18,... | collective-permute-start | bytes 1572872 | tf_op jit(solution)/shard_map/ppermute | solution.py:376
  149.0 29.8 %copy-start.18 = (bf16[256,2048]{1,0:T(8,128)(2,1)S(1)}, bf16[256,2048]{1,0:T(8,128)(2,1)}, u32[]{:S(2)}) copy-start(bf16[256,2048]{1,0:T(8,128)(2,1)} %get-tuple-element.53) | copy-start | bytes 3145732
  151.4 44.4 %collective-permute-start.19 = (bf16[128,2048]{1,0:T(8,128)(2,1)S(1)}, bf16[128,2048]{1,0:T(8,128)(2,1)S(1)}, u32[]{:S(2)}, u32[]{:S(2)}) collective-permute-start(bf16[128,2048]{1,0:T(8,128)(2,1)S(1)} %get-tuple-element.78.refs_0_), channel_id=1, source_target_pairs={{0,1},{1,0},{2,3},{3,2},{4,5},{5,4},{6,7},{7,6},{8,9},{9,8},{10,11... | collective-permute-start | bytes 1572872 | tf_op jit(solution)/shard_map/ppermute | solution.py:376
  156.2 41.9 %collective-permute-start.18 = (bf16[128,2048]{1,0:T(8,128)(2,1)S(1)}, bf16[128,2048]{1,0:T(8,128)(2,1)S(1)}, u32[]{:S(2)}, u32[]{:S(2)}) collective-permute-start(bf16[128,2048]{1,0:T(8,128)(2,1)S(1)} %get-tuple-element.75.refs_3_), channel_id=1, source_target_pairs={{1,2},{2,1},{5,6},{6,5},{9,10},{10,9},{13,14},{14,13},{17,18},{18,... | collective-permute-start | bytes 1572872 | tf_op jit(solution)/shard_map/ppermute | solution.py:376
  168.5 29.6 %collective-permute-start.17 = (bf16[128,2048]{1,0:T(8,128)(2,1)S(1)}, bf16[128,2048]{1,0:T(8,128)(2,1)S(1)}, u32[]{:S(2)}, u32[]{:S(2)}) collective-permute-start(bf16[128,2048]{1,0:T(8,128)(2,1)S(1)} %get-tuple-element.77.refs_2_), channel_id=1, source_target_pairs={{0,1},{1,0},{2,3},{3,2},{4,5},{5,4},{6,7},{7,6},{8,9},{9,8},{10,11... | collective-permute-start | bytes 1572872 | tf_op jit(solution)/shard_map/ppermute | solution.py:376
  180.0 25.8 %collective-permute-start.23 = (bf16[256,2048]{1,0:T(8,128)(2,1)S(1)}, bf16[256,2048]{1,0:T(8,128)(2,1)S(1)}, u32[]{:S(2)}, u32[]{:S(2)}) collective-permute-start(bf16[256,2048]{1,0:T(8,128)(2,1)S(1)} %subtract_convert_fusion.refs_12_), channel_id=1, source_target_pairs={{16,0},{0,16},{17,1},{1,17},{18,2},{2,18},{19,3},{3,19},{20,4},{4,... | collective-permute-start | bytes 3145736 | tf_op jit(solution)/shard_map/ppermute | solution.py:372
  181.6 14.1 %copy-start.17 = (bf16[256,2048]{1,0:T(8,128)(2,1)S(1)}, bf16[256,2048]{1,0:T(8,128)(2,1)}, u32[]{:S(2)}) copy-start(bf16[256,2048]{1,0:T(8,128)(2,1)} %get-tuple-element.67) | copy-start | bytes 3145732
  194.4 5.8 %collective-permute-start.16 = (bf16[2,256,1024]{2,1,0:T(8,128)(2,1)S(1)}, bf16[2,256,1024]{2,1,0:T(8,128)(2,1)S(1)}, u32[]{:S(2)}, u32[]{:S(2)}) collective-permute-start(bf16[2,256,1024]{2,1,0:T(8,128)(2,1)S(1)} %get-tuple-element.64), channel_id=1, source_target_pairs={{4,0},{8,4},{12,8},{5,1},{9,5},{13,9},{6,2},{10,6},{14,10},{7,3},{... | collective-permute-start | bytes 3145736 | tf_op jit(solution)/shard_map/ppermute | solution.py:367
  197.1 19.9 %collective-permute-start.22 = (bf16[128,2048]{1,0:T(8,128)(2,1)S(1)}, bf16[128,2048]{1,0:T(8,128)(2,1)S(1)}, u32[]{:S(2)}, u32[]{:S(2)}) collective-permute-start(bf16[128,2048]{1,0:T(8,128)(2,1)S(1)} %subtract_convert_fusion.2.refs_0_), channel_id=1, source_target_pairs={{16,0},{0,16},{17,1},{1,17},{18,2},{2,18},{19,3},{3,19},{20,4},{4,... | collective-permute-start | bytes 1572872 | tf_op jit(solution)/shard_map/ppermute | solution.py:372
  199.0 29.3 %collective-permute-start.21 = (bf16[128,2048]{1,0:T(8,128)(2,1)S(1)}, bf16[128,2048]{1,0:T(8,128)(2,1)S(1)}, u32[]{:S(2)}, u32[]{:S(2)}) collective-permute-start(bf16[128,2048]{1,0:T(8,128)(2,1)S(1)} %subtract_convert_fusion.1.refs_5_), channel_id=1, source_target_pairs={{16,0},{0,16},{17,1},{1,17},{18,2},{2,18},{19,3},{3,19},{20,4},{4,... | collective-permute-start | bytes 1572872 | tf_op jit(solution)/shard_map/ppermute | solution.py:372
  (12 other events, 28.4 us)

commit v3 on v2

v3 whole, which is shorter than its diff:
```python
import functools

import jax
import jax.numpy as jnp
from jax import lax
from jax.experimental import pallas as pl
from jax.experimental.pallas import tpu as pltpu
from jax.sharding import PartitionSpec as P

HD = 128
WINDOW = 512
NEG = -1e30
HALF = 256
PIECES = [(0, 256), (256, 128), (384, 128)]
PAIR = 4
VMEM_LIMIT = 50 * 1024 * 1024
COST = 1.0

OUTER = [(0, 1), (1, 0), (2, 3), (3, 2)]
MIDDLE = [(1, 2), (2, 1)]
OUTER_INWARD = [(0, 1), (3, 2)]
OUTER_OUTWARD = [(1, 0), (2, 3)]


def params():
    return pltpu.CompilerParams(vmem_limit_bytes=VMEM_LIMIT)


def dot(a, b, contract):
    return lax.dot_general(a, b, ((contract[0], contract[1]), ((), ())), preferred_element_type=jnp.float32)


def nt(a, b):
    return dot(a, b, ((1,), (1,)))


def nn(a, b):
    return dot(a, b, ((1,), (0,)))


def tn(a, b):
    return dot(a, b, ((0,), (0,)))


def lower(size):
    row = lax.broadcasted_iota(jnp.int32, (size, size), 0)
    col = lax.broadcasted_iota(jnp.int32, (size, size), 1)
    return col <= row


def forward_kernel(steps, index_ref, doc_ref, q_ref, k_ref, v_ref, kp_ref, vp_ref, far_ref, att_ref, w_ref, far0_ref, far1_ref, bias_ref, all_ref):
    rows = q_ref.shape[0]
    step = pl.program_id(0)
    scaling = HD ** (-0.5)

    @pl.when(step == 0)
    def _():
        index = index_ref[1]
        own = doc_ref[:, pl.ds(pl.multiple_of(index * rows, rows), rows)]
        before = doc_ref[:, pl.ds(pl.multiple_of(jnp.maximum(index - 1, 0) * rows, rows), rows)]
        before = jnp.where(index > 0, before, -1)
        own = jnp.broadcast_to(own, (rows, rows))
        before = jnp.broadcast_to(before, (rows, rows))
        key_doc = jnp.where(lower(rows), own, before)
        bias_ref[...] = jnp.where(key_doc == own.T, 0.0, NEG)

    @pl.when(step < steps)
    def _():
        tri = lower(HALF)
        for head in range(q_ref.shape[1] // HD):
            cols = pl.ds(head * HD, HD)
            for qb in range(2):
                qs = pl.ds(qb * HALF, HALF)
                ks = pl.ds((1 - qb) * HALF, HALF)
                q = q_ref[qs, cols]
                diagonal = jnp.where(tri, nt(q, k_ref[qs, cols]), nt(q, kp_ref[qs, cols]))
                if qb == 0:
                    scores = jnp.concatenate([diagonal, nt(q, kp_ref[ks, cols])], 1)
                else:
                    scores = jnp.concatenate([nt(q, k_ref[ks, cols]), diagonal], 1)
                scores = scores * scaling + bias_ref[qs, :]
                row_max = jnp.max(scores, axis=1, keepdims=True)
                exponent = jnp.exp(scores - row_max)
                row_sum = jnp.sum(exponent, axis=1, keepdims=True)
                prob = exponent * (1.0 / row_sum)
                w_ref[head, qs, :] = prob.astype(jnp.bfloat16)
                mine = prob[:, qb * HALF : (qb + 1) * HALF]
                rest = prob[:, (1 - qb) * HALF : (2 - qb) * HALF].astype(jnp.bfloat16)
                mine_own = jnp.where(tri, mine, 0.0).astype(jnp.bfloat16)
                mine_before = jnp.where(tri, 0.0, mine).astype(jnp.bfloat16)
                att = nn(mine_own, v_ref[qs, cols]) + nn(mine_before, vp_ref[qs, cols])
                att = att + nn(rest, (vp_ref if qb == 0 else v_ref)[ks, cols])
                att_ref[qs, cols] = att.astype(jnp.bfloat16)

    for j in range(steps):

        @pl.when(step == j)
        def _():
            all_ref[j] = att_ref[...]

    @pl.when(step >= steps)
    def _():
        wide = PAIR * HD
        out = nn(all_ref[0], far_ref[:wide, :])
        for j in range(1, steps):
            out += nn(all_ref[j], far_ref[j * wide : (j + 1) * wide, :])
        out = out.astype(jnp.bfloat16)
        far0_ref[...] = out[:HALF]
        far1_ref[...] = out[HALF:]


def cost(flops, moved, transcendentals=0):
    return pl.CostEstimate(flops=int(flops * COST), bytes_accessed=int(moved * COST), transcendentals=int(transcendentals * COST))


ANY = pl.BlockSpec(memory_space=pl.ANY)


def corner(x):
    block = (1,) * (x.ndim - 2) + (16, HD)
    return pl.BlockSpec(block, lambda *_: (0,) * x.ndim)


def call(kernel, index, grid, blocked, after, out_specs, out_shape, moved, flops, name, scratch=(), aliases=None):
    count = len(blocked)
    waits = len(after)
    outs = len(out_shape)

    def run(index_ref, *refs):
        kernel(index_ref, *refs[:count], *refs[count + waits : count + waits + outs], *refs[count + waits + outs + 1 :])
        refs[count + waits + outs][0, 0] = jnp.float32(0.0)

    result = pl.pallas_call(
        run,
        grid_spec=pltpu.PrefetchScalarGridSpec(
            num_scalar_prefetch=1,
            grid=grid,
            in_specs=[spec for _, spec in blocked] + [corner(x) for x in after],
            out_specs=list(out_specs) + [pl.BlockSpec((1, 1), lambda *_: (0, 0), memory_space=pltpu.SMEM)],
            scratch_shapes=list(scratch),
        ),
        out_shape=list(out_shape) + [jax.ShapeDtypeStruct((1, 1), jnp.float32)],
        input_output_aliases=aliases or {},
        compiler_params=params(),
        cost_estimate=cost(flops, moved),
        name=name,
    )(index, *[x for x, _ in blocked], *after)
    return result[:-1], result[-1].reshape(())


def tie(index, after):
    _, zero = call(lambda index_ref: None, index, (1,), [], after, [], [], 8192, 0, "tie")
    return zero


def forward(index, doc, q, k, v, kp, vp, weight):
    rows, feature = q.shape
    pairs = feature // HD // PAIR
    block = 512
    width = weight.shape[1] // 4
    blocks = width // block
    head = pl.BlockSpec((rows, PAIR * HD), lambda n, *_: (0, jnp.minimum(n, pairs - 1)))
    late = lambda n: jnp.maximum(n - pairs, 0)
    far = pl.BlockSpec((HALF, block), lambda n, *_: (0, late(n)))
    out = jax.ShapeDtypeStruct((HALF, width), jnp.bfloat16)
    return call(
        functools.partial(forward_kernel, pairs), index, (pairs + blocks,),
        [(doc, pl.BlockSpec(doc.shape, lambda n, *_: (0, 0)))] + [(x, head) for x in (q, k, v, kp, vp)]
        + [(weight, pl.BlockSpec((feature, block), lambda n, idx: (0, idx[0] * blocks + late(n))))], [],
        [head, pl.BlockSpec((PAIR, rows, rows), lambda n, *_: (jnp.minimum(n, pairs - 1), 0, 0)), far, far],
        [jax.ShapeDtypeStruct((rows, feature), jnp.bfloat16), jax.ShapeDtypeStruct((PAIR * pairs, rows, rows), jnp.bfloat16), out, out],
        2**23, 12 * 2 * 2**23 * PAIR * pairs, "attend",
        scratch=[pltpu.VMEM((rows, rows), jnp.float32), pltpu.VMEM((pairs, rows, PAIR * HD), jnp.bfloat16)],
    )


def project(weight, index, groups, total, after):
    rows = sum(piece[0].shape[0] for piece in groups[0])
    depth = groups[0][0][0].shape[1]
    out_rows = weight.shape[0]
    block = 256
    shape = [[(len(piece), piece[0].shape[0]) for piece in g] for g in groups]
    has_total = total is not None

    def kernel(index_ref, *refs):
        refs = list(refs)
        w = [refs.pop(0)[...] for _ in groups]
        out_ref = refs[-1]
        start = 0
        base = refs[-2] if has_total else None
        sums = {}
        for j, pieces in enumerate(shape):
            start = 0
            for many, height in pieces:
                x = refs.pop(0)[...]
                for _ in range(many - 1):
                    x = x + refs.pop(0)[...]
                term = nt(x, w[j])
                key = (start, height)
                at = pl.ds(start, height)
                if j == 0:
                    out_ref[at, :] = term + base[at, :] if has_total else term
                else:
                    out_ref[at, :] += term
                start += height

    blocked = [(weight, pl.BlockSpec((block, depth), lambda n, idx, j=j: (n, idx[j]))) for j in range(len(groups))]
    for g in groups:
        for piece in g:
            for x in piece:
                blocked.append((x, pl.BlockSpec(x.shape, lambda n, idx: (0, 0))))
    if has_total:
        blocked.append((total, pl.BlockSpec((rows, block), lambda n, idx: (0, n))))
    return call(
        kernel, index, (out_rows // block,), blocked, after,
        [pl.BlockSpec((rows, block), lambda n, idx: (0, n))],
        [jax.ShapeDtypeStruct((rows, out_rows), jnp.float32)],
        2 * out_rows * depth * len(groups), 2 * rows * depth * out_rows * len(groups), "project",
    )


def parts(weight, index, attended, count, after, stream=None):
    rows, depth = attended.shape
    width = weight.shape[1] // 4
    block = 512
    steps = width // block

    def kernel(index_ref, x_ref, *refs):
        base = count + (stream is not None)
        for j in range(count):
            out = nn(x_ref[...], refs[j][...])
            if stream is not None and j == count - 1:
                out = refs[count][...].astype(jnp.float32) - out
            out = out.astype(jnp.bfloat16)
            refs[base + 2 * j][...] = out[:HALF]
            refs[base + 2 * j + 1][...] = out[HALF:]

    blocked = [(attended, pl.BlockSpec((rows, depth), lambda n, idx: (0, 0)))]
    for j in range(count):
        blocked.append((weight, pl.BlockSpec((depth, block), lambda n, idx, j=j: (0, idx[j] * steps + n))))
    if stream is not None:
        blocked.append((stream, pl.BlockSpec((rows, block), lambda n, idx: (0, n))))
    return call(
        kernel, index, (steps,), blocked, after,
        [pl.BlockSpec((HALF, block), lambda n, idx: (0, n))] * (2 * count),
        [jax.ShapeDtypeStruct((HALF, width), jnp.bfloat16)] * (2 * count),
        count * 2 * depth * width, 2 * rows * depth * width * count, "parts",
    )


def place(index, whole, rows, piece, start, after):
    height, width = piece.shape
    blocked = [(piece, pl.BlockSpec((height, width), lambda n, idx: (0, 0)))]
    aliases = None
    if whole is not None:
        blocked.append((whole, ANY))
        aliases = {2: 0}

    def kernel(index_ref, x_ref, *refs):
        refs[-1][...] = x_ref[...]

    (out,), zero = call(
        kernel, index, (1,), blocked, after,
        [pl.BlockSpec((height, width), lambda n, idx: (start // height, 0))],
        [jax.ShapeDtypeStruct((rows, width), piece.dtype)],
        4 * height * width, 0, "place", aliases=aliases,
    )
    return out, zero


def settle(index, which, grads, k, v, back, after):
    height, width = k.shape
    wide = 512

    def kernel(index_ref, k_ref, v_ref, back_ref, *refs):
        gk_ref, gv_ref = refs[-2:]
        gk_ref[...] = (k_ref[...].astype(jnp.float32) + back_ref[0].astype(jnp.float32)).astype(jnp.bfloat16)
        gv_ref[...] = (v_ref[...].astype(jnp.float32) + back_ref[1].astype(jnp.float32)).astype(jnp.bfloat16)

    flat = pl.BlockSpec((height, wide), lambda n, idx: (0, n))
    out_spec = pl.BlockSpec((height, wide), lambda n, idx: (which, n))
    out = jax.ShapeDtypeStruct((2 * height, width), jnp.bfloat16)
    return call(
        kernel, index, (width // wide,),
        [(k, flat), (v, flat), (back, pl.BlockSpec((2, height, wide), lambda n, idx: (0, 0, n)))] + [(x, ANY) for x in grads],
        after, [out_spec, out_spec], [out, out],
        16 * height * width, 0, "settle", aliases={4: 0, 5: 1} if grads else None,
    )


def gate(index, x, after):
    (out,), _ = call(
        lambda *refs: None, index, (1,), [(x, ANY)], after, [ANY], [jax.ShapeDtypeStruct(x.shape, x.dtype)], 8192, 0, "gate", aliases={1: 0}
    )
    return out


def total_of(*terms):
    result = terms[0].astype(jnp.float32)
    for x in terms[1:]:
        result = result + x.astype(jnp.float32)
    return result


def backward(qb, weight, index, total, outer, middle, probs, attended, q, k, v, kp, vp, carried, after, steps, earlier=()):
    rows, feature = q.shape
    heads = feature // HD
    depth = outer.shape[1]
    wide = PAIR * HD
    scaling = HD ** (-0.5)
    bf = jnp.bfloat16
    first = steps[0]
    kept = list(earlier) if earlier else list(carried[:1])
    skip = len(after) + len(kept)

    def kernel(index_ref, w_ref, total_ref, outer_ref, middle_ref, p_ref, att_ref, q_ref, k_ref, v_ref, kp_ref, vp_ref, *refs):
        refs = refs[skip:]
        carry = refs[:4] if qb else ()
        dq_ref, send_ref, k0_ref, v0_ref, k1_ref, v1_ref, x_ref = refs[len(carry) :]

        @pl.when((pl.program_id(0) == 0) & (index_ref[1] == 1))
        def _():
            x_ref[...] = outer_ref[...]

        @pl.when((pl.program_id(0) == 0) & (index_ref[1] == 0))
        def _():
            x_ref[...] = middle_ref[...]

        qs = pl.ds(qb * HALF, HALF)
        ks = pl.ds((1 - qb) * HALF, HALF)
        tri = lower(HALF)
        d_out_pair = (total_ref[...] + nt(x_ref[...], w_ref[...])).astype(bf)
        for head in range(PAIR):
            cols = pl.ds(head * HD, HD)
            d_out = d_out_pair[:, head * HD : (head + 1) * HD]
            row_delta = jnp.sum(
                d_out.astype(jnp.float32) * att_ref[:, cols].astype(jnp.float32), axis=1, keepdims=True
            )
            qh = q_ref[:, cols]
            k_rest_ref, v_rest_ref = (k_ref, v_ref) if qb else (kp_ref, vp_ref)
            k_rest, v_rest = k_rest_ref[ks, cols], v_rest_ref[ks, cols]
            own, prev = (qs, pl.ds(0, HALF)) if qb else (pl.ds(0, HALF), qs)
            p_diag = p_ref[head, :, qb * HALF : (qb + 1) * HALF].astype(jnp.float32)
            p_rest = p_ref[head, :, (1 - qb) * HALF : (2 - qb) * HALF]
            dp_diag = jnp.where(tri, nt(d_out, v_ref[own, cols]), nt(d_out, vp_ref[prev, cols]))
            dp_rest = nt(d_out, v_rest)
            ds_diag = p_diag * (dp_diag - row_delta)
            ds_rest = (p_rest.astype(jnp.float32) * (dp_rest - row_delta)).astype(bf)
            ds_own = jnp.where(tri, ds_diag, 0.0).astype(bf)
            ds_before = jnp.where(tri, 0.0, ds_diag).astype(bf)
            p_own = jnp.where(tri, p_diag, 0.0).astype(bf)
            p_before = jnp.where(tri, 0.0, p_diag).astype(bf)
            dq = nn(ds_own, k_ref[own, cols]) + nn(ds_before, kp_ref[prev, cols]) + nn(ds_rest, k_rest)
            dq_ref[:, cols] = (dq * scaling).astype(bf)
            dk_own, dv_own = tn(ds_own, qh) * scaling, tn(p_own, d_out)
            dk_before, dv_before = tn(ds_before, qh) * scaling, tn(p_before, d_out)
            dk_rest, dv_rest = tn(ds_rest, qh) * scaling, tn(p_rest, d_out)
            if qb == 0:
                send_ref[0, :, cols] = dk_before.astype(bf)
                send_ref[1, :, cols] = dv_before.astype(bf)
                k0_ref[:, cols], v0_ref[:, cols] = dk_own.astype(bf), dv_own.astype(bf)
                k1_ref[:, cols], v1_ref[:, cols] = dk_rest.astype(bf), dv_rest.astype(bf)
            else:
                k0i, v0i, kri, vri = carry
                send_ref[0, :, cols] = (dk_before + kri[:, cols].astype(jnp.float32)).astype(bf)
                send_ref[1, :, cols] = (dv_before + vri[:, cols].astype(jnp.float32)).astype(bf)
                k0_ref[:, cols] = (dk_rest + k0i[:, cols].astype(jnp.float32)).astype(bf)
                v0_ref[:, cols] = (dv_rest + v0i[:, cols].astype(jnp.float32)).astype(bf)
                k1_ref[:, cols], v1_ref[:, cols] = dk_own.astype(bf), dv_own.astype(bf)

    whole = pl.BlockSpec((rows, wide), lambda h, *_: (0, first + h))
    half = pl.BlockSpec((HALF, wide), lambda h, *_: (0, first + h))
    mine = pl.BlockSpec((HALF, wide), lambda h, *_: (qb, first + h))
    blocked = [
        (weight, pl.BlockSpec((wide, depth), lambda h, idx: (first + h, idx[0]))),
        (total, mine),
        (outer, pl.BlockSpec((HALF, depth), lambda h, *_: (0, 0))),
        (middle, pl.BlockSpec((HALF, depth), lambda h, *_: (qb, 0))),
        (probs, pl.BlockSpec((PAIR, HALF, rows), lambda h, *_: (first + h, qb, 0))),
        (attended, mine),
        (q, mine),
        (k, whole if qb else mine),
        (v, whole if qb else mine),
        (kp, mine if qb else whole),
        (vp, mine if qb else whole),
    ]
    aliases = {1 + len(blocked) + i: i for i in range(len(kept))}
    pair = pl.BlockSpec((2, HALF, wide), lambda h, *_: (0, 0, first + h))
    blocked += [(x, ANY) for x in kept] + [(x, corner(x)) for x in after] + [(x, half) for x in carried[1:]]
    half_out = jax.ShapeDtypeStruct((HALF, feature), bf)
    whole_out = jax.ShapeDtypeStruct((rows, feature), bf)
    return call(
        kernel, index, (steps[1] - first,), blocked, [],
        [mine, pair] + [half] * 4,
        [whole_out, jax.ShapeDtypeStruct((2, HALF, feature), bf)] + [half_out] * 4,
        16 * 2**20, 2 * HALF * depth * feature * 3, "backward", aliases=aliases,
        scratch=[pltpu.VMEM((HALF, depth), bf)],
    )


def from_behind(block, axis, distance):
    devices = range(lax.axis_size(axis))
    route = [(i - distance, i) for i in devices if i - distance in devices]
    return lax.ppermute(block, axis, route)


def shifted(block, axis, distance):
    count = lax.axis_size(axis)
    return lax.ppermute(block, axis, [((i - distance) % count, i) for i in range(count)])


def hop(block, pairs, name):
    with jax.named_scope(name):
        return lax.ppermute(block, "tp", pairs)


def body(queries, keys, values, stream, grad_stream, out_proj, doc_ids):
    q, k, v, weight = queries[0], keys[0], values[0], out_proj[0]
    grad = grad_stream[0]
    rows, feature = q.shape
    chunks = rows // HALF
    me = lax.axis_index("tp").astype(jnp.int32)
    ctx = lax.axis_index("ctx").astype(jnp.int32)
    near, across, far = me ^ 1, me ^ 2, 3 - me
    one = lambda x: x.reshape(1)

    idx = one(me)
    end = (me == 0) | (me == 3)
    bf = jnp.bfloat16
    half = lambda x, c: x[c * HALF : (c + 1) * HALF]
    both = range(chunks)

    kp = from_behind(k, "ctx", 1)
    vp = from_behind(v, "ctx", 1)
    o1 = hop(grad, OUTER, "outer1")
    m1 = hop(grad, MIDDLE, "middle1")
    grad_next = shifted(grad, "pipe", -1)
    (attended, probs, *pa), zero = forward(jnp.stack([far, ctx]), doc_ids, q, k, v, kp, vp, weight)
    o1 = gate(idx, o1, [attended])
    m2 = hop(o1, MIDDLE, "middle2")
    to_x2 = []
    for c in both:
        to_x2.append(total_of(jnp.where(end, pa[c], half(m1, c)), zero).astype(bf))
        zero = tie(idx, [to_x2[c]])
    x2 = [hop(x, OUTER, f"outer2{'ab'[c]}") for c, x in enumerate(to_x2)]
    (pb0, pb1, pc0, pc1, pd0, pd1), _ = parts(weight, jnp.stack([across, near, me]), attended, 3, to_x2, stream[0])
    pb, pc, pd = (pb0, pb1), (pc0, pc1), (pd0, pd1)
    (total,), zero = project(weight, jnp.stack([me, near]), [[(grad,)], [(o1,)]], None, [pb0])
    n3, x3 = [], []
    for c in both:
        to_n3 = total_of(pb[c], x2[c], zero).astype(bf)
        to_x3 = total_of(jnp.where(end, pb[c], half(m2, c)), zero).astype(bf)
        n3.append(hop(to_n3, MIDDLE, f"middle3{'ab'[c]}"))
        x3.append(hop(to_x3, OUTER, f"outer3{'ab'[c]}"))
        if c == 0:
            zero = tie(idx, [to_n3, to_x3])
    (total,), zero = project(
        weight, one(across), [[(jnp.where(end, x2[c], half(m2, c)),) for c in both]], total, [to_n3, to_x3]
    )
    next_grad, zero = place(idx, None, 2 * HALF, grad_next, 0, [total])
    far_and_end = jnp.stack([far, end.astype(jnp.int32)])
    hops = {}

    def launch(p, zero):
        at, height = PIECES[p]
        c = at // HALF
        piece = slice(at - c * HALF, at - c * HALF + height)
        to_f4 = total_of(pc[c][piece], n3[c][piece], zero).astype(bf)
        to_n4 = total_of(pa[c][piece], x3[c][piece], zero).astype(bf)
        hops[p] = (hop(to_f4, OUTER, f"outer4{'abcd'[p]}"), hop(to_n4, MIDDLE, f"middle4{'abcd'[p]}"))
        return [to_f4, to_n4]

    arrived, done = [], []

    def finish(p, zero):
        at, height = PIECES[p]
        c = at // HALF
        own = pd[c][at - c * HALF : at - c * HALF + height]
        rebuilt = (own.astype(jnp.float32) - total_of(*hops[p], zero)).astype(bf)
        arrived.append(shifted(rebuilt, "pipe", -1))
        done.append(rebuilt)
        return tie(idx, [rebuilt])

    pairs = feature // HD // PAIR
    run = lambda c, *rest: backward(c, weight, far_and_end, total, x3[c], m1, probs, attended, q, k, v, kp, vp, *rest)
    sends = launch(0, zero)
    (dq, send0, k0, v0, k1, v1), zero = run(0, (), sends, (0, pairs))
    back0 = from_behind(send0, "ctx", -1)
    zero = tie(idx, [n3[1], x3[1], dq])
    sends = launch(1, zero)
    (dq, send1, k0, v0, k1, v1), zero = run(1, (dq, k0, v0, k1, v1), sends, (0, pairs))
    zero = finish(0, zero)
    grads, zero = settle(idx, 0, [], k0, v0, back0, [done[0]])
    zero = tie(idx, launch(2, zero))
    zero = finish(1, zero)
    back1 = from_behind(gate(idx, send1, [done[1]]), "ctx", -1)
    finish(2, zero)
    stream_next, zero = place(idx, None, 2 * HALF, arrived[0], 0, [done[2]])
    (grad_keys, grad_values), _ = settle(idx, 1, grads, k1, v1, back1, [stream_next])
    after = [grad_keys]
    for (at, height), piece in list(zip(PIECES, arrived))[1:]:
        stream_next, _ = place(idx, stream_next, 2 * HALF, piece, at, after)
        after = []
    return tuple(x[None] for x in (dq, grad_keys, grad_values, stream_next, next_grad))


def solution(mesh):
    cut = P("pipe", "ctx", "tp")
    in_specs = (cut, cut, cut, cut, cut, P("pipe", "tp", None), P("pipe", None))
    out_specs = (cut, cut, cut, cut, cut)
    return jax.shard_map(body, mesh=mesh, in_specs=in_specs, out_specs=out_specs, check_vma=False)
```

time: 231 us -> 227 us (0.983)
  starting transfers between devices: 76.8 us -> 65.3 us
  waiting for transfers between devices: 39.7 us -> 48.9 us
    ppermute x16 -> x15, waiting for transfers between devices: 15.9 us -> 28.1 us  [hop(): return lax.ppermute(block, 'tp', pairs)]
    ppermute x16 -> x15, starting transfers between devices: 62.3 us -> 51.6 us  [hop(): return lax.ppermute(block, 'tp', pairs)]
    convert_element_type x4 -> x2, other arithmetic: 10.2 us -> 6.67 us  [body(): to_x3 = total_of(jnp.where(end, pb[c], half(m2, c)), zero).astype(bf)]
    ppermute x4, waiting for transfers between devices: 23.7 us -> 20.8 us  [shifted(): lax.ppermute(block, axis, [((i - distance) % count, i) for i in range(cou...]
    convert_element_type x3, other arithmetic: 2.96 us -> 5.55 us  [finish(): rebuilt = (own.astype(jnp.float32) - total_of(*hops[p], zero)).astype(bf)]
    pallas_call x16 -> x19, Pallas kernels: 77.9 us -> 78.3 us  [call(): pl.pallas_call(run, grid_spec=pltpu.PrefetchScalarGridSpec(num_scalar_pre...]
  transfers between devices with their start and end apart: 24 -> 23, of which waited for: 6 -> 8; matrix products, arithmetic and copies ran while one was open for 12% -> 12% of each run, Pallas kernels for 34% -> 34%
where the time goes in v3:
time: 227 us; the launch traced here: 225 us
  Pallas kernels  78.3 us (34%)
  starting transfers between devices  65.3 us (29%)
  waiting for transfers between devices  48.9 us (22%)
  other arithmetic  26.7 us (12%)
  local copies, waits for them, and re-layouts  4.56 us (2%)
    pallas_call x19, Pallas kernels, call(): pl.pallas_call(run, grid_spec=pltpu.PrefetchScalarGridSpec(num_scalar_pre...  78.3 us
    ppermute x15, starting transfers between devices, hop(): return lax.ppermute(block, 'tp', pairs)  51.6 us
    ppermute x15, waiting for transfers between devices, hop(): return lax.ppermute(block, 'tp', pairs)  28.1 us
    ppermute x4, waiting for transfers between devices, shifted(): lax.ppermute(block, axis, [((i - distance) % count, i) for i in range(cou...  20.8 us
    ppermute x4, starting transfers between devices, from_behind(): return lax.ppermute(block, axis, route)  8.96 us
    convert_element_type x2, other arithmetic, body(): to_x3 = total_of(jnp.where(end, pb[c], half(m2, c)), zero).astype(bf)  6.67 us
    convert_element_type x3, other arithmetic, finish(): rebuilt = (own.astype(jnp.float32) - total_of(*hops[p], zero)).astype(bf)  5.55 us
    convert_element_type x2, other arithmetic, body(): to_x2.append(total_of(jnp.where(end, pa[c], half(m1, c)), zero).astype(bf))  5.43 us
  transfers between devices with their start and end apart: 23, of which 8 were waited for; matrix products, arithmetic and copies ran while one was open for 12% of the time, Pallas kernels for 34%

profile of v3, /device:TPU:0, one launch (start us, length us, event | category | flops | bytes accessed | tf_op | source)
XLA Modules:
  0.0 225.0 jit_solution(10065631578458386750)
XLA Ops:
  0.6 3.1 %collective-permute-start.4 = (bf16[512,2048]{1,0:T(8,128)(2,1)}, bf16[512,2048]{1,0:T(8,128)(2,1)S(1)}, u32[]{:S(2)}, u32[]{:S(2)}) collective-permute-start(bf16[512,2048]{1,0:T(8,128)(2,1)} %bitcast.51), channel_id=1, source_target_pairs={{0,1},{1,0},{2,3},{3,2},{4,5},{5,4},{6,7},{7,6},{8,9},{9,8},{10,11... | collective-permute-start | bytes 6291464 | tf_op jit(solution)/shard_map/outer1/ppermute | solution.py:414
  3.7 2.0 collective-permute-start.2
  7.2 4.9 %collective-permute-start.1 = (bf16[512,1024]{1,0:T(8,128)(2,1)}, bf16[512,1024]{1,0:T(8,128)(2,1)}, u32[]{:S(2)}, u32[]{:S(2)}) collective-permute-start(bf16[512,1024]{1,0:T(8,128)(2,1)} %bitcast.46), channel_id=1, source_target_pairs={{0,4},{4,8},{8,12},{1,5},{5,9},{9,13},{2,6},{6,10},{10,14},{3,7},{... | collective-permute-start | bytes 3145736 | tf_op jit(solution)/shard_map/ppermute | solution.py:404
  15.5 16.9 %attend.1 = (bf16[512,1024]{1,0:T(8,128)(2,1)S(1)}, bf16[8,512,512]{2,1,0:T(8,128)(2,1)}, bf16[256,2048]{1,0:T(8,128)(2,1)S(1)}, bf16[256,2048]{1,0:T(8,128)(2,1)S(1)}, f32[1,1]{1,0:T(1,128)}) custom-call(s32[2]{0:T(128)S(1)} %pad_add_fusion.1.index_ref, s32[1,2048]{1,0:T(1,128)S(1)} %copy-done.12, bf16[512,1024]{1,0:T(8,128)(2,1)} %bitcast.39, ...), custom_call_target="tpu_custom_call" | custom-call | flops 1610612736 | bytes 8388608 | tf_op jit(solution)/shard_map/attend/pallas_call | solution.py:133
  32.5 17.1 %collective-permute-done.4.refs_0_ = bf16[512,2048]{1,0:T(8,128)(2,1)S(1)} collective-permute-done((bf16[512,2048]{1,0:T(8,128)(2,1)}, bf16[512,2048]{1,0:T(8,128)(2,1)S(1)}, u32[]{:S(2)}, u32[]{:S(2)}) %collective-permute-start.4) | collective-permute-done | bytes 2097184 | tf_op jit(solution)/shard_map/outer1/ppermute | solution.py:414
  50.1 2.0 collective-permute-start.5
  52.2 2.3 %add_convert_fusion.7.refs_0_.refs_5_ = bf16[256,2048]{1,0:T(8,128)(2,1)S(1)} fusion(bf16[256,2048]{1,0:T(8,128)(2,1)S(1)} %get-tuple-element.44, bf16[512,2048]{1,0:T(8,128)(2,1)} %collective-permute-done.2.refs_3_, f32[]{:T(128)} %bitcast.9, pred[]{:T(512)S(6)} %or.3), kind=kLoop, calls=%fused_computation.8 | loop fusion | flops 2097152 | bytes 3145733 | tf_op jit(solution)/shard_map/convert_element_type | solution.py:443
  55.0 3.3 %collective-permute-start.3 = (bf16[256,2048]{1,0:T(8,128)(2,1)S(1)}, bf16[256,2048]{1,0:T(8,128)(2,1)}, u32[]{:S(2)}, u32[]{:S(2)}) collective-permute-start(bf16[256,2048]{1,0:T(8,128)(2,1)S(1)} %add_convert_fusion.7.refs_0_.refs_5_), channel_id=1, source_target_pairs={{0,1},{1,0},{2,3},{3,2},{4,5},{5,4},{6,7},{7,6},{8,9},{9,8},{10,11... | collective-permute-start | bytes 3145736 | tf_op jit(solution)/shard_map/outer2a/ppermute | solution.py:414
  58.3 3.2 %add_convert_fusion.6.refs_6_ = bf16[256,2048]{1,0:T(8,128)(2,1)} fusion(bf16[256,2048]{1,0:T(8,128)(2,1)S(1)} %get-tuple-element.48, bf16[512,2048]{1,0:T(8,128)(2,1)} %collective-permute-done.2.refs_3_, f32[]{:T(128)} %bitcast.11, pred[]{:T(512)S(6)} %or.3), kind=kLoop, calls=%fused_computation.7 | loop fusion | flops 2097152 | bytes 3145733 | tf_op jit(solution)/shard_map/convert_element_type | solution.py:443
  61.5 12.3 %parts.1 = (bf16[256,2048]{1,0:T(8,128)(2,1)S(1)}, bf16[256,2048]{1,0:T(8,128)(2,1)S(1)}, bf16[256,2048]{1,0:T(8,128)(2,1)S(1)}, bf16[256,2048]{1,0:T(8,128)(2,1...) custom-call(s32[3]{0:T(128)S(1)} %pad_add_fusion.3.index_ref, bf16[512,1024]{1,0:T(8,128)(2,1)} %copy-done, ...), custom_call_target="tpu_custom_call" | custom-call | flops 6442450944 | bytes 12582912 | tf_op jit(solution)/shard_map/parts/pallas_call | solution.py:133
  73.8 9.6 %project.2 = (f32[512,1024]{1,0:T(8,128)S(1)}, f32[1,1]{1,0:T(1,128)}) custom-call(s32[2]{0:T(128)S(1)} %pad_add_fusion.2.index_ref, bf16[1024,8192]{1,0:T(8,128)(2,1)} %bitcast.33, bf16[1024,8192]{1,0:T(8,128)(2,1)} %bitcast.34, bf16[512,2048]{1,0:T(8,128)(2,1)} %bitcast.54, bf16[512,2048]{1,0:T(8,128)(2,1)} %copy-done.4, ...), custom_call_target="tpu_custom_call" | custom-call | flops 4294967296 | bytes 8388608 | tf_op jit(solution)/shard_map/project/pallas_call | solution.py:133
  83.4 2.9 %add_convert_fusion.4 = (bf16[256,2048]{1,0:T(8,128)(2,1)S(1)}, bf16[256,2048]{1,0:T(8,128)(2,1)S(1)}) fusion(bf16[256,2048]{1,0:T(8,128)(2,1)S(1)} %get-tuple-element.49.refs_4_, f32[]{:T(128)} %bitcast.14, pred[]{:T(512)S(6)} %or.3, bf16[512,2048]{1,0:T(8,128)(2,1)} %collective-permute-done.5, bf16[256,2048]{1,0:T(8,128)(2,1)} %collective-permute-done.3), kind=kLoop, calls=%fused_computation.5 | loop fusion | flops 4718592 | bytes 5242885 | tf_op jit(solution)/shard_map/convert_element_type | solution.py:452
  86.3 18.0 %collective-permute-start.8 = (bf16[256,2048]{1,0:T(8,128)(2,1)S(1)}, bf16[256,2048]{1,0:T(8,128)(2,1)S(1)}, u32[]{:S(2)}, u32[]{:S(2)}) collective-permute-start(bf16[256,2048]{1,0:T(8,128)(2,1)S(1)} %get-tuple-element.87.refs_1_), channel_id=1, source_target_pairs={{0,1},{1,0},{2,3},{3,2},{4,5},{5,4},{6,7},{7,6},{8,9},{9,8},{10,11... | collective-permute-start | bytes 3145736 | tf_op jit(solution)/shard_map/outer3a/ppermute | solution.py:414
  105.6 3.8 %add_convert_fusion.2 = (bf16[256,2048]{1,0:T(8,128)(2,1)}, bf16[256,2048]{1,0:T(8,128)(2,1)S(1)}) fusion(bf16[256,2048]{1,0:T(8,128)(2,1)S(1)} %get-tuple-element.51, f32[]{:T(128)} %bitcast.15, pred[]{:T(512)S(6)} %or.3, bf16[512,2048]{1,0:T(8,128)(2,1)} %collective-permute-done.5, bf16[256,2048]{1,0:T(8,128)(2,1)} %collective-permute-done.6), kind=kLoop, calls=%fused_computation.3 | loop fusion | flops 4718592 | bytes 5242885 | tf_op jit(solution)/shard_map/convert_element_type | solution.py:452
  109.4 3.4 %collective-permute-start.7 = (bf16[256,2048]{1,0:T(8,128)(2,1)}, bf16[256,2048]{1,0:T(8,128)(2,1)S(1)}, u32[]{:S(2)}, u32[]{:S(2)}) collective-permute-start(bf16[256,2048]{1,0:T(8,128)(2,1)} %get-tuple-element.85.refs_5_), channel_id=1, source_target_pairs={{0,1},{1,0},{2,3},{3,2},{4,5},{5,4},{6,7},{7,6},{8,9},{9,8},{10,11... | collective-permute-start | bytes 3145736 | tf_op jit(solution)/shard_map/outer3b/ppermute | solution.py:414
  113.5 2.4 %broadcast_select_fusion = (bf16[256,2048]{1,0:T(8,128)(2,1)S(1)}, bf16[256,2048]{1,0:T(8,128)(2,1)S(1)}) fusion(bf16[256,2048]{1,0:T(8,128)(2,1)} %collective-permute-done.6, pred[]{:T(512)S(6)} %or.3, bf16[512,2048]{1,0:T(8,128)(2,1)} %collective-permute-done.5, bf16[256,2048]{1,0:T(8,128)(2,1)} %collective-permute-done.3), kind=kLoop, calls=%fused_computation.17 | loop fusion | flops 1048576 | bytes 6291457 | tf_op jit(solution)/shard_map/jit(_where)/select_n | solution.py:458
  115.9 6.2 %project.3 = (f32[512,1024]{1,0:T(8,128)}, f32[1,1]{1,0:T(1,128)}) custom-call(s32[1]{0:T(128)} %bitcast.3.index_ref, bf16[1024,8192]{1,0:T(8,128)(2,1)} %bitcast.35, bf16[256,2048]{1,0:T(8,128)(2,1)S(1)} %get-tuple-element.84.refs_1_, bf16[256,2048]{1,0:T(8,128)(2,1)S(1)} %get-tuple-element.83.refs_2_, f32[512,1024]{1,0:T(8,128)} %copy-done.7, ...), custom_call_target="tpu_custom_call" | custom-call | flops 2147483648 | bytes 4194304 | tf_op jit(solution)/shard_map/project/pallas_call | solution.py:133
  122.1 3.1 %place.4 = (bf16[512,2048]{1,0:T(8,128)(2,1)}, f32[1,1]{1,0:T(1,128)}) custom-call(s32[1]{0:T(128)} %bitcast.10.index_ref, bf16[512,2048]{1,0:T(8,128)(2,1)} %collective-permute-done.10.refs_0_, f32[512,1024]{1,0:T(8,128)} %get-tuple-element.53.refs_1_), custom_call_target="tpu_custom_call" | custom-call | bytes 4194304 | tf_op jit(solution)/shard_map/place/pallas_call | solution.py:133
  125.1 2.9 %collective-permute-done.8.refs_2_ = bf16[256,2048]{1,0:T(8,128)(2,1)S(1)} collective-permute-done((bf16[256,2048]{1,0:T(8,128)(2,1)S(1)}, bf16[256,2048]{1,0:T(8,128)(2,1)S(1)}, u32[]{:S(2)}, u32[]{:S(2)}) %collective-permute-start.8) | collective-permute-done | bytes 1048608 | tf_op jit(solution)/shard_map/outer3a/ppermute | solution.py:414
  128.1 2.1 add_convert_fusion.refs_12_
  132.9 5.0 %collective-permute-start.15 = (bf16[256,2048]{1,0:T(8,128)(2,1)S(1)}, bf16[256,2048]{1,0:T(8,128)(2,1)}, u32[]{:S(2)}, u32[]{:S(2)}) collective-permute-start(bf16[256,2048]{1,0:T(8,128)(2,1)S(1)} %add_convert_fusion.1.refs_11_), channel_id=1, source_target_pairs={{0,1},{1,0},{2,3},{3,2},{4,5},{5,4},{6,7},{7,6},{8,9},{9,8},{10,11... | collective-permute-start | bytes 3145736 | tf_op jit(solution)/shard_map/outer4a/ppermute | solution.py:414
  137.9 10.3 %backward.2 = (bf16[512,1024]{1,0:T(8,128)(2,1)}, bf16[2,256,1024]{2,1,0:T(8,128)(2,1)S(1)}, bf16[256,1024]{1,0:T(8,128)(2,1)S(1)}, bf16[256,1024]{1,0:T(8,128)(...) custom-call(s32[2]{0:T(128)S(1)} %pad_add_fusion.index_ref, ...), custom_call_target="tpu_custom_call" | custom-call | flops 3221225472 | bytes 16777216 | tf_op jit(solution)/shard_map/backward/pallas_call | solution.py:133
  148.2 2.4 %collective-permute-done.7.refs_1_.refs_2_ = bf16[256,2048]{1,0:T(8,128)(2,1)S(1)} collective-permute-done((bf16[256,2048]{1,0:T(8,128)(2,1)}, bf16[256,2048]{1,0:T(8,128)(2,1)S(1)}, u32[]{:S(2)}, u32[]{:S(2)}) %collective-permute-start.7) | collective-permute-done | bytes 1048608 | tf_op jit(solution)/shard_map/outer3b/ppermute | solution.py:414
  153.5 4.6 %collective-permute-start.12 = (bf16[128,2048]{1,0:T(8,128)(2,1)S(1)}, bf16[128,2048]{1,0:T(8,128)(2,1)S(1)}, u32[]{:S(2)}, u32[]{:S(2)}) collective-permute-start(bf16[128,2048]{1,0:T(8,128)(2,1)S(1)} %add_convert_fusion.11.refs_12_), channel_id=1, source_target_pairs={{0,1},{1,0},{2,3},{3,2},{4,5},{5,4},{6,7},{7,6},{8,9},{9,8},{10,11... | collective-permute-start | bytes 1572872 | tf_op jit(solution)/shard_map/outer4b/ppermute | solution.py:414
  161.7 10.7 %backward.3 = (bf16[512,1024]{1,0:T(8,128)(2,1)}, bf16[2,256,1024]{2,1,0:T(8,128)(2,1)}, bf16[256,1024]{1,0:T(8,128)(2,1)S(1)}, bf16[256,1024]{1,0:T(8,128)(2,1)...) custom-call(s32[2]{0:T(128)S(1)} %pad_add_fusion.index_ref, ...), custom_call_target="tpu_custom_call", output_to_operand_aliasing={{0}: (12, {})} | custom-call | flops 3221225472 | bytes 16777216 | tf_op jit(solution)/shard_map/backward/pallas_call | solution.py:133
  173.1 2.7 %subtract_convert_fusion.refs_3_ = bf16[256,2048]{1,0:T(8,128)(2,1)S(1)} fusion(bf16[256,2048]{1,0:T(8,128)(2,1)} %collective-permute-done.16, bf16[256,2048]{1,0:T(8,128)(2,1)} %collective-permute-done.15, bf16[256,2048]{1,0:T(8,128)(2,1)S(1)} %copy-done.17, f32[]{:T(128)} %bitcast.19), kind=kLoop, calls=%fused_computation | loop fusion | flops 3670016 | bytes 4194308 | tf_op jit(solution)/shard_map/convert_element_type | solution.py:479
  179.5 4.9 %collective-permute-start.19 = (bf16[128,2048]{1,0:T(8,128)(2,1)S(1)}, bf16[128,2048]{1,0:T(8,128)(2,1)S(1)}, u32[]{:S(2)}, u32[]{:S(2)}) collective-permute-start(bf16[128,2048]{1,0:T(8,128)(2,1)S(1)} %add_convert_fusion.9.refs_0_), channel_id=1, source_target_pairs={{0,1},{1,0},{2,3},{3,2},{4,5},{5,4},{6,7},{7,6},{8,9},{9,8},{10,11... | collective-permute-start | bytes 1572872 | tf_op jit(solution)/shard_map/outer4c/ppermute | solution.py:414
  186.5 1.9 subtract_convert_fusion.2.refs_1_.refs_0_
  191.4 4.9 %collective-permute-done.19 = bf16[128,2048]{1,0:T(8,128)(2,1)S(1)} collective-permute-done((bf16[128,2048]{1,0:T(8,128)(2,1)S(1)}, bf16[128,2048]{1,0:T(8,128)(2,1)S(1)}, u32[]{:S(2)}, u32[]{:S(2)}) %collective-permute-start.19) | collective-permute-done | bytes 524320 | tf_op jit(solution)/shard_map/outer4c/ppermute | solution.py:414
  198.3 3.6 %collective-permute-done.18.refs_0_ = bf16[256,2048]{1,0:T(8,128)(2,1)S(1)} collective-permute-done((bf16[256,2048]{1,0:T(8,128)(2,1)S(1)}, bf16[256,2048]{1,0:T(8,128)(2,1)S(1)}, u32[]{:S(2)}, u32[]{:S(2)}) %collective-permute-start.18) | collective-permute-done | bytes 1048608 | tf_op jit(solution)/shard_map/ppermute | solution.py:409
  204.8 8.3 %collective-permute-done.22.refs_0_ = bf16[128,2048]{1,0:T(8,128)(2,1)S(1)} collective-permute-done((bf16[128,2048]{1,0:T(8,128)(2,1)S(1)}, bf16[128,2048]{1,0:T(8,128)(2,1)S(1)}, u32[]{:S(2)}, u32[]{:S(2)}) %collective-permute-start.22) | collective-permute-done | bytes 524320 | tf_op jit(solution)/shard_map/ppermute | solution.py:409
  215.2 8.8 %collective-permute-done.21.refs_0_ = bf16[128,2048]{1,0:T(8,128)(2,1)S(1)} collective-permute-done((bf16[128,2048]{1,0:T(8,128)(2,1)S(1)}, bf16[128,2048]{1,0:T(8,128)(2,1)S(1)}, u32[]{:S(2)}, u32[]{:S(2)}) %collective-permute-start.21) | collective-permute-done | bytes 524320 | tf_op jit(solution)/shard_map/ppermute | solution.py:409
  (91 shorter events, 34.3 us)
Async XLA Ops:
  0.6 48.9 %collective-permute-start.4 = (bf16[512,2048]{1,0:T(8,128)(2,1)}, bf16[512,2048]{1,0:T(8,128)(2,1)S(1)}, u32[]{:S(2)}, u32[]{:S(2)}) collective-permute-start(bf16[512,2048]{1,0:T(8,128)(2,1)} %bitcast.51), channel_id=1, source_target_pairs={{0,1},{1,0},{2,3},{3,2},{4,5},{5,4},{6,7},{7,6},{8,9},{9,8},{10,11... | collective-permute-start | bytes 6291464 | tf_op jit(solution)/shard_map/outer1/ppermute | solution.py:414
  3.7 48.4 %collective-permute-start.2 = (bf16[512,2048]{1,0:T(8,128)(2,1)}, bf16[512,2048]{1,0:T(8,128)(2,1)}, u32[]{:S(2)}, u32[]{:S(2)}) collective-permute-start(bf16[512,2048]{1,0:T(8,128)(2,1)} %bitcast.52), channel_id=1, source_target_pairs={{1,2},{2,1},{5,6},{6,5},{9,10},{10,9},{13,14},{14,13},{17,18},{18,... | collective-permute-start | bytes 6291464 | tf_op jit(solution)/shard_map/middle1/ppermute | solution.py:414
  5.7 8.1 %collective-permute-start = (bf16[512,1024]{1,0:T(8,128)(2,1)}, bf16[512,1024]{1,0:T(8,128)(2,1)S(1)}, u32[]{:S(2)}, u32[]{:S(2)}) collective-permute-start(bf16[512,1024]{1,0:T(8,128)(2,1)} %bitcast.42), channel_id=1, source_target_pairs={{0,4},{4,8},{8,12},{1,5},{5,9},{9,13},{2,6},{6,10},{10,14},{3,7},{... | collective-permute-start | bytes 3145736 | tf_op jit(solution)/shard_map/ppermute | solution.py:404
  7.2 6.6 %collective-permute-start.1 = (bf16[512,1024]{1,0:T(8,128)(2,1)}, bf16[512,1024]{1,0:T(8,128)(2,1)}, u32[]{:S(2)}, u32[]{:S(2)}) collective-permute-start(bf16[512,1024]{1,0:T(8,128)(2,1)} %bitcast.46), channel_id=1, source_target_pairs={{0,4},{4,8},{8,12},{1,5},{5,9},{9,13},{2,6},{6,10},{10,14},{3,7},{... | collective-permute-start | bytes 3145736 | tf_op jit(solution)/shard_map/ppermute | solution.py:404
  12.1 110.0 %collective-permute-start.10 = (bf16[512,2048]{1,0:T(8,128)(2,1)}, bf16[512,2048]{1,0:T(8,128)(2,1)}, u32[]{:S(2)}, u32[]{:S(2)}) collective-permute-start(bf16[512,2048]{1,0:T(8,128)(2,1)} %bitcast.53), channel_id=1, source_target_pairs={{16,0},{0,16},{17,1},{1,17},{18,2},{2,18},{19,3},{3,19},{20,4},{4,... | collective-permute-start | bytes 6291464 | tf_op jit(solution)/shard_map/ppermute | solution.py:409
  32.5 22.0 %copy-start = (bf16[512,1024]{1,0:T(8,128)(2,1)}, bf16[512,1024]{1,0:T(8,128)(2,1)S(1)}, u32[]{:S(2)}) copy-start(bf16[512,1024]{1,0:T(8,128)(2,1)S(1)} %get-tuple-element.46.refs_1_.refs_0_.refs_5_) | copy-start | bytes 3145732
  50.1 33.3 %collective-permute-start.5 = (bf16[512,2048]{1,0:T(8,128)(2,1)S(1)}, bf16[512,2048]{1,0:T(8,128)(2,1)}, u32[]{:S(2)}, u32[]{:S(2)}) collective-permute-start(bf16[512,2048]{1,0:T(8,128)(2,1)S(1)} %get-tuple-element.47.refs_3_), channel_id=1, source_target_pairs={{1,2},{2,1},{5,6},{6,5},{9,10},{10,9},{13,14},{14,13},{17,18},{18,... | collective-permute-start | bytes 6291464 | tf_op jit(solution)/shard_map/middle2/ppermute | solution.py:414
  54.5 7.0 %copy-start.3 = (bf16[256,2048]{1,0:T(8,128)(2,1)}, bf16[256,2048]{1,0:T(8,128)(2,1)S(1)}, u32[]{:S(2)}) copy-start(bf16[256,2048]{1,0:T(8,128)(2,1)S(1)} %add_convert_fusion.7.refs_0_.refs_5_) | copy-start | bytes 3145732
  55.0 28.4 %collective-permute-start.3 = (bf16[256,2048]{1,0:T(8,128)(2,1)S(1)}, bf16[256,2048]{1,0:T(8,128)(2,1)}, u32[]{:S(2)}, u32[]{:S(2)}) collective-permute-start(bf16[256,2048]{1,0:T(8,128)(2,1)S(1)} %add_convert_fusion.7.refs_0_.refs_5_), channel_id=1, source_target_pairs={{0,1},{1,0},{2,3},{3,2},{4,5},{5,4},{6,7},{7,6},{8,9},{9,8},{10,11... | collective-permute-start | bytes 3145736 | tf_op jit(solution)/shard_map/outer2a/ppermute | solution.py:414
  61.5 44.1 %collective-permute-start.6 = (bf16[256,2048]{1,0:T(8,128)(2,1)}, bf16[256,2048]{1,0:T(8,128)(2,1)}, u32[]{:S(2)}, u32[]{:S(2)}) collective-permute-start(bf16[256,2048]{1,0:T(8,128)(2,1)} %add_convert_fusion.6.refs_6_), channel_id=1, source_target_pairs={{0,1},{1,0},{2,3},{3,2},{4,5},{5,4},{6,7},{7,6},{8,9},{9,8},{10,11... | collective-permute-start | bytes 3145736 | tf_op jit(solution)/shard_map/outer2b/ppermute | solution.py:414
  86.3 41.8 %collective-permute-start.8 = (bf16[256,2048]{1,0:T(8,128)(2,1)S(1)}, bf16[256,2048]{1,0:T(8,128)(2,1)S(1)}, u32[]{:S(2)}, u32[]{:S(2)}) collective-permute-start(bf16[256,2048]{1,0:T(8,128)(2,1)S(1)} %get-tuple-element.87.refs_1_), channel_id=1, source_target_pairs={{0,1},{1,0},{2,3},{3,2},{4,5},{5,4},{6,7},{7,6},{8,9},{9,8},{10,11... | collective-permute-start | bytes 3145736 | tf_op jit(solution)/shard_map/outer3a/ppermute | solution.py:414
  104.9 26.9 %collective-permute-start.9 = (bf16[256,2048]{1,0:T(8,128)(2,1)S(1)}, bf16[256,2048]{1,0:T(8,128)(2,1)S(1)}, u32[]{:S(2)}, u32[]{:S(2)}) collective-permute-start(bf16[256,2048]{1,0:T(8,128)(2,1)S(1)} %get-tuple-element.88.refs_0_), channel_id=1, source_target_pairs={{1,2},{2,1},{5,6},{6,5},{9,10},{10,9},{13,14},{14,13},{17,18},{18,... | collective-permute-start | bytes 3145736 | tf_op jit(solution)/shard_map/middle3a/ppermute | solution.py:414
  109.4 41.2 %collective-permute-start.7 = (bf16[256,2048]{1,0:T(8,128)(2,1)}, bf16[256,2048]{1,0:T(8,128)(2,1)S(1)}, u32[]{:S(2)}, u32[]{:S(2)}) collective-permute-start(bf16[256,2048]{1,0:T(8,128)(2,1)} %get-tuple-element.85.refs_5_), channel_id=1, source_target_pairs={{0,1},{1,0},{2,3},{3,2},{4,5},{5,4},{6,7},{7,6},{8,9},{9,8},{10,11... | collective-permute-start | bytes 3145736 | tf_op jit(solution)/shard_map/outer3b/ppermute | solution.py:414
  112.7 37.8 %collective-permute-start.11 = (bf16[256,2048]{1,0:T(8,128)(2,1)S(1)}, bf16[256,2048]{1,0:T(8,128)(2,1)S(1)}, u32[]{:S(2)}, u32[]{:S(2)}) collective-permute-start(bf16[256,2048]{1,0:T(8,128)(2,1)S(1)} %get-tuple-element.86.refs_4_), channel_id=1, source_target_pairs={{1,2},{2,1},{5,6},{6,5},{9,10},{10,9},{13,14},{14,13},{17,18},{18,... | collective-permute-start | bytes 3145736 | tf_op jit(solution)/shard_map/middle3b/ppermute | solution.py:414
  130.2 42.2 %collective-permute-start.16 = (bf16[256,2048]{1,0:T(8,128)(2,1)}, bf16[256,2048]{1,0:T(8,128)(2,1)}, u32[]{:S(2)}, u32[]{:S(2)}) collective-permute-start(bf16[256,2048]{1,0:T(8,128)(2,1)} %add_convert_fusion.refs_12_), channel_id=1, source_target_pairs={{1,2},{2,1},{5,6},{6,5},{9,10},{10,9},{13,14},{14,13},{17,18},{18,... | collective-permute-start | bytes 3145736 | tf_op jit(solution)/shard_map/middle4a/ppermute | solution.py:414
  132.9 40.3 %collective-permute-start.15 = (bf16[256,2048]{1,0:T(8,128)(2,1)S(1)}, bf16[256,2048]{1,0:T(8,128)(2,1)}, u32[]{:S(2)}, u32[]{:S(2)}) collective-permute-start(bf16[256,2048]{1,0:T(8,128)(2,1)S(1)} %add_convert_fusion.1.refs_11_), channel_id=1, source_target_pairs={{0,1},{1,0},{2,3},{3,2},{4,5},{5,4},{6,7},{7,6},{8,9},{9,8},{10,11... | collective-permute-start | bytes 3145736 | tf_op jit(solution)/shard_map/outer4a/ppermute | solution.py:414
  137.9 14.8 %copy-start.18 = (bf16[256,2048]{1,0:T(8,128)(2,1)S(1)}, bf16[256,2048]{1,0:T(8,128)(2,1)}, u32[]{:S(2)}) copy-start(bf16[256,2048]{1,0:T(8,128)(2,1)} %get-tuple-element.58) | copy-start | bytes 3145732
  148.1 5.4 %copy-start.9 = (bf16[256,1024]{1,0:T(8,128)(2,1)}, bf16[256,1024]{1,0:T(8,128)(2,1)S(1)}, u32[]{:S(2)}) copy-start(bf16[256,1024]{1,0:T(8,128)(2,1)S(1)} %get-tuple-element.60.refs_15_) | copy-start | bytes 1572868
  150.6 8.8 %copy-start.1 = (bf16[256,2048]{1,0:T(8,128)(2,1)}, bf16[256,2048]{1,0:T(8,128)(2,1)S(1)}, u32[]{:S(2)}) copy-start(bf16[256,2048]{1,0:T(8,128)(2,1)S(1)} %collective-permute-done.7.refs_1_.refs_2_) | copy-start | bytes 3145732
  153.5 33.0 %collective-permute-start.12 = (bf16[128,2048]{1,0:T(8,128)(2,1)S(1)}, bf16[128,2048]{1,0:T(8,128)(2,1)S(1)}, u32[]{:S(2)}, u32[]{:S(2)}) collective-permute-start(bf16[128,2048]{1,0:T(8,128)(2,1)S(1)} %add_convert_fusion.11.refs_12_), channel_id=1, source_target_pairs={{0,1},{1,0},{2,3},{3,2},{4,5},{5,4},{6,7},{7,6},{8,9},{9,8},{10,11... | collective-permute-start | bytes 1572872 | tf_op jit(solution)/shard_map/outer4b/ppermute | solution.py:414
  158.1 19.4 %collective-permute-start.14 = (bf16[2,256,1024]{2,1,0:T(8,128)(2,1)S(1)}, bf16[2,256,1024]{2,1,0:T(8,128)(2,1)S(1)}, u32[]{:S(2)}, u32[]{:S(2)}) collective-permute-start(bf16[2,256,1024]{2,1,0:T(8,128)(2,1)S(1)} %get-tuple-element.70), channel_id=1, source_target_pairs={{4,0},{8,4},{12,8},{5,1},{9,5},{13,9},{6,2},{10,6},{14,10},{7,3},{... | collective-permute-start | bytes 3145736 | tf_op jit(solution)/shard_map/ppermute | solution.py:404
  160.2 26.3 %collective-permute-start.13 = (bf16[128,2048]{1,0:T(8,128)(2,1)S(1)}, bf16[128,2048]{1,0:T(8,128)(2,1)}, u32[]{:S(2)}, u32[]{:S(2)}) collective-permute-start(bf16[128,2048]{1,0:T(8,128)(2,1)S(1)} %add_convert_fusion.10.refs_13_), channel_id=1, source_target_pairs={{1,2},{2,1},{5,6},{6,5},{9,10},{10,9},{13,14},{14,13},{17,18},{18,... | collective-permute-start | bytes 1572872 | tf_op jit(solution)/shard_map/middle4b/ppermute | solution.py:414
  161.7 11.5 %copy-start.17 = (bf16[256,2048]{1,0:T(8,128)(2,1)S(1)}, bf16[256,2048]{1,0:T(8,128)(2,1)}, u32[]{:S(2)}) copy-start(bf16[256,2048]{1,0:T(8,128)(2,1)} %get-tuple-element.71) | copy-start | bytes 3145732
  175.9 26.0 %collective-permute-start.18 = (bf16[256,2048]{1,0:T(8,128)(2,1)S(1)}, bf16[256,2048]{1,0:T(8,128)(2,1)S(1)}, u32[]{:S(2)}, u32[]{:S(2)}) collective-permute-start(bf16[256,2048]{1,0:T(8,128)(2,1)S(1)} %subtract_convert_fusion.refs_3_), channel_id=1, source_target_pairs={{16,0},{0,16},{17,1},{1,17},{18,2},{2,18},{19,3},{3,19},{20,4},{4,... | collective-permute-start | bytes 3145736 | tf_op jit(solution)/shard_map/ppermute | solution.py:409
  177.4 7.0 %copy-start.2 = (bf16[256,2048]{1,0:T(8,128)(2,1)S(1)}, bf16[256,2048]{1,0:T(8,128)(2,1)}, u32[]{:S(2)}) copy-start(bf16[256,2048]{1,0:T(8,128)(2,1)} %copy-done.1) | copy-start | bytes 3145732
  178.7 7.9 %copy-start.16 = (bf16[256,2048]{1,0:T(8,128)(2,1)S(1)}, bf16[256,2048]{1,0:T(8,128)(2,1)}, u32[]{:S(2)}) copy-start(bf16[256,2048]{1,0:T(8,128)(2,1)} %get-tuple-element.67) | copy-start | bytes 3145732
  179.5 8.9 %copy-start.8 = (bf16[2,256,1024]{2,1,0:T(8,128)(2,1)S(1)}, bf16[2,256,1024]{2,1,0:T(8,128)(2,1)}, u32[]{:S(2)}) copy-start(bf16[2,256,1024]{2,1,0:T(8,128)(2,1)} %get-tuple-element.66.refs_0_) | copy-start | bytes 3145732
  179.5 16.7 %collective-permute-start.19 = (bf16[128,2048]{1,0:T(8,128)(2,1)S(1)}, bf16[128,2048]{1,0:T(8,128)(2,1)S(1)}, u32[]{:S(2)}, u32[]{:S(2)}) collective-permute-start(bf16[128,2048]{1,0:T(8,128)(2,1)S(1)} %add_convert_fusion.9.refs_0_), channel_id=1, source_target_pairs={{0,1},{1,0},{2,3},{3,2},{4,5},{5,4},{6,7},{7,6},{8,9},{9,8},{10,11... | collective-permute-start | bytes 1572872 | tf_op jit(solution)/shard_map/outer4c/ppermute | solution.py:414
  185.8 10.5 %collective-permute-start.20 = (bf16[128,2048]{1,0:T(8,128)(2,1)S(1)}, bf16[128,2048]{1,0:T(8,128)(2,1)S(1)}, u32[]{:S(2)}, u32[]{:S(2)}) collective-permute-start(bf16[128,2048]{1,0:T(8,128)(2,1)S(1)} %add_convert_fusion.8.refs_1_), channel_id=1, source_target_pairs={{1,2},{2,1},{5,6},{6,5},{9,10},{10,9},{13,14},{14,13},{17,18},{18,... | collective-permute-start | bytes 1572872 | tf_op jit(solution)/shard_map/middle4c/ppermute | solution.py:414
  189.0 13.9 %collective-permute-start.17 = (bf16[2,256,1024]{2,1,0:T(8,128)(2,1)S(1)}, bf16[2,256,1024]{2,1,0:T(8,128)(2,1)S(1)}, u32[]{:S(2)}, u32[]{:S(2)}) collective-permute-start(bf16[2,256,1024]{2,1,0:T(8,128)(2,1)S(1)} %get-tuple-element.74), channel_id=1, source_target_pairs={{4,0},{8,4},{12,8},{5,1},{9,5},{13,9},{6,2},{10,6},{14,10},{7,3},{... | collective-permute-start | bytes 3145736 | tf_op jit(solution)/shard_map/ppermute | solution.py:404
  190.8 22.3 %collective-permute-start.22 = (bf16[128,2048]{1,0:T(8,128)(2,1)S(1)}, bf16[128,2048]{1,0:T(8,128)(2,1)S(1)}, u32[]{:S(2)}, u32[]{:S(2)}) collective-permute-start(bf16[128,2048]{1,0:T(8,128)(2,1)S(1)} %subtract_convert_fusion.2.refs_1_.refs_0_), channel_id=1, source_target_pairs={{16,0},{0,16},{17,1},{1,17},{18,2},{2,18},{19,3},{3,19},{20,4},{4,... | collective-permute-start | bytes 1572872 | tf_op jit(solution)/shard_map/ppermute | solution.py:409
  197.2 26.8 %collective-permute-start.21 = (bf16[128,2048]{1,0:T(8,128)(2,1)S(1)}, bf16[128,2048]{1,0:T(8,128)(2,1)S(1)}, u32[]{:S(2)}, u32[]{:S(2)}) collective-permute-start(bf16[128,2048]{1,0:T(8,128)(2,1)S(1)} %subtract_convert_fusion.1.refs_1_), channel_id=1, source_target_pairs={{16,0},{0,16},{17,1},{1,17},{18,2},{2,18},{19,3},{3,19},{20,4},{4,... | collective-permute-start | bytes 1572872 | tf_op jit(solution)/shard_map/ppermute | solution.py:409
  (11 other events, 35.7 us)

commit v4 on v3

--- a/solution.py
+++ b/solution.py
@@ -13,7 +13,7 @@
 HALF = 256
 PIECES = [(0, 256), (256, 128), (384, 128)]
 PAIR = 4
-VMEM_LIMIT = 50 * 1024 * 1024
+VMEM_LIMIT = 44 * 1024 * 1024
 COST = 1.0
 
 OUTER = [(0, 1), (1, 0), (2, 3), (3, 2)]

time: 227 us -> 224 us (0.987)
  the two profiles are of different devices: /device:TPU:0 before, /device:TPU:17 now
where the time goes in v4:
time: 224 us; the launch traced here: 223 us
  Pallas kernels  74 us (33%)
  waiting for transfers between devices  70.8 us (32%)
  starting transfers between devices  38.6 us (17%)
  other arithmetic  25.7 us (11%)
  local copies, waits for them, and re-layouts  12.1 us (5%)
    pallas_call x19, Pallas kernels, call(): pl.pallas_call(run, grid_spec=pltpu.PrefetchScalarGridSpec(num_scalar_pre...  74 us
    ppermute x15, waiting for transfers between devices, hop(): return lax.ppermute(block, 'tp', pairs)  32.8 us
    ppermute x15, starting transfers between devices, hop(): return lax.ppermute(block, 'tp', pairs)  23 us
    ppermute x4, waiting for transfers between devices, from_behind(): return lax.ppermute(block, axis, route)  19.8 us
    ppermute x4, waiting for transfers between devices, shifted(): lax.ppermute(block, axis, [((i - distance) % count, i) for i in range(cou...  18.2 us
    unnamed x50, local copies, waits for them, and re-layouts  12.1 us
    ppermute x4, starting transfers between devices, from_behind(): return lax.ppermute(block, axis, route)  9.73 us
    convert_element_type x2, other arithmetic, body(): to_x3 = total_of(jnp.where(end, pb[c], half(m2, c)), zero).astype(bf)  6.34 us
  transfers between devices with their start and end apart: 23, of which 12 were waited for; matrix products, arithmetic and copies ran while one was open for 12% of the time, Pallas kernels for 33%

profile of v4, /device:TPU:17, one launch (start us, length us, event | category | flops | bytes accessed | tf_op | source)
XLA Modules:
  0.0 222.5 jit_solution(402813724635024888)
XLA Ops:
  3.9 4.0 %collective-permute-start = (bf16[512,1024]{1,0:T(8,128)(2,1)}, bf16[512,1024]{1,0:T(8,128)(2,1)S(1)}, u32[]{:S(2)}, u32[]{:S(2)}) collective-permute-start(bf16[512,1024]{1,0:T(8,128)(2,1)} %bitcast.31), channel_id=1, source_target_pairs={{0,4},{4,8},{8,12},{1,5},{5,9},{9,13},{2,6},{6,10},{10,14},{3,7},{... | collective-permute-start | bytes 3145736 | tf_op jit(solution)/shard_map/ppermute | solution.py:404
  11.3 8.6 %collective-permute-done.refs_4_.refs_9_ = bf16[512,1024]{1,0:T(8,128)(2,1)S(1)} collective-permute-done((bf16[512,1024]{1,0:T(8,128)(2,1)}, bf16[512,1024]{1,0:T(8,128)(2,1)S(1)}, u32[]{:S(2)}, u32[]{:S(2)}) %collective-permute-start) | collective-permute-done | bytes 1048608 | tf_op jit(solution)/shard_map/ppermute | solution.py:404
  19.9 11.2 %collective-permute-done.1.refs_5_.refs_10_ = bf16[512,1024]{1,0:T(8,128)(2,1)S(1)} collective-permute-done((bf16[512,1024]{1,0:T(8,128)(2,1)}, bf16[512,1024]{1,0:T(8,128)(2,1)S(1)}, u32[]{:S(2)}, u32[]{:S(2)}) %collective-permute-start.1) | collective-permute-done | bytes 1048608 | tf_op jit(solution)/shard_map/ppermute | solution.py:404
  35.9 16.4 %attend.1 = (bf16[512,1024]{1,0:T(8,128)(2,1)S(1)}, bf16[8,512,512]{2,1,0:T(8,128)(2,1)}, bf16[256,2048]{1,0:T(8,128)(2,1)S(1)}, bf16[256,2048]{1,0:T(8,128)(2,1)S(1)}, f32[1,1]{1,0:T(1,128)}) custom-call(s32[2]{0:T(128)S(1)} %pad_add_fusion.1.index_ref, s32[1,2048]{1,0:T(1,128)S(1)} %copy-done.24, bf16[512,1024]{1,0:T(8,128)(2,1)S(1)} %bitcast.28, ...), custom_call_target="tpu_custom_call" | custom-call | flops 1610612736 | bytes 8388608 | tf_op jit(solution)/shard_map/attend/pallas_call | solution.py:133
  52.8 3.6 %collective-permute-start.5 = (bf16[512,2048]{1,0:T(8,128)(2,1)}, bf16[512,2048]{1,0:T(8,128)(2,1)}, u32[]{:S(2)}, u32[]{:S(2)}) collective-permute-start(bf16[512,2048]{1,0:T(8,128)(2,1)} %get-tuple-element.47.refs_3_), channel_id=1, source_target_pairs={{1,2},{2,1},{5,6},{6,5},{9,10},{10,9},{13,14},{14,13},{17,18},{18,... | collective-permute-start | bytes 6291464 | tf_op jit(solution)/shard_map/middle2/ppermute | solution.py:414
  56.5 2.3 %add_convert_fusion.7.refs_0_.refs_5_ = bf16[256,2048]{1,0:T(8,128)(2,1)S(1)} fusion(bf16[256,2048]{1,0:T(8,128)(2,1)S(1)} %get-tuple-element.44, bf16[512,2048]{1,0:T(8,128)(2,1)} %collective-permute-done.2.refs_3_, f32[]{:T(128)} %bitcast.9, pred[]{:T(512)S(6)} %or.3), kind=kLoop, calls=%fused_computation.8 | loop fusion | flops 2097152 | bytes 3145733 | tf_op jit(solution)/shard_map/convert_element_type | solution.py:443
  59.4 2.3 %add_convert_fusion.6.refs_6_ = bf16[256,2048]{1,0:T(8,128)(2,1)S(1)} fusion(bf16[256,2048]{1,0:T(8,128)(2,1)S(1)} %get-tuple-element.48, bf16[512,2048]{1,0:T(8,128)(2,1)} %collective-permute-done.2.refs_3_, f32[]{:T(128)} %bitcast.11, pred[]{:T(512)S(6)} %or.3), kind=kLoop, calls=%fused_computation.7 | loop fusion | flops 2097152 | bytes 3145733 | tf_op jit(solution)/shard_map/convert_element_type | solution.py:443
  63.2 11.1 %parts.1 = (bf16[256,2048]{1,0:T(8,128)(2,1)S(1)}, bf16[256,2048]{1,0:T(8,128)(2,1)S(1)}, bf16[256,2048]{1,0:T(8,128)(2,1)S(1)}, bf16[256,2048]{1,0:T(8,128)(2,1...) custom-call(s32[3]{0:T(128)S(1)} %pad_add_fusion.3.index_ref, ...), custom_call_target="tpu_custom_call" | custom-call | flops 6442450944 | bytes 12582912 | tf_op jit(solution)/shard_map/parts/pallas_call | solution.py:133
  76.3 9.1 %project.2 = (f32[512,1024]{1,0:T(8,128)S(1)}, f32[1,1]{1,0:T(1,128)}) custom-call(s32[2]{0:T(128)S(1)} %pad_add_fusion.2.index_ref, bf16[1024,8192]{1,0:T(8,128)(2,1)} %bitcast.49, bf16[1024,8192]{1,0:T(8,128)(2,1)} %bitcast.50, bf16[512,2048]{1,0:T(8,128)(2,1)S(1)} %bitcast.44, bf16[512,2048]{1,0:T(8,128)(2,1)} %get-tuple-element.47.refs_3_, ...), custom_call_target="tpu_custom_call" | custom-call | flops 4294967296 | bytes 8388608 | tf_op jit(solution)/shard_map/project/pallas_call | solution.py:133
  86.7 12.9 %collective-permute-done.5 = bf16[512,2048]{1,0:T(8,128)(2,1)} collective-permute-done((bf16[512,2048]{1,0:T(8,128)(2,1)}, bf16[512,2048]{1,0:T(8,128)(2,1)}, u32[]{:S(2)}, u32[]{:S(2)}) %collective-permute-start.5) | collective-permute-done | bytes 2097184 | tf_op jit(solution)/shard_map/middle2/ppermute | solution.py:414
  99.6 2.5 %add_convert_fusion.4 = (bf16[256,2048]{1,0:T(8,128)(2,1)S(1)}, bf16[256,2048]{1,0:T(8,128)(2,1)S(1)}) fusion(bf16[256,2048]{1,0:T(8,128)(2,1)S(1)} %get-tuple-element.49.refs_4_, f32[]{:T(128)} %bitcast.14, pred[]{:T(512)S(6)} %or.3, bf16[512,2048]{1,0:T(8,128)(2,1)} %collective-permute-done.5, bf16[256,2048]{1,0:T(8,128)(2,1)S(1)} %collective-permute-done.3), kind=kLoop, calls=%fused_computation.5 | loop fusion | flops 4718592 | bytes 5242885 | tf_op jit(solution)/shard_map/convert_element_type | solution.py:452
  102.7 2.4 %collective-permute-start.9 = (bf16[256,2048]{1,0:T(8,128)(2,1)S(1)}, bf16[256,2048]{1,0:T(8,128)(2,1)}, u32[]{:S(2)}, u32[]{:S(2)}) collective-permute-start(bf16[256,2048]{1,0:T(8,128)(2,1)S(1)} %get-tuple-element.88.refs_0_), channel_id=1, source_target_pairs={{1,2},{2,1},{5,6},{6,5},{9,10},{10,9},{13,14},{14,13},{17,18},{18,... | collective-permute-start | bytes 3145736 | tf_op jit(solution)/shard_map/middle3a/ppermute | solution.py:414
  105.1 3.8 %add_convert_fusion.2 = (bf16[256,2048]{1,0:T(8,128)(2,1)}, bf16[256,2048]{1,0:T(8,128)(2,1)S(1)}) fusion(bf16[256,2048]{1,0:T(8,128)(2,1)S(1)} %get-tuple-element.51, f32[]{:T(128)} %bitcast.15, pred[]{:T(512)S(6)} %or.3, bf16[512,2048]{1,0:T(8,128)(2,1)} %collective-permute-done.5, bf16[256,2048]{1,0:T(8,128)(2,1)} %collective-permute-done.6), kind=kLoop, calls=%fused_computation.3 | loop fusion | flops 4718592 | bytes 5242885 | tf_op jit(solution)/shard_map/convert_element_type | solution.py:452
  109.7 2.7 %collective-permute-start.11 = (bf16[256,2048]{1,0:T(8,128)(2,1)S(1)}, bf16[256,2048]{1,0:T(8,128)(2,1)S(1)}, u32[]{:S(2)}, u32[]{:S(2)}) collective-permute-start(bf16[256,2048]{1,0:T(8,128)(2,1)S(1)} %get-tuple-element.86.refs_4_), channel_id=1, source_target_pairs={{1,2},{2,1},{5,6},{6,5},{9,10},{10,9},{13,14},{14,13},{17,18},{18,... | collective-permute-start | bytes 3145736 | tf_op jit(solution)/shard_map/middle3b/ppermute | solution.py:414
  114.3 5.6 %project.3 = (f32[512,1024]{1,0:T(8,128)S(1)}, f32[1,1]{1,0:T(1,128)}) custom-call(s32[1]{0:T(128)} %bitcast.3.index_ref, bf16[1024,8192]{1,0:T(8,128)(2,1)} %bitcast.51, bf16[256,2048]{1,0:T(8,128)(2,1)S(1)} %get-tuple-element.84.refs_1_, bf16[256,2048]{1,0:T(8,128)(2,1)S(1)} %get-tuple-element.83.refs_2_, f32[512,1024]{1,0:T(8,128)S(1)} %copy-done.14, ...), custom_call_target="tpu_custom_call" | custom-call | flops 2147483648 | bytes 4194304 | tf_op jit(solution)/shard_map/project/pallas_call | solution.py:133
  119.9 3.8 %place.4 = (bf16[512,2048]{1,0:T(8,128)(2,1)}, f32[1,1]{1,0:T(1,128)}) custom-call(s32[1]{0:T(128)} %bitcast.10.index_ref, bf16[512,2048]{1,0:T(8,128)(2,1)} %collective-permute-done.10.refs_0_, f32[512,1024]{1,0:T(8,128)S(1)} %get-tuple-element.53.refs_1_), custom_call_target="tpu_custom_call" | custom-call | bytes 4194304 | tf_op jit(solution)/shard_map/place/pallas_call | solution.py:133
  123.7 3.7 %collective-permute-done.8.refs_2_ = bf16[256,2048]{1,0:T(8,128)(2,1)S(1)} collective-permute-done((bf16[256,2048]{1,0:T(8,128)(2,1)S(1)}, bf16[256,2048]{1,0:T(8,128)(2,1)S(1)}, u32[]{:S(2)}, u32[]{:S(2)}) %collective-permute-start.8) | collective-permute-done | bytes 1048608 | tf_op jit(solution)/shard_map/outer3a/ppermute | solution.py:414
  129.4 3.8 %collective-permute-start.16 = (bf16[256,2048]{1,0:T(8,128)(2,1)}, bf16[256,2048]{1,0:T(8,128)(2,1)}, u32[]{:S(2)}, u32[]{:S(2)}) collective-permute-start(bf16[256,2048]{1,0:T(8,128)(2,1)} %add_convert_fusion.refs_12_), channel_id=1, source_target_pairs={{1,2},{2,1},{5,6},{6,5},{9,10},{10,9},{13,14},{14,13},{17,18},{18,... | collective-permute-start | bytes 3145736 | tf_op jit(solution)/shard_map/middle4a/ppermute | solution.py:414
  133.2 3.1 %add_convert_fusion.1.refs_11_ = bf16[256,2048]{1,0:T(8,128)(2,1)} fusion(bf16[256,2048]{1,0:T(8,128)(2,1)} %collective-permute-done.9, bf16[256,2048]{1,0:T(8,128)(2,1)S(1)} %copy-done.23, f32[]{:T(128)} %bitcast.16), kind=kLoop, calls=%fused_computation.2 | loop fusion | flops 2621440 | bytes 3145732 | tf_op jit(solution)/shard_map/convert_element_type | solution.py:468
  136.4 9.6 %backward.2 = (bf16[512,1024]{1,0:T(8,128)(2,1)}, bf16[2,256,1024]{2,1,0:T(8,128)(2,1)}, bf16[256,1024]{1,0:T(8,128)(2,1)S(1)}, bf16[256,1024]{1,0:T(8,128)(2,1)...) custom-call(s32[2]{0:T(128)S(1)} %pad_add_fusion.index_ref, ...), custom_call_target="tpu_custom_call" | custom-call | flops 3221225472 | bytes 16777216 | tf_op jit(solution)/shard_map/backward/pallas_call | solution.py:133
  146.0 4.0 %collective-permute-done.7.refs_1_.refs_2_ = bf16[256,2048]{1,0:T(8,128)(2,1)S(1)} collective-permute-done((bf16[256,2048]{1,0:T(8,128)(2,1)}, bf16[256,2048]{1,0:T(8,128)(2,1)S(1)}, u32[]{:S(2)}, u32[]{:S(2)}) %collective-permute-start.7) | collective-permute-done | bytes 1048608 | tf_op jit(solution)/shard_map/outer3b/ppermute | solution.py:414
  150.0 2.4 %collective-permute-done.11.refs_0_ = bf16[256,2048]{1,0:T(8,128)(2,1)S(1)} collective-permute-done((bf16[256,2048]{1,0:T(8,128)(2,1)S(1)}, bf16[256,2048]{1,0:T(8,128)(2,1)S(1)}, u32[]{:S(2)}, u32[]{:S(2)}) %collective-permute-start.11) | collective-permute-done | bytes 1048608 | tf_op jit(solution)/shard_map/middle3b/ppermute | solution.py:414
  157.8 2.4 %collective-permute-start.13 = (bf16[128,2048]{1,0:T(8,128)(2,1)S(1)}, bf16[128,2048]{1,0:T(8,128)(2,1)S(1)}, u32[]{:S(2)}, u32[]{:S(2)}) collective-permute-start(bf16[128,2048]{1,0:T(8,128)(2,1)S(1)} %add_convert_fusion.10.refs_13_), channel_id=1, source_target_pairs={{1,2},{2,1},{5,6},{6,5},{9,10},{10,9},{13,14},{14,13},{17,18},{18,... | collective-permute-start | bytes 1572872 | tf_op jit(solution)/shard_map/middle4b/ppermute | solution.py:414
  160.2 9.8 %backward.3 = (bf16[512,1024]{1,0:T(8,128)(2,1)}, bf16[2,256,1024]{2,1,0:T(8,128)(2,1)S(1)}, bf16[256,1024]{1,0:T(8,128)(2,1)S(1)}, bf16[256,1024]{1,0:T(8,128)(...) custom-call(s32[2]{0:T(128)S(1)} %pad_add_fusion.index_ref, ...), custom_call_target="tpu_custom_call", output_to_operand_aliasing={{0}: (12, {})} | custom-call | flops 3221225472 | bytes 16777216 | tf_op jit(solution)/shard_map/backward/pallas_call | solution.py:133
  170.0 4.8 %collective-permute-done.16 = bf16[256,2048]{1,0:T(8,128)(2,1)} collective-permute-done((bf16[256,2048]{1,0:T(8,128)(2,1)}, bf16[256,2048]{1,0:T(8,128)(2,1)}, u32[]{:S(2)}, u32[]{:S(2)}) %collective-permute-start.16) | collective-permute-done | bytes 1048608 | tf_op jit(solution)/shard_map/middle4a/ppermute | solution.py:414
  174.8 2.4 %subtract_convert_fusion.refs_3_ = bf16[256,2048]{1,0:T(8,128)(2,1)S(1)} fusion(bf16[256,2048]{1,0:T(8,128)(2,1)} %collective-permute-done.16, bf16[256,2048]{1,0:T(8,128)(2,1)S(1)} %collective-permute-done.15, bf16[256,2048]{1,0:T(8,128)(2,1)S(1)} %copy-done.18, f32[]{:T(128)} %bitcast.19), kind=kLoop, calls=%fused_computation | loop fusion | flops 3670016 | bytes 4194308 | tf_op jit(solution)/shard_map/convert_element_type | solution.py:479
  182.0 2.4 %collective-permute-start.20 = (bf16[128,2048]{1,0:T(8,128)(2,1)S(1)}, bf16[128,2048]{1,0:T(8,128)(2,1)S(1)}, u32[]{:S(2)}, u32[]{:S(2)}) collective-permute-start(bf16[128,2048]{1,0:T(8,128)(2,1)S(1)} %add_convert_fusion.8.refs_1_), channel_id=1, source_target_pairs={{1,2},{2,1},{5,6},{6,5},{9,10},{10,9},{13,14},{14,13},{17,18},{18,... | collective-permute-start | bytes 1572872 | tf_op jit(solution)/shard_map/middle4c/ppermute | solution.py:414
  190.3 2.8 %collective-permute-done.19 = bf16[128,2048]{1,0:T(8,128)(2,1)S(1)} collective-permute-done((bf16[128,2048]{1,0:T(8,128)(2,1)S(1)}, bf16[128,2048]{1,0:T(8,128)(2,1)S(1)}, u32[]{:S(2)}, u32[]{:S(2)}) %collective-permute-start.19) | collective-permute-done | bytes 524320 | tf_op jit(solution)/shard_map/outer4c/ppermute | solution.py:414
  193.1 2.1 collective-permute-done.20
  197.4 5.1 %collective-permute-done.18.refs_0_ = bf16[256,2048]{1,0:T(8,128)(2,1)S(1)} collective-permute-done((bf16[256,2048]{1,0:T(8,128)(2,1)S(1)}, bf16[256,2048]{1,0:T(8,128)(2,1)S(1)}, u32[]{:S(2)}, u32[]{:S(2)}) %collective-permute-start.18) | collective-permute-done | bytes 1048608 | tf_op jit(solution)/shard_map/ppermute | solution.py:409
  206.4 7.4 %collective-permute-done.22.refs_0_ = bf16[128,2048]{1,0:T(8,128)(2,1)S(1)} collective-permute-done((bf16[128,2048]{1,0:T(8,128)(2,1)S(1)}, bf16[128,2048]{1,0:T(8,128)(2,1)S(1)}, u32[]{:S(2)}, u32[]{:S(2)}) %collective-permute-start.22) | collective-permute-done | bytes 524320 | tf_op jit(solution)/shard_map/ppermute | solution.py:409
  215.8 5.7 %collective-permute-done.21.refs_0_ = bf16[128,2048]{1,0:T(8,128)(2,1)S(1)} collective-permute-done((bf16[128,2048]{1,0:T(8,128)(2,1)S(1)}, bf16[128,2048]{1,0:T(8,128)(2,1)S(1)}, u32[]{:S(2)}, u32[]{:S(2)}) %collective-permute-start.21) | collective-permute-done | bytes 524320 | tf_op jit(solution)/shard_map/ppermute | solution.py:409
  (101 shorter events, 47.6 us)
Async XLA Ops:
  0.6 51.6 %collective-permute-start.4 = (bf16[512,2048]{1,0:T(8,128)(2,1)}, bf16[512,2048]{1,0:T(8,128)(2,1)}, u32[]{:S(2)}, u32[]{:S(2)}) collective-permute-start(bf16[512,2048]{1,0:T(8,128)(2,1)} %bitcast.41), channel_id=1, source_target_pairs={{0,1},{1,0},{2,3},{3,2},{4,5},{5,4},{6,7},{7,6},{8,9},{9,8},{10,11... | collective-permute-start | bytes 6291464 | tf_op jit(solution)/shard_map/outer1/ppermute | solution.py:414
  2.0 54.5 %collective-permute-start.2 = (bf16[512,2048]{1,0:T(8,128)(2,1)}, bf16[512,2048]{1,0:T(8,128)(2,1)}, u32[]{:S(2)}, u32[]{:S(2)}) collective-permute-start(bf16[512,2048]{1,0:T(8,128)(2,1)} %bitcast.42), channel_id=1, source_target_pairs={{1,2},{2,1},{5,6},{6,5},{9,10},{10,9},{13,14},{14,13},{17,18},{18,... | collective-permute-start | bytes 6291464 | tf_op jit(solution)/shard_map/middle1/ppermute | solution.py:414
  3.9 16.0 %collective-permute-start = (bf16[512,1024]{1,0:T(8,128)(2,1)}, bf16[512,1024]{1,0:T(8,128)(2,1)S(1)}, u32[]{:S(2)}, u32[]{:S(2)}) collective-permute-start(bf16[512,1024]{1,0:T(8,128)(2,1)} %bitcast.31), channel_id=1, source_target_pairs={{0,4},{4,8},{8,12},{1,5},{5,9},{9,13},{2,6},{6,10},{10,14},{3,7},{... | collective-permute-start | bytes 3145736 | tf_op jit(solution)/shard_map/ppermute | solution.py:404
  7.9 23.3 %collective-permute-start.1 = (bf16[512,1024]{1,0:T(8,128)(2,1)}, bf16[512,1024]{1,0:T(8,128)(2,1)S(1)}, u32[]{:S(2)}, u32[]{:S(2)}) collective-permute-start(bf16[512,1024]{1,0:T(8,128)(2,1)} %bitcast.35), channel_id=1, source_target_pairs={{0,4},{4,8},{8,12},{1,5},{5,9},{9,13},{2,6},{6,10},{10,14},{3,7},{... | collective-permute-start | bytes 3145736 | tf_op jit(solution)/shard_map/ppermute | solution.py:404
  9.8 110.0 %collective-permute-start.10 = (bf16[512,2048]{1,0:T(8,128)(2,1)}, bf16[512,2048]{1,0:T(8,128)(2,1)}, u32[]{:S(2)}, u32[]{:S(2)}) collective-permute-start(bf16[512,2048]{1,0:T(8,128)(2,1)} %bitcast.43), channel_id=1, source_target_pairs={{16,0},{0,16},{17,1},{1,17},{18,2},{2,18},{19,3},{3,19},{20,4},{4,... | collective-permute-start | bytes 6291464 | tf_op jit(solution)/shard_map/ppermute | solution.py:409
  19.9 116.4 %copy-start.8 = (bf16[512,1024]{1,0:T(8,128)(2,1)}, bf16[512,1024]{1,0:T(8,128)(2,1)S(1)}, u32[]{:S(2)}) copy-start(bf16[512,1024]{1,0:T(8,128)(2,1)S(1)} %collective-permute-done.refs_4_.refs_9_) | copy-start | bytes 3145732
  31.2 21.1 %copy-start.9 = (bf16[512,1024]{1,0:T(8,128)(2,1)}, bf16[512,1024]{1,0:T(8,128)(2,1)S(1)}, u32[]{:S(2)}) copy-start(bf16[512,1024]{1,0:T(8,128)(2,1)S(1)} %collective-permute-done.1.refs_5_.refs_10_) | copy-start | bytes 3145732
  52.8 46.8 %collective-permute-start.5 = (bf16[512,2048]{1,0:T(8,128)(2,1)}, bf16[512,2048]{1,0:T(8,128)(2,1)}, u32[]{:S(2)}, u32[]{:S(2)}) collective-permute-start(bf16[512,2048]{1,0:T(8,128)(2,1)} %get-tuple-element.47.refs_3_), channel_id=1, source_target_pairs={{1,2},{2,1},{5,6},{6,5},{9,10},{10,9},{13,14},{14,13},{17,18},{18,... | collective-permute-start | bytes 6291464 | tf_op jit(solution)/shard_map/middle2/ppermute | solution.py:414
  59.3 27.3 %collective-permute-start.3 = (bf16[256,2048]{1,0:T(8,128)(2,1)S(1)}, bf16[256,2048]{1,0:T(8,128)(2,1)S(1)}, u32[]{:S(2)}, u32[]{:S(2)}) collective-permute-start(bf16[256,2048]{1,0:T(8,128)(2,1)S(1)} %add_convert_fusion.7.refs_0_.refs_5_), channel_id=1, source_target_pairs={{0,1},{1,0},{2,3},{3,2},{4,5},{5,4},{6,7},{7,6},{8,9},{9,8},{10,11... | collective-permute-start | bytes 3145736 | tf_op jit(solution)/shard_map/outer2a/ppermute | solution.py:414
  61.7 43.4 %collective-permute-start.6 = (bf16[256,2048]{1,0:T(8,128)(2,1)S(1)}, bf16[256,2048]{1,0:T(8,128)(2,1)}, u32[]{:S(2)}, u32[]{:S(2)}) collective-permute-start(bf16[256,2048]{1,0:T(8,128)(2,1)S(1)} %add_convert_fusion.6.refs_6_), channel_id=1, source_target_pairs={{0,1},{1,0},{2,3},{3,2},{4,5},{5,4},{6,7},{7,6},{8,9},{9,8},{10,11... | collective-permute-start | bytes 3145736 | tf_op jit(solution)/shard_map/outer2b/ppermute | solution.py:414
  63.2 13.1 %copy-start.12 = (bf16[1,512,2048]{2,1,0:T(8,128)(2,1)S(1)}, bf16[1,512,2048]{2,1,0:T(8,128)(2,1)}, u32[]{:S(2)}) copy-start(bf16[1,512,2048]{2,1,0:T(8,128)(2,1)} %param.11) | copy-start | bytes 6291460
  76.3 9.1 %copy-start.19 = (bf16[256,2048]{1,0:T(8,128)(2,1)}, bf16[256,2048]{1,0:T(8,128)(2,1)S(1)}, u32[]{:S(2)}) copy-start(bf16[256,2048]{1,0:T(8,128)(2,1)S(1)} %get-tuple-element.58) | copy-start | bytes 3145732
  76.3 9.1 %copy-start.22 = (bf16[256,2048]{1,0:T(8,128)(2,1)}, bf16[256,2048]{1,0:T(8,128)(2,1)S(1)}, u32[]{:S(2)}) copy-start(bf16[256,2048]{1,0:T(8,128)(2,1)S(1)} %get-tuple-element.55) | copy-start | bytes 3145732
  102.1 25.3 %collective-permute-start.8 = (bf16[256,2048]{1,0:T(8,128)(2,1)S(1)}, bf16[256,2048]{1,0:T(8,128)(2,1)S(1)}, u32[]{:S(2)}, u32[]{:S(2)}) collective-permute-start(bf16[256,2048]{1,0:T(8,128)(2,1)S(1)} %get-tuple-element.87.refs_1_), channel_id=1, source_target_pairs={{0,1},{1,0},{2,3},{3,2},{4,5},{5,4},{6,7},{7,6},{8,9},{9,8},{10,11... | collective-permute-start | bytes 3145736 | tf_op jit(solution)/shard_map/outer3a/ppermute | solution.py:414
  102.7 30.5 %collective-permute-start.9 = (bf16[256,2048]{1,0:T(8,128)(2,1)S(1)}, bf16[256,2048]{1,0:T(8,128)(2,1)}, u32[]{:S(2)}, u32[]{:S(2)}) collective-permute-start(bf16[256,2048]{1,0:T(8,128)(2,1)S(1)} %get-tuple-element.88.refs_0_), channel_id=1, source_target_pairs={{1,2},{2,1},{5,6},{6,5},{9,10},{10,9},{13,14},{14,13},{17,18},{18,... | collective-permute-start | bytes 3145736 | tf_op jit(solution)/shard_map/middle3a/ppermute | solution.py:414
  108.9 41.0 %collective-permute-start.7 = (bf16[256,2048]{1,0:T(8,128)(2,1)}, bf16[256,2048]{1,0:T(8,128)(2,1)S(1)}, u32[]{:S(2)}, u32[]{:S(2)}) collective-permute-start(bf16[256,2048]{1,0:T(8,128)(2,1)} %get-tuple-element.85.refs_5_), channel_id=1, source_target_pairs={{0,1},{1,0},{2,3},{3,2},{4,5},{5,4},{6,7},{7,6},{8,9},{9,8},{10,11... | collective-permute-start | bytes 3145736 | tf_op jit(solution)/shard_map/outer3b/ppermute | solution.py:414
  109.7 42.8 %collective-permute-start.11 = (bf16[256,2048]{1,0:T(8,128)(2,1)S(1)}, bf16[256,2048]{1,0:T(8,128)(2,1)S(1)}, u32[]{:S(2)}, u32[]{:S(2)}) collective-permute-start(bf16[256,2048]{1,0:T(8,128)(2,1)S(1)} %get-tuple-element.86.refs_4_), channel_id=1, source_target_pairs={{1,2},{2,1},{5,6},{6,5},{9,10},{10,9},{13,14},{14,13},{17,18},{18,... | collective-permute-start | bytes 3145736 | tf_op jit(solution)/shard_map/middle3b/ppermute | solution.py:414
  123.7 9.5 %copy-start.23 = (bf16[256,2048]{1,0:T(8,128)(2,1)S(1)}, bf16[256,2048]{1,0:T(8,128)(2,1)}, u32[]{:S(2)}) copy-start(bf16[256,2048]{1,0:T(8,128)(2,1)} %copy-done.22) | copy-start | bytes 3145732
  129.4 7.0 %copy-start.7 = (bf16[1,512,1024]{2,1,0:T(8,128)(2,1)S(1)}, bf16[1,512,1024]{2,1,0:T(8,128)(2,1)}, u32[]{:S(2)}) copy-start(bf16[1,512,1024]{2,1,0:T(8,128)(2,1)} %param.9) | copy-start | bytes 3145732
  129.4 45.4 %collective-permute-start.16 = (bf16[256,2048]{1,0:T(8,128)(2,1)}, bf16[256,2048]{1,0:T(8,128)(2,1)}, u32[]{:S(2)}, u32[]{:S(2)}) collective-permute-start(bf16[256,2048]{1,0:T(8,128)(2,1)} %add_convert_fusion.refs_12_), channel_id=1, source_target_pairs={{1,2},{2,1},{5,6},{6,5},{9,10},{10,9},{13,14},{14,13},{17,18},{18,... | collective-permute-start | bytes 3145736 | tf_op jit(solution)/shard_map/middle4a/ppermute | solution.py:414
  136.4 38.4 %collective-permute-start.15 = (bf16[256,2048]{1,0:T(8,128)(2,1)}, bf16[256,2048]{1,0:T(8,128)(2,1)S(1)}, u32[]{:S(2)}, u32[]{:S(2)}) collective-permute-start(bf16[256,2048]{1,0:T(8,128)(2,1)} %add_convert_fusion.1.refs_11_), channel_id=1, source_target_pairs={{0,1},{1,0},{2,3},{3,2},{4,5},{5,4},{6,7},{7,6},{8,9},{9,8},{10,11... | collective-permute-start | bytes 3145736 | tf_op jit(solution)/shard_map/outer4a/ppermute | solution.py:414
  136.4 17.8 %copy-start.20 = (bf16[256,2048]{1,0:T(8,128)(2,1)S(1)}, bf16[256,2048]{1,0:T(8,128)(2,1)}, u32[]{:S(2)}) copy-start(bf16[256,2048]{1,0:T(8,128)(2,1)} %copy-done.19) | copy-start | bytes 3145732
  155.0 29.4 %collective-permute-start.12 = (bf16[128,2048]{1,0:T(8,128)(2,1)S(1)}, bf16[128,2048]{1,0:T(8,128)(2,1)S(1)}, u32[]{:S(2)}, u32[]{:S(2)}) collective-permute-start(bf16[128,2048]{1,0:T(8,128)(2,1)S(1)} %add_convert_fusion.11.refs_12_), channel_id=1, source_target_pairs={{0,1},{1,0},{2,3},{3,2},{4,5},{5,4},{6,7},{7,6},{8,9},{9,8},{10,11... | collective-permute-start | bytes 1572872 | tf_op jit(solution)/shard_map/outer4b/ppermute | solution.py:414
  155.1 23.4 %collective-permute-start.14 = (bf16[2,256,1024]{2,1,0:T(8,128)(2,1)}, bf16[2,256,1024]{2,1,0:T(8,128)(2,1)S(1)}, u32[]{:S(2)}, u32[]{:S(2)}) collective-permute-start(bf16[2,256,1024]{2,1,0:T(8,128)(2,1)} %get-tuple-element.70), channel_id=1, source_target_pairs={{4,0},{8,4},{12,8},{5,1},{9,5},{13,9},{6,2},{10,6},{14,10},{7,3},{... | collective-permute-start | bytes 3145736 | tf_op jit(solution)/shard_map/ppermute | solution.py:404
  157.8 26.6 %collective-permute-start.13 = (bf16[128,2048]{1,0:T(8,128)(2,1)S(1)}, bf16[128,2048]{1,0:T(8,128)(2,1)S(1)}, u32[]{:S(2)}, u32[]{:S(2)}) collective-permute-start(bf16[128,2048]{1,0:T(8,128)(2,1)S(1)} %add_convert_fusion.10.refs_13_), channel_id=1, source_target_pairs={{1,2},{2,1},{5,6},{6,5},{9,10},{10,9},{13,14},{14,13},{17,18},{18,... | collective-permute-start | bytes 1572872 | tf_op jit(solution)/shard_map/middle4b/ppermute | solution.py:414
  160.2 14.6 %copy-start.18 = (bf16[256,2048]{1,0:T(8,128)(2,1)S(1)}, bf16[256,2048]{1,0:T(8,128)(2,1)}, u32[]{:S(2)}) copy-start(bf16[256,2048]{1,0:T(8,128)(2,1)} %copy-done.17) | copy-start | bytes 3145732
  177.2 25.3 %collective-permute-start.18 = (bf16[256,2048]{1,0:T(8,128)(2,1)S(1)}, bf16[256,2048]{1,0:T(8,128)(2,1)S(1)}, u32[]{:S(2)}, u32[]{:S(2)}) collective-permute-start(bf16[256,2048]{1,0:T(8,128)(2,1)S(1)} %subtract_convert_fusion.refs_3_), channel_id=1, source_target_pairs={{16,0},{0,16},{17,1},{1,17},{18,2},{2,18},{19,3},{3,19},{20,4},{4,... | collective-permute-start | bytes 3145736 | tf_op jit(solution)/shard_map/ppermute | solution.py:409
  180.6 12.5 %collective-permute-start.19 = (bf16[128,2048]{1,0:T(8,128)(2,1)S(1)}, bf16[128,2048]{1,0:T(8,128)(2,1)S(1)}, u32[]{:S(2)}, u32[]{:S(2)}) collective-permute-start(bf16[128,2048]{1,0:T(8,128)(2,1)S(1)} %add_convert_fusion.9.refs_0_), channel_id=1, source_target_pairs={{0,1},{1,0},{2,3},{3,2},{4,5},{5,4},{6,7},{7,6},{8,9},{9,8},{10,11... | collective-permute-start | bytes 1572872 | tf_op jit(solution)/shard_map/outer4c/ppermute | solution.py:414
  182.0 13.2 %collective-permute-start.20 = (bf16[128,2048]{1,0:T(8,128)(2,1)S(1)}, bf16[128,2048]{1,0:T(8,128)(2,1)S(1)}, u32[]{:S(2)}, u32[]{:S(2)}) collective-permute-start(bf16[128,2048]{1,0:T(8,128)(2,1)S(1)} %add_convert_fusion.8.refs_1_), channel_id=1, source_target_pairs={{1,2},{2,1},{5,6},{6,5},{9,10},{10,9},{13,14},{14,13},{17,18},{18,... | collective-permute-start | bytes 1572872 | tf_op jit(solution)/shard_map/middle4c/ppermute | solution.py:414
  185.9 17.7 %collective-permute-start.17 = (bf16[2,256,1024]{2,1,0:T(8,128)(2,1)S(1)}, bf16[2,256,1024]{2,1,0:T(8,128)(2,1)S(1)}, u32[]{:S(2)}, u32[]{:S(2)}) collective-permute-start(bf16[2,256,1024]{2,1,0:T(8,128)(2,1)S(1)} %get-tuple-element.74), channel_id=1, source_target_pairs={{4,0},{8,4},{12,8},{5,1},{9,5},{13,9},{6,2},{10,6},{14,10},{7,3},{... | collective-permute-start | bytes 3145736 | tf_op jit(solution)/shard_map/ppermute | solution.py:404
  188.3 25.4 %collective-permute-start.22 = (bf16[128,2048]{1,0:T(8,128)(2,1)S(1)}, bf16[128,2048]{1,0:T(8,128)(2,1)S(1)}, u32[]{:S(2)}, u32[]{:S(2)}) collective-permute-start(bf16[128,2048]{1,0:T(8,128)(2,1)S(1)} %subtract_convert_fusion.2.refs_1_.refs_0_), channel_id=1, source_target_pairs={{16,0},{0,16},{17,1},{1,17},{18,2},{2,18},{19,3},{3,19},{20,4},{4,... | collective-permute-start | bytes 1572872 | tf_op jit(solution)/shard_map/ppermute | solution.py:409
  196.1 25.4 %collective-permute-start.21 = (bf16[128,2048]{1,0:T(8,128)(2,1)S(1)}, bf16[128,2048]{1,0:T(8,128)(2,1)S(1)}, u32[]{:S(2)}, u32[]{:S(2)}) collective-permute-start(bf16[128,2048]{1,0:T(8,128)(2,1)S(1)} %subtract_convert_fusion.1.refs_1_), channel_id=1, source_target_pairs={{16,0},{0,16},{17,1},{1,17},{18,2},{2,18},{19,3},{3,19},{20,4},{4,... | collective-permute-start | bytes 1572872 | tf_op jit(solution)/shard_map/ppermute | solution.py:409
  (16 other events, 41.6 us)

commit v5 on v4

--- a/solution.py
+++ b/solution.py
@@ -13,7 +13,7 @@
 HALF = 256
 PIECES = [(0, 256), (256, 128), (384, 128)]
 PAIR = 4
-VMEM_LIMIT = 44 * 1024 * 1024
+VMEM_LIMIT = 42 * 1024 * 1024
 COST = 1.0
 
 OUTER = [(0, 1), (1, 0), (2, 3), (3, 2)]

time: 224 us -> 223 us (level)
  the two profiles are of different devices: /device:TPU:17 before, /device:TPU:0 now
where the time goes in v5:
time: 223 us; the launch traced here: 218 us
  Pallas kernels  73.4 us (33%)
  starting transfers between devices  54.4 us (24%)
  waiting for transfers between devices  53.9 us (24%)
  other arithmetic  21.4 us (10%)
  local copies, waits for them, and re-layouts  13.8 us (6%)
    pallas_call x19, Pallas kernels, call(): pl.pallas_call(run, grid_spec=pltpu.PrefetchScalarGridSpec(num_scalar_pre...  73.4 us
    ppermute x15, starting transfers between devices, hop(): return lax.ppermute(block, 'tp', pairs)  40.1 us
    ppermute x15, waiting for transfers between devices, hop(): return lax.ppermute(block, 'tp', pairs)  37.4 us
    ppermute x4, waiting for transfers between devices, shifted(): lax.ppermute(block, axis, [((i - distance) % count, i) for i in range(cou...  15.9 us
    unnamed x52, local copies, waits for them, and re-layouts  13.8 us
    ppermute x4, starting transfers between devices, from_behind(): return lax.ppermute(block, axis, route)  8.05 us
    ppermute x4, starting transfers between devices, shifted(): lax.ppermute(block, axis, [((i - distance) % count, i) for i in range(cou...  6.34 us
    convert_element_type x2, other arithmetic, body(): to_x3 = total_of(jnp.where(end, pb[c], half(m2, c)), zero).astype(bf)  5.47 us
  transfers between devices with their start and end apart: 23, of which 9 were waited for; matrix products, arithmetic and copies ran while one was open for 10% of the time, Pallas kernels for 33%

profile of v5, /device:TPU:0, one launch (start us, length us, event | category | flops | bytes accessed | tf_op | source)
XLA Modules:
  0.0 218.2 jit_solution(13808081936134759891)
XLA Ops:
  0.6 3.1 %collective-permute-start.4 = (bf16[512,2048]{1,0:T(8,128)(2,1)}, bf16[512,2048]{1,0:T(8,128)(2,1)}, u32[]{:S(2)}, u32[]{:S(2)}) collective-permute-start(bf16[512,2048]{1,0:T(8,128)(2,1)} %bitcast.42), channel_id=1, source_target_pairs={{0,1},{1,0},{2,3},{3,2},{4,5},{5,4},{6,7},{7,6},{8,9},{9,8},{10,11... | collective-permute-start | bytes 6291464 | tf_op jit(solution)/shard_map/outer1/ppermute | solution.py:414
  3.7 2.0 collective-permute-start.2
  7.3 4.0 %collective-permute-start.1 = (bf16[512,1024]{1,0:T(8,128)(2,1)}, bf16[512,1024]{1,0:T(8,128)(2,1)S(1)}, u32[]{:S(2)}, u32[]{:S(2)}) collective-permute-start(bf16[512,1024]{1,0:T(8,128)(2,1)} %bitcast.35), channel_id=1, source_target_pairs={{0,4},{4,8},{8,12},{1,5},{5,9},{9,13},{2,6},{6,10},{10,14},{3,7},{... | collective-permute-start | bytes 3145736 | tf_op jit(solution)/shard_map/ppermute | solution.py:404
  18.4 16.4 %attend.1 = (bf16[512,1024]{1,0:T(8,128)(2,1)S(1)}, bf16[8,512,512]{2,1,0:T(8,128)(2,1)}, bf16[256,2048]{1,0:T(8,128)(2,1)S(1)}, bf16[256,2048]{1,0:T(8,128)(2,1)S(1)}, f32[1,1]{1,0:T(1,128)}) custom-call(s32[2]{0:T(128)S(1)} %pad_add_fusion.1.index_ref, s32[1,2048]{1,0:T(1,128)S(1)} %copy-done.23, bf16[512,1024]{1,0:T(8,128)(2,1)S(1)} %bitcast.28, ...), custom_call_target="tpu_custom_call" | custom-call | flops 1610612736 | bytes 8388608 | tf_op jit(solution)/shard_map/attend/pallas_call | solution.py:133
  34.8 14.9 %collective-permute-done.4.refs_0_ = bf16[512,2048]{1,0:T(8,128)(2,1)} collective-permute-done((bf16[512,2048]{1,0:T(8,128)(2,1)}, bf16[512,2048]{1,0:T(8,128)(2,1)}, u32[]{:S(2)}, u32[]{:S(2)}) %collective-permute-start.4) | collective-permute-done | bytes 2097184 | tf_op jit(solution)/shard_map/outer1/ppermute | solution.py:414
  50.2 2.1 collective-permute-start.5
  52.4 2.3 %add_convert_fusion.7.refs_0_.refs_5_ = bf16[256,2048]{1,0:T(8,128)(2,1)S(1)} fusion(bf16[256,2048]{1,0:T(8,128)(2,1)S(1)} %get-tuple-element.44, bf16[512,2048]{1,0:T(8,128)(2,1)} %collective-permute-done.2.refs_3_, f32[]{:T(128)} %bitcast.9, pred[]{:T(512)S(6)} %or.3), kind=kLoop, calls=%fused_computation.8 | loop fusion | flops 2097152 | bytes 3145733 | tf_op jit(solution)/shard_map/convert_element_type | solution.py:443
  55.2 3.2 %collective-permute-start.3 = (bf16[256,2048]{1,0:T(8,128)(2,1)S(1)}, bf16[256,2048]{1,0:T(8,128)(2,1)S(1)}, u32[]{:S(2)}, u32[]{:S(2)}) collective-permute-start(bf16[256,2048]{1,0:T(8,128)(2,1)S(1)} %add_convert_fusion.7.refs_0_.refs_5_), channel_id=1, source_target_pairs={{0,1},{1,0},{2,3},{3,2},{4,5},{5,4},{6,7},{7,6},{8,9},{9,8},{10,11... | collective-permute-start | bytes 3145736 | tf_op jit(solution)/shard_map/outer2a/ppermute | solution.py:414
  58.4 2.2 %add_convert_fusion.6.refs_6_ = bf16[256,2048]{1,0:T(8,128)(2,1)S(1)} fusion(bf16[256,2048]{1,0:T(8,128)(2,1)S(1)} %get-tuple-element.48, bf16[512,2048]{1,0:T(8,128)(2,1)} %collective-permute-done.2.refs_3_, f32[]{:T(128)} %bitcast.11, pred[]{:T(512)S(6)} %or.3), kind=kLoop, calls=%fused_computation.7 | loop fusion | flops 2097152 | bytes 3145733 | tf_op jit(solution)/shard_map/convert_element_type | solution.py:443
  60.7 11.0 %parts.1 = (bf16[256,2048]{1,0:T(8,128)(2,1)S(1)}, bf16[256,2048]{1,0:T(8,128)(2,1)S(1)}, bf16[256,2048]{1,0:T(8,128)(2,1)S(1)}, bf16[256,2048]{1,0:T(8,128)(2,1...) custom-call(s32[3]{0:T(128)S(1)} %pad_add_fusion.3.index_ref, ...), custom_call_target="tpu_custom_call" | custom-call | flops 6442450944 | bytes 12582912 | tf_op jit(solution)/shard_map/parts/pallas_call | solution.py:133
  74.7 2.0 copy-done.13
  76.7 9.0 %project.2 = (f32[512,1024]{1,0:T(8,128)S(1)}, f32[1,1]{1,0:T(1,128)}) custom-call(s32[2]{0:T(128)S(1)} %pad_add_fusion.2.index_ref, bf16[1024,8192]{1,0:T(8,128)(2,1)} %bitcast.50, bf16[1024,8192]{1,0:T(8,128)(2,1)} %bitcast.51, bf16[512,2048]{1,0:T(8,128)(2,1)S(1)} %bitcast.45, bf16[512,2048]{1,0:T(8,128)(2,1)} %get-tuple-element.47.refs_3_, ...), custom_call_target="tpu_custom_call" | custom-call | flops 4294967296 | bytes 8388608 | tf_op jit(solution)/shard_map/project/pallas_call | solution.py:133
  85.7 2.7 %add_convert_fusion.4 = (bf16[256,2048]{1,0:T(8,128)(2,1)S(1)}, bf16[256,2048]{1,0:T(8,128)(2,1)S(1)}) fusion(bf16[256,2048]{1,0:T(8,128)(2,1)S(1)} %get-tuple-element.49.refs_4_, f32[]{:T(128)} %bitcast.14, pred[]{:T(512)S(6)} %or.3, bf16[512,2048]{1,0:T(8,128)(2,1)} %collective-permute-done.5, bf16[256,2048]{1,0:T(8,128)(2,1)S(1)} %collective-permute-done.3), kind=kLoop, calls=%fused_computation.5 | loop fusion | flops 4718592 | bytes 5242885 | tf_op jit(solution)/shard_map/convert_element_type | solution.py:452
  88.4 12.9 %collective-permute-start.8 = (bf16[256,2048]{1,0:T(8,128)(2,1)S(1)}, bf16[256,2048]{1,0:T(8,128)(2,1)S(1)}, u32[]{:S(2)}, u32[]{:S(2)}) collective-permute-start(bf16[256,2048]{1,0:T(8,128)(2,1)S(1)} %get-tuple-element.87.refs_1_), channel_id=1, source_target_pairs={{0,1},{1,0},{2,3},{3,2},{4,5},{5,4},{6,7},{7,6},{8,9},{9,8},{10,11... | collective-permute-start | bytes 3145736 | tf_op jit(solution)/shard_map/outer3a/ppermute | solution.py:414
  102.7 2.8 %add_convert_fusion.2 = (bf16[256,2048]{1,0:T(8,128)(2,1)S(1)}, bf16[256,2048]{1,0:T(8,128)(2,1)S(1)}) fusion(bf16[256,2048]{1,0:T(8,128)(2,1)S(1)} %get-tuple-element.51, f32[]{:T(128)} %bitcast.15, pred[]{:T(512)S(6)} %or.3, bf16[512,2048]{1,0:T(8,128)(2,1)} %collective-permute-done.5, bf16[256,2048]{1,0:T(8,128)(2,1)S(1)} %collective-permute-done.6), kind=kLoop, calls=%fused_computation.3 | loop fusion | flops 4718592 | bytes 5242885 | tf_op jit(solution)/shard_map/convert_element_type | solution.py:452
  105.4 3.7 %collective-permute-start.7 = (bf16[256,2048]{1,0:T(8,128)(2,1)S(1)}, bf16[256,2048]{1,0:T(8,128)(2,1)S(1)}, u32[]{:S(2)}, u32[]{:S(2)}) collective-permute-start(bf16[256,2048]{1,0:T(8,128)(2,1)S(1)} %get-tuple-element.85.refs_5_), channel_id=1, source_target_pairs={{0,1},{1,0},{2,3},{3,2},{4,5},{5,4},{6,7},{7,6},{8,9},{9,8},{10,11... | collective-permute-start | bytes 3145736 | tf_op jit(solution)/shard_map/outer3b/ppermute | solution.py:414
  109.9 2.0 broadcast_select_fusion
  111.9 5.6 %project.3 = (f32[512,1024]{1,0:T(8,128)S(1)}, f32[1,1]{1,0:T(1,128)}) custom-call(s32[1]{0:T(128)} %bitcast.3.index_ref, bf16[1024,8192]{1,0:T(8,128)(2,1)} %bitcast.52, bf16[256,2048]{1,0:T(8,128)(2,1)S(1)} %get-tuple-element.84.refs_1_, bf16[256,2048]{1,0:T(8,128)(2,1)S(1)} %get-tuple-element.83.refs_2_, f32[512,1024]{1,0:T(8,128)S(1)} %get-tuple-element.50.refs_3_, ...), custom_call_target="tpu_custom_call" | custom-call | flops 2147483648 | bytes 4194304 | tf_op jit(solution)/shard_map/project/pallas_call | solution.py:133
  117.5 3.8 %place.4 = (bf16[512,2048]{1,0:T(8,128)(2,1)}, f32[1,1]{1,0:T(1,128)}) custom-call(s32[1]{0:T(128)} %bitcast.10.index_ref, bf16[512,2048]{1,0:T(8,128)(2,1)} %collective-permute-done.10.refs_0_, f32[512,1024]{1,0:T(8,128)S(1)} %get-tuple-element.53.refs_1_), custom_call_target="tpu_custom_call" | custom-call | bytes 4194304 | tf_op jit(solution)/shard_map/place/pallas_call | solution.py:133
  121.3 4.1 %collective-permute-done.8.refs_2_ = bf16[256,2048]{1,0:T(8,128)(2,1)S(1)} collective-permute-done((bf16[256,2048]{1,0:T(8,128)(2,1)S(1)}, bf16[256,2048]{1,0:T(8,128)(2,1)S(1)}, u32[]{:S(2)}, u32[]{:S(2)}) %collective-permute-start.8) | collective-permute-done | bytes 1048608 | tf_op jit(solution)/shard_map/outer3a/ppermute | solution.py:414
  125.5 2.0 add_convert_fusion.refs_12_
  129.6 4.0 %collective-permute-start.15 = (bf16[256,2048]{1,0:T(8,128)(2,1)S(1)}, bf16[256,2048]{1,0:T(8,128)(2,1)S(1)}, u32[]{:S(2)}, u32[]{:S(2)}) collective-permute-start(bf16[256,2048]{1,0:T(8,128)(2,1)S(1)} %add_convert_fusion.1.refs_11_), channel_id=1, source_target_pairs={{0,1},{1,0},{2,3},{3,2},{4,5},{5,4},{6,7},{7,6},{8,9},{9,8},{10,11... | collective-permute-start | bytes 3145736 | tf_op jit(solution)/shard_map/outer4a/ppermute | solution.py:414
  133.6 9.4 %backward.2 = (bf16[512,1024]{1,0:T(8,128)(2,1)}, bf16[2,256,1024]{2,1,0:T(8,128)(2,1)S(1)}, bf16[256,1024]{1,0:T(8,128)(2,1)S(1)}, bf16[256,1024]{1,0:T(8,128)(...) custom-call(s32[2]{0:T(128)S(1)} %pad_add_fusion.index_ref, ...), custom_call_target="tpu_custom_call" | custom-call | flops 3221225472 | bytes 16777216 | tf_op jit(solution)/shard_map/backward/pallas_call | solution.py:133
  143.0 5.0 %collective-permute-done.7.refs_1_.refs_2_ = bf16[256,2048]{1,0:T(8,128)(2,1)S(1)} collective-permute-done((bf16[256,2048]{1,0:T(8,128)(2,1)S(1)}, bf16[256,2048]{1,0:T(8,128)(2,1)S(1)}, u32[]{:S(2)}, u32[]{:S(2)}) %collective-permute-start.7) | collective-permute-done | bytes 1048608 | tf_op jit(solution)/shard_map/outer3b/ppermute | solution.py:414
  150.5 2.4 %collective-permute-start.12 = (bf16[128,2048]{1,0:T(8,128)(2,1)S(1)}, bf16[128,2048]{1,0:T(8,128)(2,1)S(1)}, u32[]{:S(2)}, u32[]{:S(2)}) collective-permute-start(bf16[128,2048]{1,0:T(8,128)(2,1)S(1)} %add_convert_fusion.11.refs_12_), channel_id=1, source_target_pairs={{0,1},{1,0},{2,3},{3,2},{4,5},{5,4},{6,7},{7,6},{8,9},{9,8},{10,11... | collective-permute-start | bytes 1572872 | tf_op jit(solution)/shard_map/outer4b/ppermute | solution.py:414
  155.7 9.5 %backward.3 = (bf16[512,1024]{1,0:T(8,128)(2,1)}, bf16[2,256,1024]{2,1,0:T(8,128)(2,1)S(1)}, bf16[256,1024]{1,0:T(8,128)(2,1)S(1)}, bf16[256,1024]{1,0:T(8,128)(...) custom-call(s32[2]{0:T(128)S(1)} %pad_add_fusion.index_ref, ...), custom_call_target="tpu_custom_call", output_to_operand_aliasing={{0}: (12, {})} | custom-call | flops 3221225472 | bytes 16777216 | tf_op jit(solution)/shard_map/backward/pallas_call | solution.py:133
  165.2 5.2 %collective-permute-done.15 = bf16[256,2048]{1,0:T(8,128)(2,1)S(1)} collective-permute-done((bf16[256,2048]{1,0:T(8,128)(2,1)S(1)}, bf16[256,2048]{1,0:T(8,128)(2,1)S(1)}, u32[]{:S(2)}, u32[]{:S(2)}) %collective-permute-start.15) | collective-permute-done | bytes 1048608 | tf_op jit(solution)/shard_map/outer4a/ppermute | solution.py:414
  175.3 2.5 %collective-permute-start.19 = (bf16[128,2048]{1,0:T(8,128)(2,1)S(1)}, bf16[128,2048]{1,0:T(8,128)(2,1)S(1)}, u32[]{:S(2)}, u32[]{:S(2)}) collective-permute-start(bf16[128,2048]{1,0:T(8,128)(2,1)S(1)} %add_convert_fusion.9.refs_0_), channel_id=1, source_target_pairs={{0,1},{1,0},{2,3},{3,2},{4,5},{5,4},{6,7},{7,6},{8,9},{9,8},{10,11... | collective-permute-start | bytes 1572872 | tf_op jit(solution)/shard_map/outer4c/ppermute | solution.py:414
  179.8 1.8 collective-permute-done.12
  186.5 6.4 %collective-permute-done.19 = bf16[128,2048]{1,0:T(8,128)(2,1)S(1)} collective-permute-done((bf16[128,2048]{1,0:T(8,128)(2,1)S(1)}, bf16[128,2048]{1,0:T(8,128)(2,1)S(1)}, u32[]{:S(2)}, u32[]{:S(2)}) %collective-permute-start.19) | collective-permute-done | bytes 524320 | tf_op jit(solution)/shard_map/outer4c/ppermute | solution.py:414
  199.2 6.7 %collective-permute-done.22.refs_0_ = bf16[128,2048]{1,0:T(8,128)(2,1)S(1)} collective-permute-done((bf16[128,2048]{1,0:T(8,128)(2,1)S(1)}, bf16[128,2048]{1,0:T(8,128)(2,1)S(1)}, u32[]{:S(2)}, u32[]{:S(2)}) %collective-permute-start.22) | collective-permute-done | bytes 524320 | tf_op jit(solution)/shard_map/ppermute | solution.py:409
  208.0 9.2 %collective-permute-done.21.refs_0_ = bf16[128,2048]{1,0:T(8,128)(2,1)S(1)} collective-permute-done((bf16[128,2048]{1,0:T(8,128)(2,1)S(1)}, bf16[128,2048]{1,0:T(8,128)(2,1)S(1)}, u32[]{:S(2)}, u32[]{:S(2)}) %collective-permute-start.21) | collective-permute-done | bytes 524320 | tf_op jit(solution)/shard_map/ppermute | solution.py:409
  (103 shorter events, 43.0 us)
Async XLA Ops:
  0.6 49.0 %collective-permute-start.4 = (bf16[512,2048]{1,0:T(8,128)(2,1)}, bf16[512,2048]{1,0:T(8,128)(2,1)}, u32[]{:S(2)}, u32[]{:S(2)}) collective-permute-start(bf16[512,2048]{1,0:T(8,128)(2,1)} %bitcast.42), channel_id=1, source_target_pairs={{0,1},{1,0},{2,3},{3,2},{4,5},{5,4},{6,7},{7,6},{8,9},{9,8},{10,11... | collective-permute-start | bytes 6291464 | tf_op jit(solution)/shard_map/outer1/ppermute | solution.py:414
  3.7 48.6 %collective-permute-start.2 = (bf16[512,2048]{1,0:T(8,128)(2,1)}, bf16[512,2048]{1,0:T(8,128)(2,1)}, u32[]{:S(2)}, u32[]{:S(2)}) collective-permute-start(bf16[512,2048]{1,0:T(8,128)(2,1)} %bitcast.43), channel_id=1, source_target_pairs={{1,2},{2,1},{5,6},{6,5},{9,10},{10,9},{13,14},{14,13},{17,18},{18,... | collective-permute-start | bytes 6291464 | tf_op jit(solution)/shard_map/middle1/ppermute | solution.py:414
  5.7 7.3 %collective-permute-start = (bf16[512,1024]{1,0:T(8,128)(2,1)}, bf16[512,1024]{1,0:T(8,128)(2,1)S(1)}, u32[]{:S(2)}, u32[]{:S(2)}) collective-permute-start(bf16[512,1024]{1,0:T(8,128)(2,1)} %bitcast.31), channel_id=1, source_target_pairs={{0,4},{4,8},{8,12},{1,5},{5,9},{9,13},{2,6},{6,10},{10,14},{3,7},{... | collective-permute-start | bytes 3145736 | tf_op jit(solution)/shard_map/ppermute | solution.py:404
  7.3 6.4 %collective-permute-start.1 = (bf16[512,1024]{1,0:T(8,128)(2,1)}, bf16[512,1024]{1,0:T(8,128)(2,1)S(1)}, u32[]{:S(2)}, u32[]{:S(2)}) collective-permute-start(bf16[512,1024]{1,0:T(8,128)(2,1)} %bitcast.35), channel_id=1, source_target_pairs={{0,4},{4,8},{8,12},{1,5},{5,9},{9,13},{2,6},{6,10},{10,14},{3,7},{... | collective-permute-start | bytes 3145736 | tf_op jit(solution)/shard_map/ppermute | solution.py:404
  11.2 106.3 %collective-permute-start.10 = (bf16[512,2048]{1,0:T(8,128)(2,1)}, bf16[512,2048]{1,0:T(8,128)(2,1)}, u32[]{:S(2)}, u32[]{:S(2)}) collective-permute-start(bf16[512,2048]{1,0:T(8,128)(2,1)} %bitcast.44), channel_id=1, source_target_pairs={{16,0},{0,16},{17,1},{1,17},{18,2},{2,18},{19,3},{3,19},{20,4},{4,... | collective-permute-start | bytes 6291464 | tf_op jit(solution)/shard_map/ppermute | solution.py:409
  13.1 120.5 %copy-start.8 = (bf16[512,1024]{1,0:T(8,128)(2,1)}, bf16[512,1024]{1,0:T(8,128)(2,1)S(1)}, u32[]{:S(2)}) copy-start(bf16[512,1024]{1,0:T(8,128)(2,1)S(1)} %collective-permute-done.refs_4_.refs_9_) | copy-start | bytes 3145732
  13.7 119.9 %copy-start.9 = (bf16[512,1024]{1,0:T(8,128)(2,1)}, bf16[512,1024]{1,0:T(8,128)(2,1)S(1)}, u32[]{:S(2)}) copy-start(bf16[512,1024]{1,0:T(8,128)(2,1)S(1)} %collective-permute-done.1.refs_5_.refs_10_) | copy-start | bytes 3145732
  50.2 35.5 %collective-permute-start.5 = (bf16[512,2048]{1,0:T(8,128)(2,1)}, bf16[512,2048]{1,0:T(8,128)(2,1)}, u32[]{:S(2)}, u32[]{:S(2)}) collective-permute-start(bf16[512,2048]{1,0:T(8,128)(2,1)} %get-tuple-element.47.refs_3_), channel_id=1, source_target_pairs={{1,2},{2,1},{5,6},{6,5},{9,10},{10,9},{13,14},{14,13},{17,18},{18,... | collective-permute-start | bytes 6291464 | tf_op jit(solution)/shard_map/middle2/ppermute | solution.py:414
  55.2 30.5 %collective-permute-start.3 = (bf16[256,2048]{1,0:T(8,128)(2,1)S(1)}, bf16[256,2048]{1,0:T(8,128)(2,1)S(1)}, u32[]{:S(2)}, u32[]{:S(2)}) collective-permute-start(bf16[256,2048]{1,0:T(8,128)(2,1)S(1)} %add_convert_fusion.7.refs_0_.refs_5_), channel_id=1, source_target_pairs={{0,1},{1,0},{2,3},{3,2},{4,5},{5,4},{6,7},{7,6},{8,9},{9,8},{10,11... | collective-permute-start | bytes 3145736 | tf_op jit(solution)/shard_map/outer2a/ppermute | solution.py:414
  60.6 42.0 %collective-permute-start.6 = (bf16[256,2048]{1,0:T(8,128)(2,1)S(1)}, bf16[256,2048]{1,0:T(8,128)(2,1)S(1)}, u32[]{:S(2)}, u32[]{:S(2)}) collective-permute-start(bf16[256,2048]{1,0:T(8,128)(2,1)S(1)} %add_convert_fusion.6.refs_6_), channel_id=1, source_target_pairs={{0,1},{1,0},{2,3},{3,2},{4,5},{5,4},{6,7},{7,6},{8,9},{9,8},{10,11... | collective-permute-start | bytes 3145736 | tf_op jit(solution)/shard_map/outer2b/ppermute | solution.py:414
  74.7 11.0 %copy-start.18 = (bf16[256,2048]{1,0:T(8,128)(2,1)}, bf16[256,2048]{1,0:T(8,128)(2,1)S(1)}, u32[]{:S(2)}) copy-start(bf16[256,2048]{1,0:T(8,128)(2,1)S(1)} %get-tuple-element.58) | copy-start | bytes 3145732
  88.4 37.0 %collective-permute-start.8 = (bf16[256,2048]{1,0:T(8,128)(2,1)S(1)}, bf16[256,2048]{1,0:T(8,128)(2,1)S(1)}, u32[]{:S(2)}, u32[]{:S(2)}) collective-permute-start(bf16[256,2048]{1,0:T(8,128)(2,1)S(1)} %get-tuple-element.87.refs_1_), channel_id=1, source_target_pairs={{0,1},{1,0},{2,3},{3,2},{4,5},{5,4},{6,7},{7,6},{8,9},{9,8},{10,11... | collective-permute-start | bytes 3145736 | tf_op jit(solution)/shard_map/outer3a/ppermute | solution.py:414
  101.9 26.6 %collective-permute-start.9 = (bf16[256,2048]{1,0:T(8,128)(2,1)S(1)}, bf16[256,2048]{1,0:T(8,128)(2,1)S(1)}, u32[]{:S(2)}, u32[]{:S(2)}) collective-permute-start(bf16[256,2048]{1,0:T(8,128)(2,1)S(1)} %get-tuple-element.88.refs_0_), channel_id=1, source_target_pairs={{1,2},{2,1},{5,6},{6,5},{9,10},{10,9},{13,14},{14,13},{17,18},{18,... | collective-permute-start | bytes 3145736 | tf_op jit(solution)/shard_map/middle3a/ppermute | solution.py:414
  102.7 7.2 %copy-start.25 = (bf16[256,2048]{1,0:T(8,128)(2,1)S(1)}, bf16[256,2048]{1,0:T(8,128)(2,1)}, u32[]{:S(2)}) copy-start(bf16[256,2048]{1,0:T(8,128)(2,1)} %copy-done.24) | copy-start | bytes 3145732
  105.4 42.5 %collective-permute-start.7 = (bf16[256,2048]{1,0:T(8,128)(2,1)S(1)}, bf16[256,2048]{1,0:T(8,128)(2,1)S(1)}, u32[]{:S(2)}, u32[]{:S(2)}) collective-permute-start(bf16[256,2048]{1,0:T(8,128)(2,1)S(1)} %get-tuple-element.85.refs_5_), channel_id=1, source_target_pairs={{0,1},{1,0},{2,3},{3,2},{4,5},{5,4},{6,7},{7,6},{8,9},{9,8},{10,11... | collective-permute-start | bytes 3145736 | tf_op jit(solution)/shard_map/outer3b/ppermute | solution.py:414
  109.2 38.8 %collective-permute-start.11 = (bf16[256,2048]{1,0:T(8,128)(2,1)S(1)}, bf16[256,2048]{1,0:T(8,128)(2,1)S(1)}, u32[]{:S(2)}, u32[]{:S(2)}) collective-permute-start(bf16[256,2048]{1,0:T(8,128)(2,1)S(1)} %get-tuple-element.86.refs_4_), channel_id=1, source_target_pairs={{1,2},{2,1},{5,6},{6,5},{9,10},{10,9},{13,14},{14,13},{17,18},{18,... | collective-permute-start | bytes 3145736 | tf_op jit(solution)/shard_map/middle3b/ppermute | solution.py:414
  121.3 7.2 %copy-start.22 = (bf16[256,2048]{1,0:T(8,128)(2,1)S(1)}, bf16[256,2048]{1,0:T(8,128)(2,1)}, u32[]{:S(2)}) copy-start(bf16[256,2048]{1,0:T(8,128)(2,1)} %copy-done.21) | copy-start | bytes 3145732
  127.5 6.1 %copy-start.7 = (bf16[1,512,1024]{2,1,0:T(8,128)(2,1)S(1)}, bf16[1,512,1024]{2,1,0:T(8,128)(2,1)}, u32[]{:S(2)}) copy-start(bf16[1,512,1024]{2,1,0:T(8,128)(2,1)} %param.9) | copy-start | bytes 3145732
  127.5 37.7 %collective-permute-start.16 = (bf16[256,2048]{1,0:T(8,128)(2,1)}, bf16[256,2048]{1,0:T(8,128)(2,1)S(1)}, u32[]{:S(2)}, u32[]{:S(2)}) collective-permute-start(bf16[256,2048]{1,0:T(8,128)(2,1)} %add_convert_fusion.refs_12_), channel_id=1, source_target_pairs={{1,2},{2,1},{5,6},{6,5},{9,10},{10,9},{13,14},{14,13},{17,18},{18,... | collective-permute-start | bytes 3145736 | tf_op jit(solution)/shard_map/middle4a/ppermute | solution.py:414
  129.6 40.9 %collective-permute-start.15 = (bf16[256,2048]{1,0:T(8,128)(2,1)S(1)}, bf16[256,2048]{1,0:T(8,128)(2,1)S(1)}, u32[]{:S(2)}, u32[]{:S(2)}) collective-permute-start(bf16[256,2048]{1,0:T(8,128)(2,1)S(1)} %add_convert_fusion.1.refs_11_), channel_id=1, source_target_pairs={{0,1},{1,0},{2,3},{3,2},{4,5},{5,4},{6,7},{7,6},{8,9},{9,8},{10,11... | collective-permute-start | bytes 3145736 | tf_op jit(solution)/shard_map/outer4a/ppermute | solution.py:414
  133.6 16.1 %copy-start.19 = (bf16[256,2048]{1,0:T(8,128)(2,1)S(1)}, bf16[256,2048]{1,0:T(8,128)(2,1)}, u32[]{:S(2)}) copy-start(bf16[256,2048]{1,0:T(8,128)(2,1)} %copy-done.18) | copy-start | bytes 3145732
  150.5 31.2 %collective-permute-start.12 = (bf16[128,2048]{1,0:T(8,128)(2,1)S(1)}, bf16[128,2048]{1,0:T(8,128)(2,1)S(1)}, u32[]{:S(2)}, u32[]{:S(2)}) collective-permute-start(bf16[128,2048]{1,0:T(8,128)(2,1)S(1)} %add_convert_fusion.11.refs_12_), channel_id=1, source_target_pairs={{0,1},{1,0},{2,3},{3,2},{4,5},{5,4},{6,7},{7,6},{8,9},{9,8},{10,11... | collective-permute-start | bytes 1572872 | tf_op jit(solution)/shard_map/outer4b/ppermute | solution.py:414
  152.9 20.3 %collective-permute-start.14 = (bf16[2,256,1024]{2,1,0:T(8,128)(2,1)S(1)}, bf16[2,256,1024]{2,1,0:T(8,128)(2,1)S(1)}, u32[]{:S(2)}, u32[]{:S(2)}) collective-permute-start(bf16[2,256,1024]{2,1,0:T(8,128)(2,1)S(1)} %get-tuple-element.70), channel_id=1, source_target_pairs={{4,0},{8,4},{12,8},{5,1},{9,5},{13,9},{6,2},{10,6},{14,10},{7,3},{... | collective-permute-start | bytes 3145736 | tf_op jit(solution)/shard_map/ppermute | solution.py:404
  155.0 26.7 %collective-permute-start.13 = (bf16[128,2048]{1,0:T(8,128)(2,1)S(1)}, bf16[128,2048]{1,0:T(8,128)(2,1)S(1)}, u32[]{:S(2)}, u32[]{:S(2)}) collective-permute-start(bf16[128,2048]{1,0:T(8,128)(2,1)S(1)} %add_convert_fusion.10.refs_13_), channel_id=1, source_target_pairs={{1,2},{2,1},{5,6},{6,5},{9,10},{10,9},{13,14},{14,13},{17,18},{18,... | collective-permute-start | bytes 1572872 | tf_op jit(solution)/shard_map/middle4b/ppermute | solution.py:414
  155.7 14.7 %copy-start.17 = (bf16[256,2048]{1,0:T(8,128)(2,1)S(1)}, bf16[256,2048]{1,0:T(8,128)(2,1)}, u32[]{:S(2)}) copy-start(bf16[256,2048]{1,0:T(8,128)(2,1)} %copy-done.16) | copy-start | bytes 3145732
  171.6 23.8 %collective-permute-start.18 = (bf16[256,2048]{1,0:T(8,128)(2,1)S(1)}, bf16[256,2048]{1,0:T(8,128)(2,1)S(1)}, u32[]{:S(2)}, u32[]{:S(2)}) collective-permute-start(bf16[256,2048]{1,0:T(8,128)(2,1)S(1)} %subtract_convert_fusion.refs_3_), channel_id=1, source_target_pairs={{16,0},{0,16},{17,1},{1,17},{18,2},{2,18},{19,3},{3,19},{20,4},{4,... | collective-permute-start | bytes 3145736 | tf_op jit(solution)/shard_map/ppermute | solution.py:409
  174.4 7.3 %copy-start.15 = (bf16[256,2048]{1,0:T(8,128)(2,1)S(1)}, bf16[256,2048]{1,0:T(8,128)(2,1)}, u32[]{:S(2)}) copy-start(bf16[256,2048]{1,0:T(8,128)(2,1)} %copy-done.14) | copy-start | bytes 3145732
  175.3 17.6 %collective-permute-start.19 = (bf16[128,2048]{1,0:T(8,128)(2,1)S(1)}, bf16[128,2048]{1,0:T(8,128)(2,1)S(1)}, u32[]{:S(2)}, u32[]{:S(2)}) collective-permute-start(bf16[128,2048]{1,0:T(8,128)(2,1)S(1)} %add_convert_fusion.9.refs_0_), channel_id=1, source_target_pairs={{0,1},{1,0},{2,3},{3,2},{4,5},{5,4},{6,7},{7,6},{8,9},{9,8},{10,11... | collective-permute-start | bytes 1572872 | tf_op jit(solution)/shard_map/outer4c/ppermute | solution.py:414
  179.1 13.7 %collective-permute-start.20 = (bf16[128,2048]{1,0:T(8,128)(2,1)S(1)}, bf16[128,2048]{1,0:T(8,128)(2,1)S(1)}, u32[]{:S(2)}, u32[]{:S(2)}) collective-permute-start(bf16[128,2048]{1,0:T(8,128)(2,1)S(1)} %add_convert_fusion.8.refs_1_), channel_id=1, source_target_pairs={{1,2},{2,1},{5,6},{6,5},{9,10},{10,9},{13,14},{14,13},{17,18},{18,... | collective-permute-start | bytes 1572872 | tf_op jit(solution)/shard_map/middle4c/ppermute | solution.py:414
  183.1 13.4 %collective-permute-start.17 = (bf16[2,256,1024]{2,1,0:T(8,128)(2,1)S(1)}, bf16[2,256,1024]{2,1,0:T(8,128)(2,1)S(1)}, u32[]{:S(2)}, u32[]{:S(2)}) collective-permute-start(bf16[2,256,1024]{2,1,0:T(8,128)(2,1)S(1)} %get-tuple-element.74), channel_id=1, source_target_pairs={{4,0},{8,4},{12,8},{5,1},{9,5},{13,9},{6,2},{10,6},{14,10},{7,3},{... | collective-permute-start | bytes 3145736 | tf_op jit(solution)/shard_map/ppermute | solution.py:404
  184.9 21.0 %collective-permute-start.22 = (bf16[128,2048]{1,0:T(8,128)(2,1)S(1)}, bf16[128,2048]{1,0:T(8,128)(2,1)S(1)}, u32[]{:S(2)}, u32[]{:S(2)}) collective-permute-start(bf16[128,2048]{1,0:T(8,128)(2,1)S(1)} %subtract_convert_fusion.2.refs_1_.refs_0_), channel_id=1, source_target_pairs={{16,0},{0,16},{17,1},{1,17},{18,2},{2,18},{19,3},{3,19},{20,4},{4,... | collective-permute-start | bytes 1572872 | tf_op jit(solution)/shard_map/ppermute | solution.py:409
  193.8 23.4 %collective-permute-start.21 = (bf16[128,2048]{1,0:T(8,128)(2,1)S(1)}, bf16[128,2048]{1,0:T(8,128)(2,1)S(1)}, u32[]{:S(2)}, u32[]{:S(2)}) collective-permute-start(bf16[128,2048]{1,0:T(8,128)(2,1)S(1)} %subtract_convert_fusion.1.refs_1_), channel_id=1, source_target_pairs={{16,0},{0,16},{17,1},{1,17},{18,2},{2,18},{19,3},{3,19},{20,4},{4,... | collective-permute-start | bytes 1572872 | tf_op jit(solution)/shard_map/ppermute | solution.py:409
  (17 other events, 41.4 us)
